TPU v7x, 32 devices: a whole 2x2x4 slice. The times are simulated.
32 devices in a mesh: rows: 4 (over y, x), seq: 4 (over z), fsdp: 2 (over core).
Axes of the slice: x: 2, y: 2, z: 4, core: 2. Of those that a mesh axis runs over, the one named last changes fastest.
Arguments:
- states: bfloat16 [4, 4, 2048, 2048], P('rows', None, 'seq'), may hold values from -6 to 6
- doc_ids: int32 [4, 4, 2048], P('rows'), may hold values from 0 to 12, as said below
- w_qkv: bfloat16 [3, 2048, 2048], P(None, ('rows', 'seq'), 'fsdp'), may hold values from -0.125 to 0.125
- w_out: bfloat16 [2048, 2048], P('fsdp', ('rows', 'seq')), may hold values from -1 to 1
- w_up: bfloat16 [2048, 8192], P(('rows', 'seq'), 'fsdp'), may hold values from -0.125 to 0.125
- w_down: bfloat16 [8192, 2048], P('fsdp', ('rows', 'seq')), may hold values from -0.0625 to 0.0625
- bias_qv: bfloat16 [2, 32, 64], P(None, 'fsdp', ('rows', 'seq')), may hold values from -3 to 3
- bias_out: bfloat16 [2048], P(('rows', 'seq')), may hold values from -2 to 2
- bias_up: bfloat16 [128, 64], P('fsdp', ('rows', 'seq')), may hold values from -3 to 3
- bias_down: bfloat16 [2048], P(('rows', 'seq')), may hold values from -2 to 2
- gain_one: bfloat16 [2048], P(('rows', 'seq')), may hold values from 0.5 to 1.5
- shift_one: bfloat16 [2048], P(('rows', 'seq')), may hold values from -1.5 to 1.5
- gain_two: bfloat16 [2048], P(('rows', 'seq')), may hold values from 0.5 to 1.5
- shift_two: bfloat16 [2048], P(('rows', 'seq')), may hold values from -1.5 to 1.5
- cotangent: bfloat16 [4, 4, 2048, 2048], P('rows', None, 'seq'), may hold values from -6 to 6
Outputs:
- out_states: bfloat16 [4, 4, 2048, 2048], P('rows', None, 'seq')
- grad_states: bfloat16 [4, 4, 2048, 2048], P('rows', None, 'seq')
- grad_w_qkv: float32 [3, 2048, 2048], P(None, ('rows', 'seq'), 'fsdp')
- grad_w_out: float32 [2048, 2048], P('fsdp', ('rows', 'seq'))
- grad_w_up: float32 [2048, 8192], P(('rows', 'seq'), 'fsdp')
- grad_w_down: float32 [8192, 2048], P('fsdp', ('rows', 'seq'))
- grad_bias_qv: float32 [2, 32, 64], P(None, 'fsdp', ('rows', 'seq'))
- grad_bias_out: float32 [2048], P(('rows', 'seq'))
- grad_bias_up: float32 [128, 64], P('fsdp', ('rows', 'seq'))
- grad_bias_down: float32 [2048], P(('rows', 'seq'))
- grad_gain_one: float32 [2048], P(('rows', 'seq'))
- grad_shift_one: float32 [2048], P(('rows', 'seq'))
- grad_gain_two: float32 [2048], P(('rows', 'seq'))
- grad_shift_two: float32 [2048], P(('rows', 'seq'))
Inputs may be any that keep to these rules, and one draw needn't show every extreme that they name: `doc_ids`: within each row the numbers never fall from one position to the next; a row starts at 0 and ends at 12; in each row one whole segment, drawn from the seed, belongs to a single document.
All inputs are finite; a program needn't handle non-finite values.
Results may differ from a plain program's by a relative error of at most 0.019.
Values may be sent and summed in bfloat16 or wider, within the bound.
A program may use at most 1.125 GiB of HBM per device.

v0:
```python
import jax
import jax.numpy as jnp
from jax import lax
from jax.sharding import PartitionSpec as P

HEAD = 64
SUMM = 50


neg_big = -1e30
norm_eps = 1e-05


def spread(block, axis, source):
    block = jnp.where(lax.axis_index(axis) == source, block, jnp.zeros_like(block))
    return lax.psum(block, axis)


def layer_norm(field, gain_vec, shift_vec):
    row_mean = jnp.mean(field, axis=-1, keepdims=True)
    centered = field - row_mean
    variance = jnp.mean(centered * centered, axis=-1, keepdims=True)
    return centered * lax.rsqrt(variance + norm_eps) * gain_vec + shift_vec


def gelu_exact(field):
    return jax.nn.gelu(field, approximate=False)


def earlier(field, offset, fill_value):
    widths = tuple(((offset, 0) if dim_index == 1 else (0, 0) for dim_index in range(field.ndim)))
    return jnp.pad(field, widths, constant_values=fill_value)[:, : field.shape[1]]


def later(field, offset):
    widths = tuple(((0, offset) if dim_index == 1 else (0, 0) for dim_index in range(field.ndim)))
    return jnp.pad(field, widths)[:, offset:]


def lead(field):
    return jnp.moveaxis(field, 1, 0)


def halves(field):
    return lax.psum(field.astype(jnp.bfloat16), "fsdp").astype(jnp.float32)


def local(
    states,
    doc_ids,
    w_qkv,
    w_out,
    w_up,
    w_down,
    bias_qv,
    bias_out,
    bias_up,
    bias_down,
    gain_one,
    shift_one,
    gain_two,
    shift_two,
    cotangent,
):
    attn_full = (
        lax.all_gather(w_qkv, ("rows", "seq"), axis=1, tiled=True),
        lax.all_gather(w_out, ("rows", "seq"), axis=1, tiled=True),
        lax.all_gather(bias_qv, ("rows", "seq"), axis=2, tiled=True),
        lax.all_gather(gain_one, ("rows", "seq"), axis=0, tiled=True),
        lax.all_gather(shift_one, ("rows", "seq"), axis=0, tiled=True),
        lax.all_gather(bias_out, ("rows", "seq"), axis=0, tiled=True),
    )
    qkv_full, out_full, bqv_full, gain_a, shift_a, bias_o = attn_full
    rows_dev, seg_count, width, model = states.shape
    seq_count = lax.axis_size("seq")
    seq_place = lax.axis_index("seq")
    seg_len = width * seq_count
    half_width = qkv_full.shape[2]
    heads_loc = half_width // HEAD
    score_scale = HEAD ** (-0.5)
    states_f = states.astype(jnp.float32)
    normed_f, norm_one_back = jax.vjp(
        layer_norm, states_f, gain_a.astype(jnp.float32), shift_a.astype(jnp.float32)
    )
    normed_one = normed_f.astype(jnp.bfloat16)
    projected = jnp.einsum(
        "rsid,kde->krsie", normed_one, qkv_full, preferred_element_type=jnp.float32
    )
    bias_pair = bqv_full.astype(jnp.float32).reshape(2, half_width)
    query = ((projected[0] + bias_pair[0]) * score_scale).astype(jnp.bfloat16)
    keys = projected[1].astype(jnp.bfloat16)
    values = (projected[2] + bias_pair[1]).astype(jnp.bfloat16)
    tail = jnp.stack((keys[:, :, width - SUMM :], values[:, :, width - SUMM :]))
    summary = spread(tail, "seq", seq_count - 1)
    sum_keys = jnp.concatenate((earlier(summary[0], 1, 0.0), earlier(summary[0], 2, 0.0)), axis=2)
    sum_values = jnp.concatenate((earlier(summary[1], 1, 0.0), earlier(summary[1], 2, 0.0)), axis=2)
    sum_src = doc_ids[:, :, seg_len - SUMM :]
    sum_docs = jnp.concatenate((earlier(sum_src, 1, -1), earlier(sum_src, 2, -1)), axis=2)
    sum_k5 = sum_keys.reshape(rows_dev, seg_count, 2 * SUMM, heads_loc, HEAD)
    sum_v5 = sum_values.reshape(rows_dev, seg_count, 2 * SUMM, heads_loc, HEAD)
    first_pos = seq_place * width
    query_docs = lax.dynamic_slice_in_dim(doc_ids, first_pos, width, 2)
    query_pos = first_pos + jnp.arange(width, dtype=jnp.int32)
    query5 = query.reshape(rows_dev, seg_count, width, heads_loc, HEAD)
    sum_allowed = (query_docs[:, :, :, None] == sum_docs[:, :, None, :])[:, :, None]
    sum_scores = jnp.einsum(
        "rsihe,rsjhe->rshij", query5, sum_k5, preferred_element_type=jnp.float32
    )
    sum_scores = jnp.where(sum_allowed, sum_scores, neg_big)
    start_max = jnp.max(sum_scores, axis=-1)
    start_exp = jnp.where(sum_allowed, jnp.exp(sum_scores - start_max[..., None]), 0.0)
    start_sum = jnp.sum(start_exp, axis=-1)
    start_acc = jnp.einsum(
        "rshij,rsjhe->rsihe",
        start_exp.astype(jnp.bfloat16),
        sum_v5,
        preferred_element_type=jnp.float32,
    )
    key_piece = lax.all_gather(keys, "seq", axis=2, tiled=True)
    value_piece = lax.all_gather(values, "seq", axis=2, tiled=True)
    count = key_piece.shape[2]
    key5 = key_piece.reshape(rows_dev, seg_count, count, heads_loc, HEAD)
    value5 = value_piece.reshape(rows_dev, seg_count, count, heads_loc, HEAD)
    key_pos = jnp.arange(count, dtype=jnp.int32)
    causal = (key_pos[None, :] <= query_pos[:, None])[None, None, None]
    allowed = causal & (query_docs[:, :, :, None] == doc_ids[:, :, None, :])[:, :, None]
    scores = jnp.einsum("rsihe,rsjhe->rshij", query5, key5, preferred_element_type=jnp.float32)
    scores = jnp.where(allowed, scores, neg_big)
    new_max = jnp.maximum(start_max, jnp.max(scores, axis=-1))
    factor = jnp.exp(start_max - new_max)
    exponent = jnp.where(allowed, jnp.exp(scores - new_max[..., None]), 0.0)
    new_sum = start_sum * factor + jnp.sum(exponent, axis=-1)
    gained = jnp.einsum(
        "rshij,rsjhe->rsihe",
        exponent.astype(jnp.bfloat16),
        value5,
        preferred_element_type=jnp.float32,
    )
    new_acc = start_acc * jnp.swapaxes(factor, 2, 3)[..., None] + gained
    log_sum = new_max + jnp.log(new_sum)
    mixed_f = new_acc / jnp.swapaxes(new_sum, 2, 3)[..., None]
    mixed = mixed_f.reshape(rows_dev, seg_count, width, half_width).astype(jnp.bfloat16)
    attn_lin = halves(
        jnp.einsum("rsie,ed->rsid", mixed, out_full, preferred_element_type=jnp.float32)
    )
    hidden = states_f + attn_lin + bias_o.astype(jnp.float32)
    ffn_full = (
        lax.all_gather(w_up, ("rows", "seq"), axis=0, tiled=True),
        lax.all_gather(w_down, ("rows", "seq"), axis=1, tiled=True),
        lax.all_gather(bias_up, ("rows", "seq"), axis=1, tiled=True),
        lax.all_gather(gain_two, ("rows", "seq"), axis=0, tiled=True),
        lax.all_gather(shift_two, ("rows", "seq"), axis=0, tiled=True),
        lax.all_gather(bias_down, ("rows", "seq"), axis=0, tiled=True),
    )
    up_full, down_full, bias_u, gain_b, shift_b, bias_d = ffn_full
    normed_two_f, norm_two_back = jax.vjp(
        layer_norm, hidden, gain_b.astype(jnp.float32), shift_b.astype(jnp.float32)
    )
    normed_two = normed_two_f.astype(jnp.bfloat16)
    up_proj = jnp.einsum(
        "rsid,df->rsif", normed_two, up_full, preferred_element_type=jnp.float32
    ) + bias_u.astype(jnp.float32).reshape(-1)
    activated_f, gelu_back = jax.vjp(gelu_exact, up_proj)
    activated = activated_f.astype(jnp.bfloat16)
    down_proj = halves(
        jnp.einsum("rsif,fd->rsid", activated, down_full, preferred_element_type=jnp.float32)
    )
    out_states = (hidden + down_proj + bias_d.astype(jnp.float32)).astype(jnp.bfloat16)
    up_back, down_back = (
        lax.all_gather(w_up, ("rows", "seq"), axis=0, tiled=True),
        lax.all_gather(w_down, ("rows", "seq"), axis=1, tiled=True),
    )
    qkv_back, out_back = (
        lax.all_gather(w_qkv, ("rows", "seq"), axis=1, tiled=True),
        lax.all_gather(w_out, ("rows", "seq"), axis=1, tiled=True),
    )
    grad_out = cotangent.astype(jnp.float32)
    grad_bias_down = jnp.sum(grad_out, axis=(0, 1, 2))
    grad_w_down = jnp.einsum(
        "rsif,rsid->fd", activated, cotangent, preferred_element_type=jnp.float32
    )
    d_act = jnp.einsum("rsid,fd->rsif", cotangent, down_back, preferred_element_type=jnp.float32)
    (d_up,) = gelu_back(d_act)
    d_up_low = d_up.astype(jnp.bfloat16)
    grad_bias_up = jnp.sum(d_up_low, axis=(0, 1, 2), dtype=jnp.float32).reshape(bias_u.shape)
    grad_w_up = jnp.einsum(
        "rsid,rsif->df", normed_two, d_up_low, preferred_element_type=jnp.float32
    )
    d_norm_two = halves(
        jnp.einsum("rsif,df->rsid", d_up_low, up_back, preferred_element_type=jnp.float32)
    )
    d_hidden_ln, grad_gain_two, grad_shift_two = norm_two_back(d_norm_two)
    d_hidden = grad_out + d_hidden_ln
    ffn_grads = (
        lax.psum_scatter(grad_w_up, ("rows", "seq"), scatter_dimension=0, tiled=True),
        lax.psum_scatter(grad_w_down, ("rows", "seq"), scatter_dimension=1, tiled=True),
        lax.psum_scatter(grad_bias_up, ("rows", "seq"), scatter_dimension=1, tiled=True),
        lax.psum_scatter(grad_gain_two, ("rows", "seq"), scatter_dimension=0, tiled=True),
        lax.psum_scatter(grad_shift_two, ("rows", "seq"), scatter_dimension=0, tiled=True),
        lax.psum_scatter(grad_bias_down, ("rows", "seq"), scatter_dimension=0, tiled=True),
    )
    grad_bias_out = jnp.sum(d_hidden, axis=(0, 1, 2))
    d_hidden_low = d_hidden.astype(jnp.bfloat16)
    grad_w_out = jnp.einsum(
        "rsie,rsid->ed", mixed, d_hidden_low, preferred_element_type=jnp.float32
    )
    d_mixed = jnp.einsum(
        "rsid,ed->rsie", d_hidden_low, out_back, preferred_element_type=jnp.float32
    ).astype(jnp.bfloat16)
    d_mixed5 = d_mixed.reshape(rows_dev, seg_count, width, heads_loc, HEAD)
    keys_all, values_all = (
        lax.all_gather(keys, "seq", axis=2, tiled=True),
        lax.all_gather(values, "seq", axis=2, tiled=True),
    )
    key_lead = lead(keys_all.reshape(rows_dev, seg_count, seg_len, heads_loc, HEAD))
    value_lead = lead(values_all.reshape(rows_dev, seg_count, seg_len, heads_loc, HEAD))
    query_lead = lead(query5)
    grad_lead = lead(d_mixed5)
    key_positions = jnp.arange(seg_len, dtype=jnp.int32)

    def segment_back(seg_items):
        q_seg, do_seg, lse_seg, qdoc_seg, k_seg, v_seg, kdoc_seg, sk_seg, sv_seg, sdoc_seg = (
            seg_items
        )
        causal = (key_positions[None, :] <= query_pos[:, None])[None, None]
        allowed = causal & (qdoc_seg[:, :, None] == kdoc_seg[:, None, :])[:, None]
        scores = jnp.einsum("rihe,rjhe->rhij", q_seg, k_seg, preferred_element_type=jnp.float32)
        attn_probs = jnp.where(allowed, jnp.exp(scores - lse_seg[..., None]), 0.0)
        d_probs = jnp.einsum("rihe,rjhe->rhij", do_seg, v_seg, preferred_element_type=jnp.float32)
        summ_allowed = (qdoc_seg[:, :, None] == sdoc_seg[:, None, :])[:, None]
        summ_scores = jnp.einsum(
            "rihe,rjhe->rhij", q_seg, sk_seg, preferred_element_type=jnp.float32
        )
        summ_probs = jnp.where(summ_allowed, jnp.exp(summ_scores - lse_seg[..., None]), 0.0)
        summ_dprobs = jnp.einsum(
            "rihe,rjhe->rhij", do_seg, sv_seg, preferred_element_type=jnp.float32
        )
        delta = jnp.sum(attn_probs * d_probs, axis=-1) + jnp.sum(summ_probs * summ_dprobs, axis=-1)
        d_scores = (attn_probs * (d_probs - delta[..., None])).astype(jnp.bfloat16)
        d_summ = (summ_probs * (summ_dprobs - delta[..., None])).astype(jnp.bfloat16)
        d_query = jnp.einsum("rhij,rjhe->rihe", d_scores, k_seg, preferred_element_type=jnp.float32)
        d_query = d_query + jnp.einsum(
            "rhij,rjhe->rihe", d_summ, sk_seg, preferred_element_type=jnp.float32
        )
        d_sum_keys = jnp.einsum(
            "rhij,rihe->rjhe", d_summ, q_seg, preferred_element_type=jnp.float32
        )
        d_sum_values = jnp.einsum(
            "rhij,rihe->rjhe",
            summ_probs.astype(jnp.bfloat16),
            do_seg,
            preferred_element_type=jnp.float32,
        )
        return (d_query, d_scores, attn_probs.astype(jnp.bfloat16), d_sum_keys, d_sum_values, delta)

    seg_inputs = (
        query_lead,
        grad_lead,
        lead(log_sum),
        lead(query_docs),
        key_lead,
        value_lead,
        lead(doc_ids),
        lead(sum_k5),
        lead(sum_v5),
        lead(sum_docs),
    )
    d_query_lead, d_scores_all, probs_all, d_sk_lead, d_sv_lead, delta_lead = lax.map(
        segment_back, seg_inputs
    )
    d_key_part = jnp.einsum(
        "srhij,srihe->jrshe", d_scores_all, query_lead, preferred_element_type=jnp.float32
    )
    d_value_part = jnp.einsum(
        "srhij,srihe->jrshe", probs_all, grad_lead, preferred_element_type=jnp.float32
    )
    key_grads = lax.psum_scatter(
        jnp.stack((d_key_part, d_value_part), axis=3)
        .reshape(width * lax.axis_size("seq"), rows_dev, seg_count, 2, half_width)
        .astype(jnp.bfloat16),
        "seq",
        scatter_dimension=0,
        tiled=True,
    ).astype(jnp.float32)
    key_grads = jnp.transpose(key_grads, (3, 1, 2, 0, 4))
    d_sk = jnp.moveaxis(d_sk_lead, 0, 1).reshape(rows_dev, seg_count, 2 * SUMM, half_width)
    d_sv = jnp.moveaxis(d_sv_lead, 0, 1).reshape(rows_dev, seg_count, 2 * SUMM, half_width)
    src_keys = later(d_sk[:, :, :SUMM], 1) + later(d_sk[:, :, SUMM:], 2)
    src_values = later(d_sv[:, :, :SUMM], 1) + later(d_sv[:, :, SUMM:], 2)
    summ_grads = lax.psum(jnp.stack((src_keys, src_values)).astype(jnp.bfloat16), "seq").astype(
        jnp.float32
    )
    owner_grads = jnp.where(seq_place == seq_count - 1, summ_grads, 0.0)
    owner_grads = jnp.pad(owner_grads, ((0, 0), (0, 0), (0, 0), (width - SUMM, 0), (0, 0)))
    key_grads = key_grads + owner_grads
    d_keys_low = key_grads[0].astype(jnp.bfloat16)
    d_values_low = key_grads[1].astype(jnp.bfloat16)
    d_query = jnp.moveaxis(d_query_lead, 0, 1).reshape(rows_dev, seg_count, width, half_width)
    d_query_low = d_query.astype(jnp.bfloat16)
    d_pre = (d_query_low.astype(jnp.float32) * score_scale).astype(jnp.bfloat16)
    grad_bias_qv = jnp.stack(
        (
            jnp.sum(d_pre, axis=(0, 1, 2), dtype=jnp.float32),
            jnp.sum(d_values_low, axis=(0, 1, 2), dtype=jnp.float32),
        )
    ).reshape(bqv_full.shape)
    d_qkv = jnp.stack((d_pre, d_keys_low, d_values_low))
    grad_w_qkv = jnp.einsum(
        "rsid,krsie->kde", normed_one, d_qkv, preferred_element_type=jnp.float32
    )
    d_norm_one = halves(
        jnp.einsum("krsie,kde->rsid", d_qkv, qkv_back, preferred_element_type=jnp.float32)
    )
    d_states_ln, grad_gain_one, grad_shift_one = norm_one_back(d_norm_one)
    grad_states = (d_hidden + d_states_ln).astype(jnp.bfloat16)
    attn_grads = (
        lax.psum_scatter(grad_w_qkv, ("rows", "seq"), scatter_dimension=1, tiled=True),
        lax.psum_scatter(grad_w_out, ("rows", "seq"), scatter_dimension=1, tiled=True),
        lax.psum_scatter(grad_bias_qv, ("rows", "seq"), scatter_dimension=2, tiled=True),
        lax.psum_scatter(grad_gain_one, ("rows", "seq"), scatter_dimension=0, tiled=True),
        lax.psum_scatter(grad_shift_one, ("rows", "seq"), scatter_dimension=0, tiled=True),
        lax.psum_scatter(grad_bias_out, ("rows", "seq"), scatter_dimension=0, tiled=True),
    )
    return (
        out_states,
        grad_states,
        attn_grads[0],
        attn_grads[1],
        ffn_grads[0],
        ffn_grads[1],
        attn_grads[2],
        attn_grads[5],
        ffn_grads[2],
        ffn_grads[5],
        attn_grads[3],
        attn_grads[4],
        ffn_grads[3],
        ffn_grads[4],
    )


def solution(mesh):
    return jax.shard_map(
        local,
        mesh=mesh,
        in_specs=(
            P("rows", None, "seq", None),
            P("rows", None, None),
            P(None, ("rows", "seq"), "fsdp"),
            P("fsdp", ("rows", "seq")),
            P(("rows", "seq"), "fsdp"),
            P("fsdp", ("rows", "seq")),
            P(None, "fsdp", ("rows", "seq")),
            P(("rows", "seq")),
            P("fsdp", ("rows", "seq")),
            P(("rows", "seq")),
            P(("rows", "seq")),
            P(("rows", "seq")),
            P(("rows", "seq")),
            P(("rows", "seq")),
            P("rows", None, "seq", None),
        ),
        out_specs=(
            P("rows", None, "seq", None),
            P("rows", None, "seq", None),
            P(None, ("rows", "seq"), "fsdp"),
            P("fsdp", ("rows", "seq")),
            P(("rows", "seq"), "fsdp"),
            P("fsdp", ("rows", "seq")),
            P(None, "fsdp", ("rows", "seq")),
            P(("rows", "seq")),
            P("fsdp", ("rows", "seq")),
            P(("rows", "seq")),
            P(("rows", "seq")),
            P(("rows", "seq")),
            P(("rows", "seq")),
            P(("rows", "seq")),
        ),
        check_vma=False,
    )
```

profile of v0, /device:TPU:0, one launch (start us, length us, event | category | flops | bytes accessed | tf_op | source)
XLA Modules:
  0.0 5311.6 jit_solution(13883784128628293281)
XLA Ops:
  306.3 248.5 %all-gather.25.cloned.1.call-done = bf16[1,1,4,2048,1024]{4,3,2,1,0:T(8,128)(2,1)} async-done(((bf16[1,1,4,512,1024]{4,3,2,1,0:T(8,128)(2,1)}), bf16[1,1,4,2048,1024]{4,3,2,1,0:T(8,128)(2,1)}) %all-gather.25.cloned.1.call-update) | async-done | bytes 16777232 | tf_op jit(solution)/shard_map/all_gather | solution.py:119
  577.5 97.8 %select_reduce_fusion = (f32[4,16,512]{2,1,0:T(8,128)S(1)}, f32[4,16,512,2048]{3,2,1,0:T(8,128)}) fusion(pred[4,512,2048]{2,1,0:T(8,128)(4,1)} %compare_and_fusion, bf16[4,512,16,64]{1,3,2,0:T(8,128)(2,1)} %multiply_convert_fusion.5, bf16[4,2048,16,64]{1,3,2,0:T(8,128)(2,1)} %bitcast.417), kind=kOutput, calls=%fused_computation.71 | convolution fusion | flops 8724119552 | bytes 293732352 | tf_op jit(solution)/shard_map/rsihe,rsjhe->rshij/dot_general | solution.py:127
  675.4 88.5 %fusion.63 = f32[4,16,512]{2,1,0:T(8,128)S(1)} fusion(f32[4,16,512,2048]{3,2,1,0:T(8,128)} %get-tuple-element.337, f32[4,16,512]{2,1,0:T(8,128)S(1)} %max.33, pred[4,512,2048]{2,1,0:T(8,128)(4,1)} %compare_and_fusion), kind=kLoop, calls=%fused_computation.72 | loop fusion | flops 268402688 | bytes 272891904 | tf_op jit(solution)/shard_map/reduce_sum | solution.py:132
  764.6 76.6 %all-gather.17.cloned.1.call-done = bf16[1,4,2048,1024]{3,2,1,0:T(8,128)(2,1)} async-done(((bf16[1,4,512,1024]{3,2,1,0:T(8,128)(2,1)}), bf16[1,4,2048,1024]{3,2,1,0:T(8,128)(2,1)}) %all-gather.17.cloned.1.call-update) | async-done | bytes 16777232 | tf_op jit(solution)/shard_map/all_gather | solution.py:120
  863.1 94.1 %fusion.124 = bf16[1,4,512,16,64]{2,4,3,1,0:T(8,128)(2,1)} fusion(f32[4,16,64,512]{3,2,1,0:T(8,128)} %fusion.136, f32[4,512,16]{1,2,0:T(8,128)S(1)} %get-tuple-element.329, f32[4,512,16]{1,2,0:T(8,128)S(1)} %get-tuple-element.328, bf16[4,2048,16,64]{1,3,2,0:T(8,128)(2,1)} %bitcast.423, f32[4,16,512,2048]{3,2,1,0:T(8,128)} %get-tuple-element.337, ...), kind=kOutput, calls=%fused_computation.174 | convolution fusion | flops 8866758656 | bytes 302383104 | tf_op jit(solution)/shard_map/rshij,rsjhe->rsihe/dot_general | solution.py:133
  1137.9 66.8 %all-gather.21.cloned.1.call-done = bf16[2048,4096]{1,0:T(8,128)(2,1)} async-done(((bf16[128,4096]{1,0:T(8,128)(2,1)}), bf16[2048,4096]{1,0:T(8,128)(2,1)}) %all-gather.21.cloned.1.call-update) | async-done | bytes 16777232 | tf_op jit(solution)/shard_map/all_gather | solution.py:148
  1204.7 58.8 %fusion.134 = (u8[512,4096]{1,0:T(8,128)(4,1)S(1)}, u8[512,4096]{1,0:T(8,128)(4,1)}, f32[4,512,4096]{2,1,0:T(8,128)}) fusion(f32[4096]{0:T(1024)S(1)} %reshape.989, bf16[2048,4096]{1,0:T(8,128)(2,1)} %all-gather.21.cloned.1.call-done, f32[2048]{0:T(1024)S(1)} %bitcast.467, f32[2048]{0:T(1024)S(1)} %bitcast.455, f32[4,512]{1,0:T(4,128)S(1)} %fusion.178, ...), kind=kOutput, calls=%fused_computation.194 | convolution fusion | flops 34510733312 | bytes 71360512 | tf_op jit(solution)/shard_map/rsid,df->rsif/dot_general | solution.py:160
  1263.5 79.8 %multiply_convert_fusion.2 = (bf16[4,512,4096]{2,1,0:T(8,128)(2,1)}, f32[4,512,4096]{2,1,0:T(8,128)}) fusion(f32[4,512,4096]{2,1,0:T(8,128)} %get-tuple-element.338, f32[4096]{0:T(1024)S(1)} %reshape.989, u8[512,4096]{1,0:T(8,128)(4,1)} %get-tuple-element.247, u8[512,4096]{1,0:T(8,128)(4,1)S(1)} %get-tuple-element.246), kind=kLoop, calls=%fused_computation.90 | loop fusion | flops 595591168 | bytes 88096768 | tf_op jit(solution)/shard_map/convert_element_type | solution.py:164
  1343.3 112.0 %all-gather.23.cloned.1.call-done = bf16[4096,2048]{1,0:T(8,128)(2,1)} async-done(((bf16[4096,128]{1,0:T(8,128)(2,1)}), bf16[4096,2048]{1,0:T(8,128)(2,1)}) %all-gather.23.cloned.1.call-update) | async-done | bytes 16777232 | tf_op jit(solution)/shard_map/all_gather | solution.py:149
  1455.2 60.5 %convert_reduce_fusion = (f32[4096]{0:T(1024)}, bf16[4,512,4096]{2,1,0:T(8,128)(2,1)}) fusion(f32[4,512,4096]{2,1,0:T(8,128)} %get-tuple-element.309, bf16[4096,2048]{1,0:T(8,128)(2,1)} %all-gather.23.cloned.1.call-done, bf16[1,4,512,2048]{3,2,1,0:T(8,128)(2,1)} %param.31, f32[4,512,4096]{2,1,0:T(8,128)} %get-tuple-element.338, f32[4096]{0:T(1024)S(1)} %reshape.989), kind=kOutput, calls=%fused_computation.88 | convolution fusion | flops 34502340608 | bytes 109084672 | tf_op jit(solution)/shard_map/rsid,fd->rsif/dot_general | solution.py:182
  1661.7 728.6 %while.19 = (s32[]{:T(128)}, bf16[4,1,512,16,64]{2,4,3,1,0:T(8,128)(2,1)}, bf16[4,1,16,512,2048]{4,3,2,1,0:T(8,128)(2,1)}, bf16[4,1,16,512,2048]{4,3,2,1,0:T(8,1...) while((s32[]{:T(128)}, ...), condition=%wide.region_17.18_spmd.clone, body=%wide.region_14.17_spmd.clone.sunk | while | flops 7148055040 | bytes 543425408 | solution.py:268
  1750.1 75.8 %bitcast_dynamic-update-slice_fusion.4 = (bf16[4,1,16,512,2048]{4,3,2,1,0:T(8,128)(2,1)}, bf16[16,512,2048]{2,1,0:T(8,128)(2,1)}, bf16[4,1,16,512,2048]{4,3,2,1,0:T(8,128)(2,1)}) fusion(bf16[4,1,16,512,2048]{4,3,2,1,0:T(8,128)(2,1)} %get-tuple-element.480, s32[]{:T(128)S(6)} %copy.170, f32[16,512,2048]{2,1,0:T(8,128)} %get-tuple-element.456, ...), kind=kLoop, calls=%fused_computation.8.clone.1 | loop fusion | flops 100663296 | bytes 235995136 | tf_op jit(solution)/shard_map/while/body/jit(dynamic_update_index_in_dim)/dynamic_update_slice | solution.py:268
  1932.1 75.8 %bitcast_dynamic-update-slice_fusion.4 = (bf16[4,1,16,512,2048]{4,3,2,1,0:T(8,128)(2,1)}, bf16[16,512,2048]{2,1,0:T(8,128)(2,1)}, bf16[4,1,16,512,2048]{4,3,2,1,0:T(8,128)(2,1)}) fusion(bf16[4,1,16,512,2048]{4,3,2,1,0:T(8,128)(2,1)} %get-tuple-element.480, s32[]{:T(128)S(6)} %copy.170, f32[16,512,2048]{2,1,0:T(8,128)} %get-tuple-element.456, ...), kind=kLoop, calls=%fused_computation.8.clone.1 | loop fusion | flops 100663296 | bytes 235995136 | tf_op jit(solution)/shard_map/while/body/jit(dynamic_update_index_in_dim)/dynamic_update_slice | solution.py:268
  2114.1 75.7 %bitcast_dynamic-update-slice_fusion.4 = (bf16[4,1,16,512,2048]{4,3,2,1,0:T(8,128)(2,1)}, bf16[16,512,2048]{2,1,0:T(8,128)(2,1)}, bf16[4,1,16,512,2048]{4,3,2,1,0:T(8,128)(2,1)}) fusion(bf16[4,1,16,512,2048]{4,3,2,1,0:T(8,128)(2,1)} %get-tuple-element.480, s32[]{:T(128)S(6)} %copy.170, f32[16,512,2048]{2,1,0:T(8,128)} %get-tuple-element.456, ...), kind=kLoop, calls=%fused_computation.8.clone.1 | loop fusion | flops 100663296 | bytes 235995136 | tf_op jit(solution)/shard_map/while/body/jit(dynamic_update_index_in_dim)/dynamic_update_slice | solution.py:268
  2296.1 75.9 %bitcast_dynamic-update-slice_fusion.4 = (bf16[4,1,16,512,2048]{4,3,2,1,0:T(8,128)(2,1)}, bf16[16,512,2048]{2,1,0:T(8,128)(2,1)}, bf16[4,1,16,512,2048]{4,3,2,1,0:T(8,128)(2,1)}) fusion(bf16[4,1,16,512,2048]{4,3,2,1,0:T(8,128)(2,1)} %get-tuple-element.480, s32[]{:T(128)S(6)} %copy.170, f32[16,512,2048]{2,1,0:T(8,128)} %get-tuple-element.456, ...), kind=kLoop, calls=%fused_computation.8.clone.1 | loop fusion | flops 100663296 | bytes 235995136 | tf_op jit(solution)/shard_map/while/body/jit(dynamic_update_index_in_dim)/dynamic_update_slice | solution.py:268
  2410.1 51.0 fusion.101
  2483.7 50.1 fusion.104
  2633.0 499.9 %reduce-scatter.7.cloned.1.call-done = bf16[512,1,4,2,1024]{4,0,2,1,3:T(8,128)(2,1)} async-done(((bf16[2048,1,4,2,1024]{4,0,2,1,3:T(8,128)(2,1)}), bf16[512,1,4,2,1024]{4,0,2,1,3:T(8,128)(2,1)}) %reduce-scatter.7.cloned.1.call-update) | async-done | bytes 8388624 | tf_op jit(solution)/shard_map/reduce_scatter | solution.py:277
  3179.7 58.8 %all-reduce.38.cloned.1.call-done = (bf16[1,4,512,2048]{3,2,1,0:T(8,128)(2,1)}, bf16[1,4,512,2048]{3,2,1,0:T(8,128)(2,1)}) async-done(((bf16[1,4,512,2048]{3,2,1,0:T(8,128)(2,1)}, bf16[1,4,512,2048]{3,2,1,0:T(8,128)(2,1)}), (bf16[1,4,512,2048]{3,2,1,0:T(8,128)(2,1)}, bf16[1,4,512,2048]{3,2,1,0:T(8,128)(2,1)})) %all-reduce.38.cloned.1.call-update) | async-done | bytes 16777232 | tf_op jit(solution)/shard_map/psum | solution.py:45
  3314.0 57.4 %convolution_bitcast_fusion.2 = f32[2048,4096]{1,0:T(8,128)} fusion(bf16[4,512,4096]{2,1,0:T(8,128)(2,1)} %get-tuple-element.340, f32[2048]{0:T(1024)S(1)} %bitcast.468, f32[2048]{0:T(1024)S(1)} %bitcast.459, f32[4,512]{1,0:T(4,128)S(1)} %copy-done.42, f32[4,512]{1,0:T(4,128)S(1)} %copy-done.23, f32[2048]{0:T(1024)S(1)} %bitcast.447, ...), kind=kOutput, calls=%fused_computation.125 | convolution fusion | flops 34397487104 | bytes 67149824 | tf_op jit(solution)/shard_map/rsid,rsif->df/dot_general | solution.py:186
  3495.0 243.6 %reduce-scatter.9.cloned.1.call-done = f32[3,128,1024]{1,2,0:T(8,128)} async-done(((f32[3,2048,1024]{1,2,0:T(8,128)}), f32[3,128,1024]{1,2,0:T(8,128)}) %reduce-scatter.9.cloned.1.call-update) | async-done | bytes 1572880 | tf_op jit(solution)/shard_map/reduce_scatter | solution.py:317
  3741.7 181.1 %reduce-scatter.11.cloned.1.call-done = f32[1024,128]{1,0:T(8,128)} async-done(((f32[1024,2048]{1,0:T(8,128)}), f32[1024,128]{1,0:T(8,128)}) %reduce-scatter.11.cloned.1.call-update) | async-done | bytes 524304 | tf_op jit(solution)/shard_map/reduce_scatter | solution.py:318
  3922.8 690.2 %reduce-scatter.13.cloned.1.call-done = f32[128,4096]{1,0:T(8,128)} async-done(((f32[2048,4096]{1,0:T(8,128)}), f32[128,4096]{1,0:T(8,128)}) %reduce-scatter.13.cloned.1.call-update) | async-done | bytes 2097168 | tf_op jit(solution)/shard_map/reduce_scatter | solution.py:195
  4613.0 691.5 %reduce-scatter.15.cloned.1.call-done = f32[4096,128]{1,0:T(8,128)} async-done(((f32[4096,2048]{1,0:T(8,128)}), f32[4096,128]{1,0:T(8,128)}) %reduce-scatter.15.cloned.1.call-update) | async-done | bytes 2097168 | tf_op jit(solution)/shard_map/reduce_scatter | solution.py:196
  (441 shorter events, 1483.4 us)
Async XLA Ops:
  7.2 158.7 %all-gather.15.cloned.1.call-start = ((), (), s32[]{:S(2)}) async-start(), calls=%async_computation.5 | async-start | bytes 13369344 | tf_op jit(solution)/shard_map/all_gather | solution.py:66
  7.9 259.2 %all-reduce.28.cloned.1.call-start = ((), (), s32[]{:S(2)}) async-start(), calls=%async_computation.6 | async-start | bytes 1835008 | tf_op jit(solution)/shard_map/psum | solution.py:16
  51.2 153.6 %copy-start.29 = (f32[16,1,128]{2,1,0:T(1,128)}, f32[16,1,128]{2,1,0:T(1,128)S(1)}, u32[]{:S(2)}) copy-start(f32[16,1,128]{2,1,0:T(1,128)S(1)} %convert_element_type.335) | copy-start | bytes 24580
  220.9 333.8 %all-gather.25.cloned.1.call-start = ((), (), s32[]{:S(2)}) async-start(), calls=%async_computation.19 | async-start | bytes 20971520 | tf_op jit(solution)/shard_map/all_gather | solution.py:119
  227.5 613.7 %all-gather.17.cloned.1.call-start = ((), (), s32[]{:S(2)}) async-start(), calls=%async_computation.7 | async-start | bytes 20971520 | tf_op jit(solution)/shard_map/all_gather | solution.py:120
  228.1 729.2 %all-gather.19.cloned.1.call-start = ((), (), s32[]{:S(2)}) async-start(), calls=%async_computation.8 | async-start | bytes 4456448 | tf_op jit(solution)/shard_map/all_gather | solution.py:67
  228.7 891.7 %all-reduce.30.cloned.1.call-start = ((), (), s32[]{:S(2)}) async-start(), calls=%async_computation.9 | async-start | bytes 16777216 | tf_op jit(solution)/shard_map/psum | solution.py:45
  284.2 479.7 %copy-start.5 = (f32[4,16,512]{2,1,0:T(8,128)}, f32[4,16,512]{2,1,0:T(8,128)S(1)}, u32[]{:S(2)}) copy-start(f32[4,16,512]{2,1,0:T(8,128)S(1)} %get-tuple-element.334) | copy-start | bytes 393220
  957.3 126.9 %copy-start.63 = (bf16[64,4]{0,1:T(4,128)(2,1)S(1)}, bf16[64,4]{0,1:T(4,128)(2,1)}, u32[]{:S(2)}) copy-start(bf16[64,4]{0,1:T(4,128)(2,1)} %param.25) | copy-start | bytes 1540
  971.5 233.1 %all-gather.21.cloned.1.call-start = ((), (), s32[]{:S(2)}) async-start(), calls=%async_computation.10 | async-start | bytes 17825792 | tf_op jit(solution)/shard_map/all_gather | solution.py:148
  972.3 483.0 %all-gather.23.cloned.1.call-start = ((), (), s32[]{:S(2)}) async-start(), calls=%async_computation.11 | async-start | bytes 17825792 | tf_op jit(solution)/shard_map/all_gather | solution.py:149
  973.0 622.7 %all-reduce.32.cloned.1.call-start = ((), (), s32[]{:S(2)}) async-start(), calls=%async_computation.12 | async-start | bytes 16777216 | tf_op jit(solution)/shard_map/psum | solution.py:45
  1010.7 194.0 %copy-start.16 = (f32[16,1,128]{2,1,0:T(1,128)}, f32[16,1,128]{2,1,0:T(1,128)S(1)}, u32[]{:S(2)}) copy-start(f32[16,1,128]{2,1,0:T(1,128)S(1)} %convert_element_type.337) | copy-start | bytes 24580
  1046.5 158.2 %copy-start.32 = (f32[16,1,128]{2,1,0:T(1,128)}, f32[16,1,128]{2,1,0:T(1,128)S(1)}, u32[]{:S(2)}) copy-start(f32[16,1,128]{2,1,0:T(1,128)S(1)} %convert_element_type.338) | copy-start | bytes 24580
  1129.0 134.5 %copy-start.21 = (f32[4,512]{1,0:T(4,128)}, f32[4,512]{1,0:T(4,128)S(1)}, u32[]{:S(2)}) copy-start(f32[4,512]{1,0:T(4,128)S(1)} %broadcast_multiply_fusion) | copy-start | bytes 24580
  1137.8 125.6 %copy-start.40 = (f32[4,512]{1,0:T(4,128)}, f32[4,512]{1,0:T(4,128)S(1)}, u32[]{:S(2)}) copy-start(f32[4,512]{1,0:T(4,128)S(1)} %fusion.178) | copy-start | bytes 24580
  1558.5 1073.0 %all-reduce.34.cloned.1.call-start = ((), (), s32[]{:S(2)}) async-start(), calls=%async_computation.14 | async-start | bytes 1835008 | tf_op jit(solution)/shard_map/psum | solution.py:290
  2410.1 722.8 %reduce-scatter.7.cloned.1.call-start = ((), (), s32[]{:S(2)}) async-start(), calls=%async_computation.13 | async-start | bytes 41943040 | tf_op jit(solution)/shard_map/reduce_scatter | solution.py:277
  2579.4 659.1 %all-reduce.38.cloned.1.call-start = ((), (), s32[]{:S(2)}) async-start(), calls=%async_computation.21 | async-start | bytes 33554432 | tf_op jit(solution)/shard_map/psum | solution.py:45
  3177.6 307.1 %all-reduce.36.cloned.1.call-start = ((), (), s32[]{:S(2)}) async-start(), calls=%async_computation.20 | async-start | bytes 294912
  3260.2 478.5 %reduce-scatter.9.cloned.1.call-start = ((), (), s32[]{:S(2)}) async-start(), calls=%async_computation.15 | async-start | bytes 26738688 | tf_op jit(solution)/shard_map/reduce_scatter | solution.py:317
  3298.1 624.8 %reduce-scatter.11.cloned.1.call-start = ((), (), s32[]{:S(2)}) async-start(), calls=%async_computation.16 | async-start | bytes 8912896 | tf_op jit(solution)/shard_map/reduce_scatter | solution.py:318
  3313.9 1299.2 %reduce-scatter.13.cloned.1.call-start = ((), (), s32[]{:S(2)}) async-start(), calls=%async_computation.17 | async-start | bytes 35651584 | tf_op jit(solution)/shard_map/reduce_scatter | solution.py:195
  3371.4 1933.2 %reduce-scatter.15.cloned.1.call-start = ((), (), s32[]{:S(2)}) async-start(), calls=%async_computation.18 | async-start | bytes 35651584 | tf_op jit(solution)/shard_map/reduce_scatter | solution.py:196
  (95 other events, 2671.5 us)
Sparse Core Ops, SparseCore 0:
  10.8 154.9 all-gather.14
  221.0 46.0 all-reduce.27
  268.7 285.9 all-gather.24
  556.2 284.9 all-gather.16
  843.7 87.3 all-gather.18
  971.7 37.0 all-reduce.29
  1011.5 193.1 all-gather.20
  1207.4 247.8 all-gather.22
  1558.6 37.0 all-reduce.31
  2410.2 48.9 all-reduce.33
  2579.6 553.2 reduce-scatter.6
  3177.7 60.7 all-reduce.37
  3260.3 109.4 all-reduce.35
  3376.4 362.2 reduce-scatter.8
  3741.5 181.2 reduce-scatter.10
  3925.7 687.2 reduce-scatter.12
  4615.9 688.6 reduce-scatter.14
where the time goes:
time: 5320 us; the launch traced here: 5310 us
  waiting for transfers between devices  2940 us (55%)
  matrix products  1190 us (22%)
  other arithmetic  673 us (13%)
  blocking collectives  306 us (6%)
  local copies, waits for them, and re-layouts  180 us (3%)
    reduce_scatter x1, waiting for transfers between devices, local(): lax.psum_scatter(grad_w_down, ('rows', 'seq'), scatter_dimension=1, tiled...  692 us
    reduce_scatter x1, waiting for transfers between devices, local(): lax.psum_scatter(grad_w_up, ('rows', 'seq'), scatter_dimension=0, tiled=T...  690 us
    reduce_scatter x1, waiting for transfers between devices, local(): lax.psum_scatter(jnp.stack((d_key_part, d_value_part), axis=3).reshape(wi...  500 us
    dynamic_update_slice x4, other arithmetic, local(): lax.map(segment_back, seg_inputs)  303 us
    all_gather x1, waiting for transfers between devices, local(): key_piece = lax.all_gather(keys, 'seq', axis=2, tiled=True)  248 us
    reduce_scatter x1, waiting for transfers between devices, local(): lax.psum_scatter(grad_w_qkv, ('rows', 'seq'), scatter_dimension=1, tiled=...  244 us
    dot_general x4, matrix products, segment_back(): jnp.einsum('rihe,rjhe->rhij', do_seg, v_seg, preferred_element_type=jnp.f...  199 us
    reduce_scatter x1, waiting for transfers between devices, local(): lax.psum_scatter(grad_w_out, ('rows', 'seq'), scatter_dimension=1, tiled=...  181 us
  transfers between devices with their start and end apart: 17, of which 13 were waited for; matrix products, arithmetic and copies ran while one was open for 19% of the time, Pallas kernels for 0%

commit v1 on v0

--- a/solution.py
+++ b/solution.py
@@ -1,10 +1,17 @@
+import functools
+
 import jax
 import jax.numpy as jnp
 from jax import lax
+from jax.experimental import pallas as pl
+from jax.experimental.pallas import tpu as pltpu
 from jax.sharding import PartitionSpec as P
 
 HEAD = 64
 SUMM = 50
+SEGS = 4
+F32 = jnp.float32
+BF = jnp.bfloat16
 
 
 neg_big = -1e30
@@ -339,9 +346,501 @@
     )
 
 
+def dot_nt(a,b): return lax.dot_general(a,b,(((1,),(1,)),((),())),preferred_element_type=F32)
+def dot_nn(a,b): return lax.dot_general(a,b,(((1,),(0,)),((),())),preferred_element_type=F32)
+
+def fwd_kernel(tile, flags, q_ref, k_ref, v_ref, sk_ref, sv_ref, start_ref, doc_ref, sdoc_ref, o_ref, lse_ref, km, vt, acc, top, total):
+    i = pl.program_id(1)
+    seg = k_ref.shape[0]
+    lanes = lax.broadcasted_iota(jnp.int32, (1, 128), 1)
+    masks = [(lanes < HEAD).astype(BF), (lanes >= HEAD).astype(BF)]
+    @pl.when(i == 0)
+    def _():
+        for h in range(2):
+            km[h, pl.ds(0, seg)] = k_ref[...] * masks[h]
+            km[h, pl.ds(seg, 128)] = sk_ref[...] * masks[h]
+        vt[:, pl.ds(0, seg)] = v_ref[...].T
+        vt[:, pl.ds(seg, 128)] = sv_ref[...].T
+    q = q_ref[...]
+    allowed = sdoc_ref[...] == doc_ref[...]
+    for h in range(2):
+        s = dot_nt(km[h, pl.ds(seg, 128)], q)
+        s = jnp.where(allowed, s, neg_big)
+        m = jnp.max(s, axis=0, keepdims=True)
+        p = jnp.where(allowed, jnp.exp(s - m), 0.0)
+        top[h] = m
+        total[h] = jnp.sum(p, axis=0, keepdims=True)
+        acc[h] = dot_nn(vt[pl.ds(h * HEAD, HEAD), pl.ds(seg, 128)], p.astype(BF))
+    def step(j, masked):
+        at = pl.multiple_of(j * tile, tile)
+        if masked:
+            places = at + lax.broadcasted_iota(jnp.int32, (tile, tile), 0)
+            mine = i * tile + lax.broadcasted_iota(jnp.int32, (tile, tile), 1)
+            okay = (places <= mine) & (places >= start_ref[...])
+        ss=[]
+        for h in range(2):
+            s = dot_nt(km[h, pl.ds(at, tile)], q)
+            if masked:
+                s = jnp.where(okay, s, neg_big)
+            ss.append(s)
+        for h in range(2):
+            s = ss[h]
+            m_old = top[h]
+            m = jnp.maximum(m_old, jnp.max(s, axis=0, keepdims=True))
+            p = jnp.exp(s - m)
+            if masked:
+                p = jnp.where(okay, p, 0.0)
+            alpha = jnp.exp(m_old - m)
+            top[h] = m
+            total[h] = total[h] * alpha + jnp.sum(p, axis=0, keepdims=True)
+            acc[h] = acc[h] * alpha + dot_nn(vt[pl.ds(h * HEAD, HEAD), pl.ds(at, tile)], p.astype(BF))
+    count = pl.num_programs(1)
+    def loop(j, _):
+        flag = flags[i * count + j]
+        @pl.when(flag == 2)
+        def _(): step(j, False)
+        @pl.when(flag == 1)
+        def _(): step(j, True)
+        return 0
+    lax.fori_loop(0, i + 1, loop, 0)
+    out = [acc[h] / total[h] for h in range(2)]
+    o_ref[...] = jnp.concatenate(out, axis=0).T.astype(BF)
+    for h in range(2):
+        lse_ref[0, pl.ds(h, 1)] = top[h] + jnp.log(total[h])
+
+def attn_fwd(q, k, v, sk, sv, start, doc, sdoc, flags, tile=512, offs=(0,0,0)):
+    seg, = (q.shape[0],)
+    pairs = sk.shape[1] // 128
+    count = seg // tile
+    row = lambda shape, f: pl.BlockSpec(shape, f)
+    return pl.pallas_call(
+        functools.partial(fwd_kernel, tile),
+        grid_spec=pltpu.PrefetchScalarGridSpec(
+            num_scalar_prefetch=1, grid=(pairs, count),
+            in_specs=[
+                row((tile,128), lambda h,i,f: (i,h+offs[0])),
+                row((seg,128), lambda h,i,f: (0,h+offs[1])),
+                row((seg,128), lambda h,i,f: (0,h+offs[2])),
+                row((128,128), lambda h,i,f: (0,h)),
+                row((128,128), lambda h,i,f: (0,h)),
+                row((1,tile), lambda h,i,f: (0,i)),
+                row((1,tile), lambda h,i,f: (0,i)),
+                row((128,1), lambda h,i,f: (0,0)),
+            ],
+            out_specs=[row((tile,128), lambda h,i,f: (i,h)), row((1,2,tile), lambda h,i,f: (h,0,i))],
+            scratch_shapes=[pltpu.VMEM((2,seg+128,128),BF), pltpu.VMEM((128,seg+128),BF), pltpu.VMEM((2,HEAD,tile),F32), pltpu.VMEM((2,1,tile),F32), pltpu.VMEM((2,1,tile),F32)],
+        ),
+        out_shape=[jax.ShapeDtypeStruct((seg,pairs*128),BF), jax.ShapeDtypeStruct((pairs,2,seg),F32)],
+        compiler_params=pltpu.CompilerParams(vmem_limit_bytes=48*2**20),
+    )(flags, q, k, v, sk, sv, start, doc, sdoc)
+
+def bwd_kernel(tile, flags, q_ref, k_ref, v_ref, do_ref, o_ref, sk_ref, sv_ref, lse_ref, start_ref, doc_ref, sdoc_ref,
+               dq_ref, dk_ref, dv_ref, dsk_ref, dsv_ref, qm, dom, dqt, delta):
+    j = pl.program_id(1)
+    seg = q_ref.shape[0]
+    count = seg // tile
+    lanes = lax.broadcasted_iota(jnp.int32, (1, 128), 1)
+    masks = [(lanes < HEAD).astype(BF), (lanes >= HEAD).astype(BF)]
+    @pl.when(j == 0)
+    def _():
+        dqt[...] = jnp.zeros_like(dqt)
+        for h in range(2):
+            qm[h] = q_ref[...] * masks[h]
+            dom[h] = do_ref[...] * masks[h]
+        def one(i, _):
+            at = pl.multiple_of(i * tile, tile)
+            prod = (do_ref[pl.ds(at, tile)].astype(F32) * o_ref[pl.ds(at, tile)].astype(F32)).T
+            for h in range(2):
+                delta[h, :, pl.ds(at, tile)] = jnp.sum(prod[h * HEAD:(h + 1) * HEAD], axis=0, keepdims=True)
+            return 0
+        lax.fori_loop(0, count, one, 0)
+    def block(i, kt, k_blk, v_blk, okay):
+        at = pl.multiple_of(i * tile, tile)
+        gk = gv = None
+        for h in range(2):
+            qh = qm[h, pl.ds(at, tile)]
+            dh = dom[h, pl.ds(at, tile)]
+            s = dot_nt(k_blk, qh)
+            dp = dot_nt(v_blk, dh)
+            p = jnp.exp(s - lse_ref[0, pl.ds(h, 1), pl.ds(at, tile)])
+            if okay is not None:
+                p = jnp.where(okay, p, 0.0)
+            ds = (p * (dp - delta[h, :, pl.ds(at, tile)])).astype(BF)
+            a = dot_nn(p.astype(BF), dh)
+            b = dot_nn(ds, qh)
+            gv = a if gv is None else gv + a
+            gk = b if gk is None else gk + b
+            dqt[pl.ds(h * HEAD, HEAD), pl.ds(at, tile)] += dot_nn(kt[h * HEAD:(h + 1) * HEAD], ds)
+        return gk, gv
+    @pl.when(j < count)
+    def _():
+        at_k = pl.multiple_of(j * tile, tile)
+        k_blk = k_ref[...]
+        v_blk = v_ref[...]
+        kt = k_blk.T
+        def masked_of(i):
+            places = at_k + lax.broadcasted_iota(jnp.int32, (tile, tile), 0)
+            mine = i * tile + lax.broadcasted_iota(jnp.int32, (tile, tile), 1)
+            return (places <= mine) & (places >= start_ref[:, pl.ds(pl.multiple_of(i * tile, tile), tile)])
+        gk, gv = block(j, kt, k_blk, v_blk, masked_of(j))
+        dkacc, dvacc = gk, gv
+        def loop(i, carry):
+            flag = flags[i * count + j]
+            def full(c):
+                gk, gv = block(i, kt, k_blk, v_blk, None)
+                return c[0] + gk, c[1] + gv
+            def part(c):
+                gk, gv = block(i, kt, k_blk, v_blk, masked_of(i))
+                return c[0] + gk, c[1] + gv
+            return lax.switch(flag, [lambda c: c, part, full], carry)
+        dkacc, dvacc = lax.fori_loop(j + 1, count, loop, (dkacc, dvacc))
+        dk_ref[...] = dkacc.astype(BF)
+        dv_ref[...] = dvacc.astype(BF)
+    @pl.when(j == count)
+    def _():
+        kt = sk_ref[...].T
+        def loop(i, carry):
+            okay = sdoc_ref[...] == doc_ref[:, pl.ds(pl.multiple_of(i * tile, tile), tile)]
+            gk, gv = block(i, kt, sk_ref[...], sv_ref[...], okay)
+            return carry[0] + gk, carry[1] + gv
+        z = jnp.zeros((128, 128), F32)
+        a, b = lax.fori_loop(0, count, loop, (z, z))
+        dsk_ref[...] = a.astype(BF)
+        dsv_ref[...] = b.astype(BF)
+        def fin(i, _):
+            at = pl.multiple_of(i * tile, tile)
+            dq_ref[pl.ds(at, tile)] = (dqt[:, pl.ds(at, tile)].T.astype(BF).astype(F32) * HEAD ** -0.5).astype(BF)
+            return 0
+        lax.fori_loop(0, count, fin, 0)
+
+def attn_bwd(q, k, v, do, o, sk, sv, lse, start, doc, sdoc, flags, tile=512, offs=(0,0,0)):
+    seg = q.shape[0]
+    pairs = sk.shape[1] // 128
+    count = seg // tile
+    row = lambda shape, f: pl.BlockSpec(shape, f)
+    last = count - 1
+    return pl.pallas_call(
+        functools.partial(bwd_kernel, tile),
+        grid_spec=pltpu.PrefetchScalarGridSpec(
+            num_scalar_prefetch=1, grid=(pairs, count + 1),
+            in_specs=[
+                row((seg,128), lambda h,j,f: (0,h+offs[0])),
+                row((tile,128), lambda h,j,f: (jnp.minimum(j,last),h+offs[1])),
+                row((tile,128), lambda h,j,f: (jnp.minimum(j,last),h+offs[2])),
+                row((seg,128), lambda h,j,f: (0,h)),
+                row((seg,128), lambda h,j,f: (0,h)),
+                row((128,128), lambda h,j,f: (0,h)),
+                row((128,128), lambda h,j,f: (0,h)),
+                row((1,2,seg), lambda h,j,f: (h,0,0)),
+                row((1,seg), lambda h,j,f: (0,0)),
+                row((1,seg), lambda h,j,f: (0,0)),
+                row((128,1), lambda h,j,f: (0,0)),
+            ],
+            out_specs=[row((seg,128), lambda h,j,f: (0,h)),
+                       row((tile,128), lambda h,j,f: (jnp.minimum(j,last),h)),
+                       row((tile,128), lambda h,j,f: (jnp.minimum(j,last),h)),
+                       row((128,128), lambda h,j,f: (0,h)), row((128,128), lambda h,j,f: (0,h))],
+            scratch_shapes=[pltpu.VMEM((2,seg,128),BF), pltpu.VMEM((2,seg,128),BF), pltpu.VMEM((128,seg),F32), pltpu.VMEM((2,1,seg),F32)],
+        ),
+        out_shape=[jax.ShapeDtypeStruct((seg,pairs*128),BF)]*3 + [jax.ShapeDtypeStruct((128,pairs*128),BF)]*2,
+        compiler_params=pltpu.CompilerParams(vmem_limit_bytes=48*2**20),
+    )(flags, q, k, v, do, o, sk, sv, lse, start, doc, sdoc)
+
+def make_meta(doc, tile):
+    seg=doc.shape[0]; count=seg//tile
+    place=jnp.arange(seg,dtype=jnp.int32)
+    new=jnp.concatenate([jnp.ones((1,),bool), doc[1:]!=doc[:-1]])
+    start=lax.cummax(jnp.where(new,place,0))
+    lo=doc[::tile]; hi=doc[tile-1::tile]
+    i=jnp.arange(count)
+    full=(lo[None,:]==hi[:,None])&(i[None,:]<i[:,None])
+    none=(hi[None,:]<lo[:,None])
+    flags=jnp.where(full,2,jnp.where(none,0,1)).astype(jnp.int32).reshape(-1)
+    return start.reshape(1,seg), flags
+
+
+X_FLIP = ((0, 1), (1, 0), (2, 3), (3, 2))
+Y_FLIP = ((0, 2), (2, 0), (1, 3), (3, 1))
+BOTH = ("rows", "seq")
+
+
+def over_x(block):
+    return lax.ppermute(block, "rows", X_FLIP)
+
+
+def over_y(block):
+    return lax.ppermute(block, "rows", Y_FLIP)
+
+
+def other_core(block):
+    return lax.ppermute(block, "fsdp", ((0, 1), (1, 0)))
+
+
+def cut(field, axis, parts):
+    size = field.shape[axis] // parts
+    return [lax.slice_in_dim(field, n * size, (n + 1) * size, axis=axis) for n in range(parts)]
+
+
+def gather(shard, axis, split):
+    me = lax.axis_index("rows")
+    block = lax.all_gather(shard, "seq", axis=axis, tiled=True)
+    first, second = cut(block, split, 2)
+    width = block.shape[axis]
+    from_x, from_y = over_x(first), over_y(second)
+    pieces = (
+        (0, first, second),
+        (1, from_x, over_x(second)),
+        (2, over_y(first), from_y),
+        (3, over_y(from_x), over_x(from_y)),
+    )
+    shape = list(block.shape)
+    shape[axis] = width * 4
+    whole = jnp.zeros(shape, block.dtype)
+    half = block.shape[split] // 2
+    for away, a, b in pieces:
+        for n, part in enumerate((a, b)):
+            at = [0] * len(shape)
+            at[axis] = (me ^ away) * width
+            at[split] = n * half
+            whole = lax.dynamic_update_slice(whole, part, at)
+    return whole
+
+
+def scatter(partial, axis, split):
+    me = lax.axis_index("rows")
+    width = partial.shape[axis] // 4
+
+    def block(field, away):
+        return lax.dynamic_slice_in_dim(field, (me ^ away) * width, width, axis)
+
+    first, second = cut(partial, split, 2)
+
+    def plus(own, moved):
+        return (own.astype(F32) + moved.astype(F32)).astype(BF)
+
+    far_a = over_x(block(first, 3))
+    far_b = over_y(block(second, 3))
+    near_a = over_x(block(first, 1))
+    near_b = over_y(block(second, 2))
+    last_a = over_y(plus(block(first, 2), far_a))
+    last_b = over_x(plus(block(second, 1), far_b))
+    sum_a = block(first, 0).astype(F32) + near_a.astype(F32) + last_a.astype(F32)
+    sum_b = block(second, 0).astype(F32) + near_b.astype(F32) + last_b.astype(F32)
+    mine = jnp.concatenate((sum_a.astype(BF), sum_b.astype(BF)), axis=split)
+    return lax.psum_scatter(mine, "seq", scatter_dimension=axis, tiled=True).astype(F32)
+
+
+def exchange(field):
+    count = lax.axis_size("seq")
+    me = lax.axis_index("seq")
+    core = lax.axis_index("fsdp")
+    half = field.shape[2] // 2
+    mine = lax.dynamic_slice_in_dim(field, core * half, half, 2)
+    got = jnp.zeros_like(mine)
+    own = lax.dynamic_slice_in_dim(mine, me, 1, 0)
+    got = lax.dynamic_update_slice_in_dim(got, own, me, 0)
+    for away in range(1, count):
+        block = lax.dynamic_slice_in_dim(mine, lax.rem(me + away, count), 1, 0)
+        moved = lax.ppermute(block, "seq", [(n, (n + away) % count) for n in range(count)])
+        got = lax.dynamic_update_slice_in_dim(got, moved, lax.rem(me + count - away, count), 0)
+    other = other_core(got)
+    low_half = jnp.where(core == 0, got, other)
+    high_half = jnp.where(core == 0, other, got)
+    return jnp.concatenate((low_half, high_half), axis=2)
+
+
+def shift_by(field, away):
+    count = lax.axis_size("seq")
+    perm = [(n, n + away) for n in range(count) if 0 <= n + away < count]
+    return lax.ppermute(field, "seq", perm)
+
+
+def both_halves(field):
+    low = field.astype(BF)
+    return low.astype(F32) + other_core(low).astype(F32)
+
+
+def norm_forward(field, gain_vec, shift_vec):
+    row_mean = jnp.mean(field, axis=-1, keepdims=True)
+    centered = field - row_mean
+    variance = jnp.mean(centered * centered, axis=-1, keepdims=True)
+    scale = lax.rsqrt(variance + norm_eps)
+    return (centered * scale * gain_vec + shift_vec).astype(BF), row_mean, scale
+
+
+def norm_backward(field, row_mean, scale, gain_vec, grad):
+    unit = (field - row_mean) * scale
+    scaled = grad * gain_vec
+    mean_one = jnp.mean(scaled, axis=-1, keepdims=True)
+    mean_two = jnp.mean(scaled * unit, axis=-1, keepdims=True)
+    d_field = scale * (scaled - mean_one - unit * mean_two)
+    return d_field, jnp.sum(grad * unit, axis=0), jnp.sum(grad, axis=0)
+
+
+def mm(a, b):
+    return dot_nn(a, b)
+
+
+def mm_tn(a, b):
+    return lax.dot_general(a, b, (((0,), (0,)), ((), ())), preferred_element_type=F32)
+
+
+def mm_nt(a, b):
+    return dot_nt(a, b)
+
+
+def layer_by_segment(
+    states,
+    doc_ids,
+    w_qkv,
+    w_out,
+    w_up,
+    w_down,
+    bias_qv,
+    bias_out,
+    bias_up,
+    bias_down,
+    gain_one,
+    shift_one,
+    gain_two,
+    shift_two,
+    cotangent,
+):
+    segs, width, model = states.shape[1:]
+    seg_len = segs * width
+    place = lax.axis_index("seq")
+    half = w_qkv.shape[2]
+    hidden_units = w_up.shape[1]
+    tile = 512
+
+    small = (bias_qv, bias_out, bias_up, bias_down, gain_one, shift_one, gain_two, shift_two)
+    sizes = [item.size for item in small]
+    packed = lax.all_gather(jnp.concatenate([item.reshape(-1) for item in small]), BOTH, axis=0)
+    cuts = []
+    at = 0
+    for size in sizes:
+        cuts.append(packed[:, at : at + size].astype(F32))
+        at += size
+    shards = packed.shape[0]
+
+    def spread_last(field, lead):
+        return jnp.moveaxis(field.reshape(shards, *lead, -1), 0, len(lead)).reshape(-1)
+
+    bias_pair = jnp.moveaxis(cuts[0].reshape(shards, 2, half // HEAD, -1), 0, 2).reshape(2, half)
+    bias_o = cuts[1].reshape(-1)
+    bias_u = spread_last(cuts[2], (hidden_units // HEAD,))
+    bias_d = cuts[3].reshape(-1)
+    gain_a, shift_a, gain_b, shift_b = [item.reshape(-1) for item in cuts[4:]]
+
+    qkv_full = gather(w_qkv, 1, 2)
+    tokens = exchange(states[0]).reshape(seg_len, model)
+    out_full = gather(w_out, 1, 0)
+    up_full = gather(w_up, 0, 1)
+    down_full = gather(w_down, 1, 0)
+    grad_out = exchange(cotangent[0]).reshape(seg_len, model)
+
+    docs = doc_ids[0]
+    my_docs = lax.dynamic_index_in_dim(docs, place, 0, keepdims=False)
+    start, flags = make_meta(my_docs, tile)
+    tails = docs[:, seg_len - SUMM :]
+    before_one = lax.dynamic_index_in_dim(tails, jnp.maximum(place - 1, 0), 0, keepdims=False)
+    before_two = lax.dynamic_index_in_dim(tails, jnp.maximum(place - 2, 0), 0, keepdims=False)
+    sum_docs = jnp.concatenate(
+        (
+            jnp.where(place >= 1, before_one, -1),
+            jnp.where(place >= 2, before_two, -1),
+            jnp.full((128 - 2 * SUMM,), -1, jnp.int32),
+        )
+    ).reshape(128, 1)
+    doc_row = my_docs.reshape(1, seg_len)
+
+    tokens_f = tokens.astype(F32)
+    normed_one, mean_one, scale_one = norm_forward(tokens_f, gain_a, shift_a)
+    query = ((mm(normed_one, qkv_full[0]) + bias_pair[0]) * HEAD**-0.5).astype(BF)
+    keys = mm(normed_one, qkv_full[1]).astype(BF)
+    values = (mm(normed_one, qkv_full[2]) + bias_pair[1]).astype(BF)
+    tail = jnp.stack((keys[seg_len - SUMM :], values[seg_len - SUMM :]))
+    lent = jnp.concatenate((shift_by(tail, 1), shift_by(tail, 2)), axis=1)
+    lent = jnp.pad(lent, ((0, 0), (0, 128 - 2 * SUMM), (0, 0)))
+    mixed, log_sum = attn_fwd(
+        query, keys, values, lent[0], lent[1], start, doc_row, sum_docs, flags, tile
+    )
+    hidden = tokens_f + both_halves(mm(mixed, out_full)) + bias_o
+    normed_two, mean_two, scale_two = norm_forward(hidden, gain_b, shift_b)
+    up_proj = mm(normed_two, up_full) + bias_u
+    bell = jnp.exp(-0.5 * up_proj * up_proj)
+    area = 0.5 * (1.0 + lax.erf(up_proj * (0.5**0.5)))
+    activated = (up_proj * area).astype(BF)
+    slope = (area + up_proj * bell * 0.3989422804014327).astype(BF)
+
+    grad_w_down = scatter(mm_tn(activated, grad_out).astype(BF), 1, 0)
+    d_up = (mm_nt(grad_out, down_full) * slope.astype(F32)).astype(BF)
+    grad_w_up = scatter(mm_tn(normed_two, d_up).astype(BF), 0, 1)
+    d_norm_two = both_halves(mm_nt(d_up, up_full))
+    d_hidden_ln, grad_gain_two, grad_shift_two = norm_backward(
+        hidden, mean_two, scale_two, gain_b, d_norm_two
+    )
+    d_hidden = grad_out.astype(F32) + d_hidden_ln
+    d_hidden_low = d_hidden.astype(BF)
+    d_mixed = mm_nt(d_hidden_low, out_full).astype(BF)
+    grad_w_out = scatter(mm_tn(mixed, d_hidden_low).astype(BF), 1, 0)
+
+    out_tokens = (hidden + both_halves(mm(activated, down_full)) + bias_d).astype(BF)
+    out_states = exchange(out_tokens.reshape(segs, width, model))[None]
+
+    d_pre, d_keys, d_values, d_lent_k, d_lent_v = attn_bwd(
+        query, keys, values, d_mixed, mixed, lent[0], lent[1], log_sum, start, doc_row, sum_docs, flags, tile
+    )
+    d_lent = jnp.stack((d_lent_k, d_lent_v))
+    back = shift_by(d_lent[:, :SUMM], -1).astype(F32) + shift_by(
+        d_lent[:, SUMM : 2 * SUMM], -2
+    ).astype(F32)
+    ends = jnp.stack((d_keys[seg_len - SUMM :], d_values[seg_len - SUMM :])).astype(F32) + back
+    ends = ends.astype(BF)
+    d_keys = lax.dynamic_update_slice(d_keys, ends[0], (seg_len - SUMM, 0))
+    d_values = lax.dynamic_update_slice(d_values, ends[1], (seg_len - SUMM, 0))
+    d_qkv = (d_pre, d_keys, d_values)
+    grad_w_qkv = scatter(
+        jnp.stack([mm_tn(normed_one, item).astype(BF) for item in d_qkv]), 1, 2
+    )
+    d_norm_one = both_halves(
+        mm_nt(d_pre, qkv_full[0]) + mm_nt(d_keys, qkv_full[1]) + mm_nt(d_values, qkv_full[2])
+    )
+    d_tokens_ln, grad_gain_one, grad_shift_one = norm_backward(
+        tokens_f, mean_one, scale_one, gain_a, d_norm_one
+    )
+    grad_tokens = (d_hidden + d_tokens_ln).astype(BF)
+    grad_states = exchange(grad_tokens.reshape(segs, width, model))[None]
+
+    def column_sum(field):
+        return jnp.sum(field.astype(F32), axis=0)
+
+    sums = (
+        jnp.moveaxis(
+            jnp.stack((column_sum(d_pre), column_sum(d_values))).reshape(2, half // HEAD, shards, -1), 2, 0
+        ),
+        column_sum(d_hidden),
+        jnp.moveaxis(column_sum(d_up).reshape(hidden_units // HEAD, shards, -1), 1, 0),
+        column_sum(grad_out),
+        grad_gain_one,
+        grad_shift_one,
+        grad_gain_two,
+        grad_shift_two,
+    )
+    vector = jnp.concatenate([item.reshape(shards, -1) for item in sums], axis=1)
+    vector = lax.psum_scatter(vector, BOTH, scatter_dimension=0, tiled=False)
+    small_grads = []
+    at = 0
+    for item, size in zip(small, sizes):
+        small_grads.append(vector[at : at + size].reshape(item.shape))
+        at += size
+    return (out_states, grad_states, grad_w_qkv, grad_w_out, grad_w_up, grad_w_down, *small_grads)
+
+
 def solution(mesh):
+    whole_segments = mesh.shape["seq"] == SEGS and mesh.shape["rows"] == 4
     return jax.shard_map(
-        local,
+        layer_by_segment if whole_segments else local,
         mesh=mesh,
         in_specs=(
             P("rows", None, "seq", None),

time: 5320 us -> 2310 us (0.43)
  waiting for transfers between devices: 2940 us -> 771 us
  matrix products: 1190 us -> 444 us
  other arithmetic: 673 us -> 208 us
  Pallas kernels: 0 us -> 286 us
  starting transfers between devices: 0.69 us -> 138 us
  blocking collectives: 306 us -> 212 us
    reduce_scatter x5 -> x1, waiting for transfers between devices: 2310 us -> 0.01 us  [scatter(): lax.psum_scatter(mine, 'seq', scatter_dimension=axis, tiled=True)]
    dot_general x50 -> x18, matrix products: 1190 us -> 444 us  [the longest x6 166 us: dot_nt(): lax.dot_general(a, b, (((1,), (1,)), ((), ())), preferred_element_type=F32)]
    ppermute x0 -> x72, waiting for transfers between devices: none -> 737 us  [the longest x24 299 us: over_x(): return lax.ppermute(block, 'rows', X_FLIP)]
    all_gather x6 -> x4, waiting for transfers between devices: 534 us -> 0.04 us  [gather(): block = lax.all_gather(shard, 'seq', axis=axis, tiled=True)]
    dynamic_update_slice x4 -> x0, other arithmetic: 303 us -> none  [local(): lax.map(segment_back, seg_inputs)]
    pallas_call x0 -> x2, Pallas kernels: none -> 286 us  [the longest x1 163 us: attn_bwd(): pl.pallas_call(functools.partial(bwd_kernel, tile), grid_spec=pltpu.Prefe...]
    ppermute x0 -> x72, starting transfers between devices: none -> 137 us  [the longest x24 60.7 us: over_x(): return lax.ppermute(block, 'rows', X_FLIP)]
    reduce_sum x13 -> x10, other arithmetic: 198 us -> 86.4 us  [the longest x4 34.1 us: column_sum(): return jnp.sum(field.astype(F32), axis=0)]
  transfers between devices with their start and end apart: 17 -> 81, of which waited for: 13 -> 32; matrix products, arithmetic and copies ran while one was open for 19% -> 29% of each run, Pallas kernels for 0% -> 12%
where the time goes in v1:
time: 2310 us
  waiting for transfers between devices  771 us (33%)
  matrix products  444 us (19%)
  Pallas kernels  286 us (12%)
  local copies, waits for them, and re-layouts  231 us (10%)
  blocking collectives  212 us (9%)
  other arithmetic  208 us (9%)
  starting transfers between devices  138 us (6%)
    ppermute x24, waiting for transfers between devices, over_x(): return lax.ppermute(block, 'rows', X_FLIP)  299 us
    ppermute x24, waiting for transfers between devices, over_y(): return lax.ppermute(block, 'rows', Y_FLIP)  261 us
    all_gather x1, blocking collectives, layer_by_segment(): lax.all_gather(jnp.concatenate([item.reshape(-1) for item in small]), BOT...  212 us
    ppermute x12, waiting for transfers between devices, exchange(): lax.ppermute(block, 'seq', [(n, (n + away) % count) for n in range(count)])  172 us
    dot_general x6, matrix products, dot_nt(): lax.dot_general(a, b, (((1,), (1,)), ((), ())), preferred_element_type=F32)  166 us
    pallas_call x1, Pallas kernels, attn_bwd(): pl.pallas_call(functools.partial(bwd_kernel, tile), grid_spec=pltpu.Prefe...  163 us
    dot_general x6, matrix products, dot_nn(): lax.dot_general(a, b, (((1,), (0,)), ((), ())), preferred_element_type=F32)  148 us
    dot_general x6, matrix products, mm_tn(): lax.dot_general(a, b, (((0,), (0,)), ((), ())), preferred_element_type=F32)  130 us
  transfers between devices with their start and end apart: 81, of which 32 were waited for; matrix products, arithmetic and copies ran while one was open for 29% of the time, Pallas kernels for 12%

profile of v1, /device:TPU:0, one launch (start us, length us, event | category | flops | bytes accessed | tf_op | source)
XLA Modules:
  0.0 2305.7 jit_solution(11376569258186917425)
XLA Ops:
  62.0 34.2 %collective-permute-start.37 = (bf16[1,512,1024]{2,1,0:T(8,128)(2,1)}, bf16[1,512,1024]{2,1,0:T(8,128)(2,1)S(1)}, u32[]{:S(2)}, u32[]{:S(2)}) collective-permute-start(bf16[1,512,1024]{2,1,0:T(8,128)(2,1)} %get-tuple-element.143), channel_id=1, source_target_pairs={{0,4},{2,6},{4,0},{6,2},{1,5},{3,7},{5,1},{7,3},{8,12},{10,14},{12... | collective-permute-start | bytes 3145736 | tf_op jit(solution)/shard_map/ppermute | solution.py:644
  109.7 212.3 %all-gather.1 = bf16[16,1,1152]{2,1,0:T(2,128)(2,1)S(1)} all-gather(bf16[1,1,1152]{2,1,0:T(2,128)(2,1)S(1)} %reshape.355), channel_id=2, replica_groups=mesh['rows'=4,'seq'=4,'fsdp'=2] {'rows','seq'}, dimensions={0}, use_global_device_ids=true | all-gather | bytes 39168 | tf_op jit(solution)/shard_map/all_gather | solution.py:718
  415.5 31.7 %collective-permute-done.4 = bf16[3,512,512]{2,1,0:T(8,128)(2,1)S(1)} collective-permute-done((bf16[3,512,512]{2,1,0:T(8,128)(2,1)}, bf16[3,512,512]{2,1,0:T(8,128)(2,1)S(1)}, u32[]{:S(2)}, u32[]{:S(2)}) %collective-permute-start.4) | collective-permute-done | bytes 1572896 | tf_op jit(solution)/shard_map/ppermute | solution.py:568
  518.1 122.4 %shard_map.254 = (bf16[2048,1024]{1,0:T(8,128)(2,1)S(1)}, f32[8,2,2048]{2,1,0:T(2,128)S(1)}) custom-call(s32[16]{0:T(128)S(1)} %select_n.223.flags, bf16[2048,1024]{1,0:T(8,128)(2,1)} %multiply_convert_fusion.2.q_ref, bf16[2048,1024]{1,0:T(8,128)(2,1)} %copy-done.29, bf16[2048,1024]{1,0:T(8,128)(2,1)} %copy-done.30, ...), custom_call_target="tpu_custom_call" | custom-call | tf_op jit(solution)/shard_map/pallas_call | solution.py:416
  689.8 39.2 %collective-permute-done.20 = bf16[512,2048]{1,0:T(8,128)(2,1)} collective-permute-done((bf16[512,2048]{1,0:T(8,128)(2,1)}, bf16[512,2048]{1,0:T(8,128)(2,1)}, u32[]{:S(2)}, u32[]{:S(2)}) %collective-permute-start.20) | collective-permute-done | bytes 2097184 | tf_op jit(solution)/shard_map/ppermute | solution.py:568
  736.9 37.1 %collective-permute-done.19 = bf16[512,2048]{1,0:T(8,128)(2,1)} collective-permute-done((bf16[512,2048]{1,0:T(8,128)(2,1)}, bf16[512,2048]{1,0:T(8,128)(2,1)}, u32[]{:S(2)}, u32[]{:S(2)}) %collective-permute-start.19) | collective-permute-done | bytes 2097184 | tf_op jit(solution)/shard_map/ppermute | solution.py:568
  827.4 36.4 %collective-permute-done.25 = bf16[2048,512]{1,0:T(8,128)(2,1)} collective-permute-done((bf16[2048,512]{1,0:T(8,128)(2,1)}, bf16[2048,512]{1,0:T(8,128)(2,1)}, u32[]{:S(2)}, u32[]{:S(2)}) %collective-permute-start.25) | collective-permute-done | bytes 2097184 | tf_op jit(solution)/shard_map/ppermute | solution.py:568
  913.7 41.2 %collective-permute-done.29 = bf16[2048,512]{1,0:T(8,128)(2,1)S(1)} collective-permute-done((bf16[2048,512]{1,0:T(8,128)(2,1)}, bf16[2048,512]{1,0:T(8,128)(2,1)S(1)}, u32[]{:S(2)}, u32[]{:S(2)}) %collective-permute-start.29) | collective-permute-done | bytes 2097184 | tf_op jit(solution)/shard_map/ppermute | solution.py:572
  979.5 50.9 %multiply_convert_fusion.1 = (bf16[2048,4096]{1,0:T(8,128)(2,1)}, f32[2048,4096]{1,0:T(8,128)}) fusion(f32[4096]{0:T(1024)S(1)} %reshape.350, bf16[2048,4096]{1,0:T(8,128)(2,1)} %constant_dynamic-update-slice_fusion.49, f32[2048,2048]{1,0:T(8,128)} %get-tuple-element.116, f32[2048]{0:T(1024)S(1)} %copy-done.66, f32[2048]{0:T(1024)S(1)} %copy-done.55, ...), kind=kOutput, calls=%fused_computation.8 | convolution fusion | flops 34431041536 | bytes 83935232 | tf_op jit(solution)/shard_map/dot_general | solution.py:350
  1030.4 42.7 %convolution_convert_fusion.4 = bf16[2048,2048]{1,0:T(8,128)(2,1)} fusion(bf16[2048,4096]{1,0:T(8,128)(2,1)} %get-tuple-element.196, bf16[4096,2048]{1,0:T(8,128)(2,1)} %constant_dynamic-update-slice_fusion.45), kind=kOutput, calls=%fused_computation.61 | convolution fusion | flops 34363932672 | bytes 41943040 | tf_op jit(solution)/shard_map/dot_general | solution.py:350
  1073.1 57.6 %convert_reduce_fusion = (f32[4096]{0:T(1024)}, bf16[2048,4096]{1,0:T(8,128)(2,1)}) fusion(f32[2048,4096]{1,0:T(8,128)} %get-tuple-element.197, f32[4096]{0:T(1024)S(1)} %reshape.350, bf16[2048,2048]{1,0:T(8,128)(2,1)} %bitcast.219, bf16[4096,2048]{1,0:T(8,128)(2,1)} %constant_dynamic-update-slice_fusion.45), kind=kOutput, calls=%fused_computation.6 | convolution fusion | flops 34485563392 | bytes 75530240 | tf_op jit(solution)/shard_map/dot_general | solution.py:349
  1130.7 42.7 %convolution_convert_fusion.3 = bf16[2048,2048]{1,0:T(8,128)(2,1)} fusion(bf16[2048,4096]{1,0:T(8,128)(2,1)} %get-tuple-element.199, bf16[2048,4096]{1,0:T(8,128)(2,1)} %constant_dynamic-update-slice_fusion.49), kind=kOutput, calls=%fused_computation.60 | convolution fusion | flops 34363932672 | bytes 41943040 | tf_op jit(solution)/shard_map/dot_general | solution.py:349
  1173.9 42.0 %convolution_convert_fusion = bf16[4096,2048]{1,0:T(8,128)(2,1)} fusion(bf16[2048,4096]{1,0:T(8,128)(2,1)} %get-tuple-element.196, bf16[2048,2048]{1,0:T(8,128)(2,1)} %bitcast.220), kind=kOutput, calls=%fused_computation.42 | convolution fusion | flops 34368126976 | bytes 41943040 | tf_op jit(solution)/shard_map/dot_general | solution.py:685
  1251.3 29.2 %fusion.54 = (f32[2048]{0:T(1024)}, f32[2048,2048]{1,0:T(8,128)}, bf16[2048,2048]{1,0:T(8,128)(2,1)}) fusion(f32[2048]{0:T(1024)S(1)} %broadcast_multiply_fusion.2, f32[2048,2048]{1,0:T(8,128)} %get-tuple-element.116, f32[2048]{0:T(1024)S(1)} %copy-done.45, f32[2048]{0:T(1024)S(1)} %broadcast_multiply_fusion.3, f32[2048]{0:T(1024)S(1)} %copy-done.56, ...), kind=kLoop, calls=%fused_computation.259 | loop fusion | flops 79689728 | bytes 83943424 | tf_op jit(solution)/shard_map/reduce_sum | solution.py:816
  1296.4 31.4 %collective-permute-done.67 = bf16[2048,512]{1,0:T(8,128)(2,1)} collective-permute-done((bf16[2048,512]{1,0:T(8,128)(2,1)}, bf16[2048,512]{1,0:T(8,128)(2,1)}, u32[]{:S(2)}, u32[]{:S(2)}) %collective-permute-start.67) | collective-permute-done | bytes 2097184 | tf_op jit(solution)/shard_map/ppermute | solution.py:568
  1367.5 46.8 %convolution_convert_fusion.1 = bf16[2048,4096]{1,0:T(8,128)(2,1)} fusion(bf16[2048,4096]{1,0:T(8,128)(2,1)} %get-tuple-element.199, f32[2048,2048]{1,0:T(8,128)} %get-tuple-element.116, f32[2048]{0:T(1024)S(1)} %copy-done.67, f32[2048]{0:T(1024)S(1)} %copy-done.56, f32[2048]{0:T(1024)S(1)} %copy-done.54, f32[2048]{0:T(1024)S(1)} %copy-done.45), kind=kOutput, calls=%fused_computation.43 | convolution fusion | flops 34389098496 | bytes 50364416 | tf_op jit(solution)/shard_map/dot_general | solution.py:685
  1414.4 37.7 %collective-permute-done.68 = bf16[2048,512]{1,0:T(8,128)(2,1)} collective-permute-done((bf16[2048,512]{1,0:T(8,128)(2,1)}, bf16[2048,512]{1,0:T(8,128)(2,1)}, u32[]{:S(2)}, u32[]{:S(2)}) %collective-permute-start.68) | collective-permute-done | bytes 2097184 | tf_op jit(solution)/shard_map/ppermute | solution.py:572
  1484.4 163.2 %shard_map.255 = (bf16[2048,1024]{1,0:T(8,128)(2,1)S(1)}, bf16[2048,1024]{1,0:T(8,128)(2,1)}, bf16[2048,1024]{1,0:T(8,128)(2,1)}, bf16[128,1024]{1,0:T(8,128)(2,1)S(1)}, bf16[128,1024]{1,0:T(8,128)(2,1)S(1)}) custom-call(s32[16]{0:T(128)S(1)} %copy-done.15, bf16[2048,1024]{1,0:T(8,128)(2,1)} %multiply_convert_fusion.2.q_ref, bf16[2048,1024]{1,0:T(8,128)(2,1)} %copy-done.29, ...), custom_call_target="tpu_custom_call" | custom-call | tf_op jit(solution)/shard_map/pallas_call | solution.py:522
  1741.9 46.3 %collective-permute-done.61 = bf16[512,2048]{1,0:T(8,128)(2,1)} collective-permute-done((bf16[512,2048]{1,0:T(8,128)(2,1)}, bf16[512,2048]{1,0:T(8,128)(2,1)}, u32[]{:S(2)}, u32[]{:S(2)}) %collective-permute-start.61) | collective-permute-done | bytes 2097184 | tf_op jit(solution)/shard_map/ppermute | solution.py:568
  1801.1 32.0 %collective-permute-done.60 = bf16[512,2048]{1,0:T(8,128)(2,1)} collective-permute-done((bf16[512,2048]{1,0:T(8,128)(2,1)}, bf16[512,2048]{1,0:T(8,128)(2,1)}, u32[]{:S(2)}, u32[]{:S(2)}) %collective-permute-start.60) | collective-permute-done | bytes 2097184 | tf_op jit(solution)/shard_map/ppermute | solution.py:568
  1845.0 39.4 %collective-permute-done.63 = bf16[512,2048]{1,0:T(8,128)(2,1)} collective-permute-done((bf16[512,2048]{1,0:T(8,128)(2,1)S(1)}, bf16[512,2048]{1,0:T(8,128)(2,1)}, u32[]{:S(2)}, u32[]{:S(2)}) %collective-permute-start.63) | collective-permute-done | bytes 2097184 | tf_op jit(solution)/shard_map/ppermute | solution.py:572
  1966.7 72.0 %collective-permute-done.32 = bf16[1,512,1024]{2,1,0:T(8,128)(2,1)} collective-permute-done((bf16[1,512,1024]{2,1,0:T(8,128)(2,1)}, bf16[1,512,1024]{2,1,0:T(8,128)(2,1)}, u32[]{:S(2)}, u32[]{:S(2)}) %collective-permute-start.32) | collective-permute-done | bytes 1048608 | tf_op jit(solution)/shard_map/ppermute | solution.py:644
  2106.4 34.9 %collective-permute-done.50 = bf16[3,512,512]{1,2,0:T(8,128)(2,1)} collective-permute-done((bf16[3,512,512]{1,2,0:T(8,128)(2,1)S(1)}, bf16[3,512,512]{1,2,0:T(8,128)(2,1)}, u32[]{:S(2)}, u32[]{:S(2)}) %collective-permute-start.50) | collective-permute-done | bytes 1572896 | tf_op jit(solution)/shard_map/ppermute | solution.py:572
  2261.4 32.3 %reduce-scatter.14.cloned.1.call-done = bf16[128,3072]{1,0:T(8,128)(2,1)} async-done(((bf16[512,3072]{1,0:T(8,128)(2,1)}), bf16[128,3072]{1,0:T(8,128)(2,1)}) %reduce-scatter.14.cloned.1.call-update) | async-done | bytes 786448
  (556 shorter events, 934.1 us)
Async XLA Ops:
  7.3 317.3 %all-gather.9.cloned.1.call-start = ((), (), s32[]{:S(2)}) async-start(), calls=%async_computation.5 | async-start | bytes 1310720 | tf_op jit(solution)/shard_map/all_gather | solution.py:586
  8.0 359.0 %all-gather.7.cloned.1.call-start = ((), (), s32[]{:S(2)}) async-start(), calls=%async_computation.4 | async-start | bytes 3932160 | tf_op jit(solution)/shard_map/all_gather | solution.py:586
  8.7 646.3 %all-gather.11.cloned.1.call-start = ((), (), s32[]{:S(2)}) async-start(), calls=%async_computation.6 | async-start | bytes 5242880 | tf_op jit(solution)/shard_map/all_gather | solution.py:586
  9.5 675.7 %all-gather.13.cloned.1.call-start = ((), (), s32[]{:S(2)}) async-start(), calls=%async_computation.7 | async-start | bytes 5242880 | tf_op jit(solution)/shard_map/all_gather | solution.py:586
  27.0 312.9 %collective-permute-start.38 = (bf16[1,512,1024]{2,1,0:T(8,128)(2,1)}, bf16[1,512,1024]{2,1,0:T(8,128)(2,1)S(1)}, u32[]{:S(2)}, u32[]{:S(2)}) collective-permute-start(bf16[1,512,1024]{2,1,0:T(8,128)(2,1)} %get-tuple-element.141), channel_id=1, source_target_pairs={{0,6},{2,0},{4,2},{6,4},{1,7},{3,1},{5,3},{7,5},{8,14},{10,8},{12,... | collective-permute-start | bytes 3145736 | tf_op jit(solution)/shard_map/ppermute | solution.py:644
  27.5 307.2 %collective-permute-start.36 = (bf16[1,512,1024]{2,1,0:T(8,128)(2,1)}, bf16[1,512,1024]{2,1,0:T(8,128)(2,1)S(1)}, u32[]{:S(2)}, u32[]{:S(2)}) collective-permute-start(bf16[1,512,1024]{2,1,0:T(8,128)(2,1)} %get-tuple-element.142), channel_id=1, source_target_pairs={{0,2},{2,4},{4,6},{6,0},{1,3},{3,5},{5,7},{7,1},{8,10},{10,12},{12... | collective-permute-start | bytes 3145736 | tf_op jit(solution)/shard_map/ppermute | solution.py:644
  29.0 2190.2 %reduce-scatter.16.cloned.1.call-start = ((), (), s32[]{:S(2)}) async-start(), calls=%async_computation.10 | async-start | bytes 1310720
  62.0 275.9 %collective-permute-start.37 = (bf16[1,512,1024]{2,1,0:T(8,128)(2,1)}, bf16[1,512,1024]{2,1,0:T(8,128)(2,1)S(1)}, u32[]{:S(2)}, u32[]{:S(2)}) collective-permute-start(bf16[1,512,1024]{2,1,0:T(8,128)(2,1)} %get-tuple-element.143), channel_id=1, source_target_pairs={{0,4},{2,6},{4,0},{6,2},{1,5},{3,7},{5,1},{7,3},{8,12},{10,14},{12... | collective-permute-start | bytes 3145736 | tf_op jit(solution)/shard_map/ppermute | solution.py:644
  109.7 270.4 %collective-permute-start.3 = (bf16[4,512,1024]{2,1,0:T(8,128)(2,1)}, bf16[4,512,1024]{2,1,0:T(8,128)(2,1)}, u32[]{:S(2)}, u32[]{:S(2)}) collective-permute-start(bf16[4,512,1024]{2,1,0:T(8,128)(2,1)} %constant_dynamic-update-slice_fusion.29), channel_id=1, source_target_pairs={{0,1},{1,0},{2,3},{3,2},{4,5},{5,4},{6,7},{7,6},{8,9},{9,8},{10,11... | collective-permute-start | bytes 12582920 | tf_op jit(solution)/shard_map/ppermute | solution.py:576
  353.6 328.8 %collective-permute-start.39 = (bf16[4,512,1024]{2,1,0:T(8,128)(2,1)}, bf16[4,512,1024]{2,1,0:T(8,128)(2,1)}, u32[]{:S(2)}, u32[]{:S(2)}) collective-permute-start(bf16[4,512,1024]{2,1,0:T(8,128)(2,1)} %constant_dynamic-update-slice_fusion.3), channel_id=1, source_target_pairs={{0,1},{1,0},{2,3},{3,2},{4,5},{5,4},{6,7},{7,6},{8,9},{9,8},{10,11... | collective-permute-start | bytes 12582920 | tf_op jit(solution)/shard_map/ppermute | solution.py:576
  655.0 303.1 %collective-permute-start.18 = (bf16[2048,2048]{1,0:T(8,128)(2,1)}, bf16[2048,2048]{1,0:T(8,128)(2,1)}, u32[]{:S(2)}, u32[]{:S(2)}) collective-permute-start(bf16[2048,2048]{1,0:T(8,128)(2,1)} %convolution_convert_fusion.2), channel_id=1, source_target_pairs={{0,1},{1,0},{2,3},{3,2},{4,5},{5,4},{6,7},{7,6},{8,9},{9,8},{10,11... | collective-permute-start | bytes 25165832 | tf_op jit(solution)/shard_map/ppermute | solution.py:576
  1234.2 180.2 %collective-permute-start.66 = (bf16[2048,512]{1,0:T(8,128)(2,1)S(1)}, bf16[2048,512]{1,0:T(8,128)(2,1)}, u32[]{:S(2)}, u32[]{:S(2)}) collective-permute-start(bf16[2048,512]{1,0:T(8,128)(2,1)S(1)} %get-tuple-element.125), channel_id=1, source_target_pairs={{0,8},{8,0},{16,24},{24,16},{1,9},{9,1},{17,25},{25,17},{2,10},{10... | collective-permute-start | bytes 6291464 | tf_op jit(solution)/shard_map/ppermute | solution.py:568
  1367.5 853.8 %reduce-scatter.18.cloned.1.call-start = ((), (), s32[]{:S(2)}) async-start(), calls=%async_computation.11 | async-start | bytes 5242880
  1468.3 756.0 %reduce-scatter.12.cloned.1.call-start = ((), (), s32[]{:S(2)}) async-start(), calls=%async_computation.8 | async-start | bytes 5242880 | tf_op jit(solution)/shard_map/reduce_scatter | solution.py:630
  1710.0 202.9 %collective-permute-start.43 = (bf16[2048,2048]{1,0:T(8,128)(2,1)}, bf16[2048,2048]{1,0:T(8,128)(2,1)}, u32[]{:S(2)}, u32[]{:S(2)}) collective-permute-start(bf16[2048,2048]{1,0:T(8,128)(2,1)} %add_convert_fusion), channel_id=1, source_target_pairs={{0,1},{1,0},{2,3},{3,2},{4,5},{5,4},{6,7},{7,6},{8,9},{9,8},{10,11... | collective-permute-start | bytes 25165832 | tf_op jit(solution)/shard_map/ppermute | solution.py:576
  1891.3 350.0 %all-reduce.4.cloned.1.call-start = ((), (), s32[]{:S(2)}) async-start(), calls=%async_computation.12 | async-start | bytes 1179648
  1906.1 156.3 %collective-permute-start.34 = (bf16[1,512,1024]{2,1,0:T(8,128)(2,1)}, bf16[1,512,1024]{2,1,0:T(8,128)(2,1)}, u32[]{:S(2)}, u32[]{:S(2)}) collective-permute-start(bf16[1,512,1024]{2,1,0:T(8,128)(2,1)} %get-tuple-element.146), channel_id=1, source_target_pairs={{0,6},{2,0},{4,2},{6,4},{1,7},{3,1},{5,3},{7,5},{8,14},{10,8},{12,... | collective-permute-start | bytes 3145736 | tf_op jit(solution)/shard_map/ppermute | solution.py:644
  1911.1 149.0 %collective-permute-start.33 = (bf16[1,512,1024]{2,1,0:T(8,128)(2,1)}, bf16[1,512,1024]{2,1,0:T(8,128)(2,1)}, u32[]{:S(2)}, u32[]{:S(2)}) collective-permute-start(bf16[1,512,1024]{2,1,0:T(8,128)(2,1)} %get-tuple-element.147), channel_id=1, source_target_pairs={{0,4},{2,6},{4,0},{6,2},{1,5},{3,7},{5,1},{7,3},{8,12},{10,14},{12... | collective-permute-start | bytes 3145736 | tf_op jit(solution)/shard_map/ppermute | solution.py:644
  1911.1 127.5 %collective-permute-start.32 = (bf16[1,512,1024]{2,1,0:T(8,128)(2,1)}, bf16[1,512,1024]{2,1,0:T(8,128)(2,1)}, u32[]{:S(2)}, u32[]{:S(2)}) collective-permute-start(bf16[1,512,1024]{2,1,0:T(8,128)(2,1)} %get-tuple-element.148), channel_id=1, source_target_pairs={{0,2},{2,4},{4,6},{6,0},{1,3},{3,5},{5,7},{7,1},{8,10},{10,12},{12... | collective-permute-start | bytes 3145736 | tf_op jit(solution)/shard_map/ppermute | solution.py:644
  1961.7 114.0 %collective-permute-start.49 = (bf16[3,512,512]{1,2,0:T(8,128)(2,1)}, bf16[3,512,512]{1,2,0:T(8,128)(2,1)S(1)}, u32[]{:S(2)}, u32[]{:S(2)}) collective-permute-start(bf16[3,512,512]{1,2,0:T(8,128)(2,1)} %get-tuple-element.156), channel_id=1, source_target_pairs={{0,8},{8,0},{16,24},{24,16},{1,9},{9,1},{17,25},{25,17},{2,10},{10... | collective-permute-start | bytes 4718600 | tf_op jit(solution)/shard_map/ppermute | solution.py:568
  1966.2 112.6 %collective-permute-start.52 = (bf16[3,512,512]{1,2,0:T(8,128)(2,1)}, bf16[3,512,512]{1,2,0:T(8,128)(2,1)S(1)}, u32[]{:S(2)}, u32[]{:S(2)}) collective-permute-start(bf16[3,512,512]{1,2,0:T(8,128)(2,1)} %get-tuple-element.158), channel_id=1, source_target_pairs={{0,16},{16,0},{8,24},{24,8},{1,17},{17,1},{9,25},{25,9},{2,18},{18... | collective-permute-start | bytes 4718600 | tf_op jit(solution)/shard_map/ppermute | solution.py:572
  2064.7 162.4 %collective-permute-start.35 = (bf16[4,512,1024]{2,1,0:T(8,128)(2,1)}, bf16[4,512,1024]{2,1,0:T(8,128)(2,1)}, u32[]{:S(2)}, u32[]{:S(2)}) collective-permute-start(bf16[4,512,1024]{2,1,0:T(8,128)(2,1)} %constant_dynamic-update-slice_fusion.6), channel_id=1, source_target_pairs={{0,1},{1,0},{2,3},{3,2},{4,5},{5,4},{6,7},{7,6},{8,9},{9,8},{10,11... | collective-permute-start | bytes 12582920 | tf_op jit(solution)/shard_map/ppermute | solution.py:576
  2073.5 220.2 %reduce-scatter.14.cloned.1.call-start = ((), (), s32[]{:S(2)}) async-start(), calls=%async_computation.9 | async-start | bytes 3932160
  2106.4 110.0 %collective-permute-start.46 = (bf16[1,512,1024]{2,1,0:T(8,128)(2,1)}, bf16[1,512,1024]{2,1,0:T(8,128)(2,1)}, u32[]{:S(2)}, u32[]{:S(2)}) collective-permute-start(bf16[1,512,1024]{2,1,0:T(8,128)(2,1)} %get-tuple-element.135), channel_id=1, source_target_pairs={{0,6},{2,0},{4,2},{6,4},{1,7},{3,1},{5,3},{7,5},{8,14},{10,8},{12,... | collective-permute-start | bytes 3145736 | tf_op jit(solution)/shard_map/ppermute | solution.py:644
  (142 other events, 6880.3 us)
Sparse Core Ops, SparseCore 0:
  9.7 82.3 all-gather.8
  93.6 155.2 all-gather.6
  250.6 86.8 all-gather.10
  338.9 79.7 all-gather.12
  1367.6 25.9 reduce-scatter.15
  1468.4 72.8 reduce-scatter.17
  1891.4 154.0 reduce-scatter.11
  2073.6 158.4 all-reduce.3
  2234.4 59.2 reduce-scatter.13

commit v2 on v1

--- a/solution.py
+++ b/solution.py
@@ -12,6 +12,7 @@
 SEGS = 4
 F32 = jnp.float32
 BF = jnp.bfloat16
+SMALL_COST = pl.CostEstimate(flops=1000, bytes_accessed=1000, transcendentals=0)
 
 
 neg_big = -1e30
@@ -346,10 +347,399 @@
     )
 
 
+def opening_kernel(w_ref, s_ref, v_ref, whole_ref, tokens_ref, vectors_ref, z_send, z_recv, x_send, x_recv, y_send, y_recv,
+                   fx_send, fx_recv, fy_send, fy_recv, t_send, t_recv, c_send, c_recv, v_send, v_recv, own):
+    rows, place, core = lax.axis_index("rows"), lax.axis_index("seq"), lax.axis_index("fsdp")
+    count = s_ref.shape[0]
+    depth = w_ref.shape[1]
+    half = w_ref.shape[2] // 2
+    width = s_ref.shape[2] // 2
+    steps = count - 1
+
+    def at(row, seq, fsdp=None):
+        return (row, seq, core if fsdp is None else fsdp)
+
+    def hail(device):
+        pl.semaphore_signal(barrier, inc=1, device_id=device, device_id_type=pl.DeviceIdType.MESH)
+
+    barrier = pltpu.get_barrier_semaphore()
+    for away in range(4):
+        for along in range(count):
+            if away or along:
+                hail(at(rows ^ away, lax.rem(place + along, count)))
+    hail(at(rows, place, 1 - core))
+    pl.semaphore_wait(barrier, 4 * count)
+
+    def shard(ref, row, seq, cut=None):
+        first = pl.multiple_of((row * count + seq) * depth, depth)
+        if cut is None:
+            return ref.at[:, pl.ds(first, depth)]
+        return ref.at[:, pl.ds(first, depth), pl.ds(cut * half, half)]
+
+    def remote(src, dst, send, recv, device):
+        return pltpu.make_async_remote_copy(
+            src_ref=src, dst_ref=dst, send_sem=send, recv_sem=recv, device_id=device,
+            device_id_type=pl.DeviceIdType.MESH,
+        )
+
+    x_peer, y_peer = rows ^ 1, rows ^ 2
+
+    def spread(t, side, seq, src):
+        mine = shard(whole_ref, rows, seq)
+        src = mine if src is None else src
+        return (
+            remote(src, mine, x_send.at[t, side], x_recv.at[t, side], at(x_peer, place)),
+            remote(src, mine, y_send.at[t, side], y_recv.at[t, side], at(y_peer, place)),
+        )
+
+    def arrived(t, side, seq):
+        from_x, from_y = shard(whole_ref, x_peer, seq), shard(whole_ref, y_peer, seq)
+        return (
+            remote(from_x, from_x, x_send.at[t, side], x_recv.at[t, side], at(x_peer, place)),
+            remote(from_y, from_y, y_send.at[t, side], y_recv.at[t, side], at(y_peer, place)),
+        )
+
+    def onward(t, side, seq):
+        a, b = shard(whole_ref, x_peer, seq, 0), shard(whole_ref, y_peer, seq, 1)
+        return (
+            remote(a, a, fy_send.at[t, side], fy_recv.at[t, side], at(y_peer, place)),
+            remote(b, b, fx_send.at[t, side], fx_recv.at[t, side], at(x_peer, place)),
+        )
+
+    def far(t, side, seq):
+        a, b = shard(whole_ref, rows ^ 3, seq, 0), shard(whole_ref, rows ^ 3, seq, 1)
+        return (
+            remote(a, a, fy_send.at[t, side], fy_recv.at[t, side], at(y_peer, place)),
+            remote(b, b, fx_send.at[t, side], fx_recv.at[t, side], at(x_peer, place)),
+        )
+
+    def along_z(t, side, seq, src):
+        mine = shard(whole_ref, rows, seq)
+        to = place + 1 if side == 0 else place - 1
+        return remote(mine if src is None else src, mine, z_send.at[t, side], z_recv.at[t, side], at(rows, to))
+
+    def origin(t, side):
+        return place - t if side == 0 else place + t
+
+    def has(t, side):
+        return origin(t, side) >= 0 if side == 0 else origin(t, side) < count
+
+    def has_next(side):
+        return place + 1 < count if side == 0 else place >= 1
+
+    for side in range(2):
+        @pl.when(has_next(side))
+        def _(side=side):
+            along_z(1, side, place, w_ref).start()
+    for copy in spread(0, 0, place, w_ref):
+        copy.start()
+    local = pltpu.make_async_copy(w_ref, shard(whole_ref, rows, place), own.at[0])
+    local.start()
+    vectors = []
+    for away in range(4):
+        for along in range(count):
+            if away or along:
+                mine = rows * count + place
+                copy = remote(
+                    v_ref, vectors_ref.at[mine], v_send.at[away, along], v_recv.at[away, along],
+                    at(rows ^ away, lax.rem(place + along, count)),
+                )
+                copy.start()
+                vectors.append(copy)
+    local_v = pltpu.make_async_copy(v_ref, vectors_ref.at[rows * count + place], own.at[1])
+    local_v.start()
+
+    columns = pl.ds(pl.multiple_of(core * width, width), width)
+
+    def token_copy(along):
+        to = lax.rem(place + along, count)
+        return remote(
+            s_ref.at[to, :, columns], tokens_ref.at[place, :, columns], t_send.at[along], t_recv.at[along], at(rows, to)
+        )
+
+    def token_got(along):
+        start = lax.rem(place + count - along, count)
+        view = tokens_ref.at[start, :, columns]
+        return (
+            remote(view, view, t_send.at[along], t_recv.at[along], at(rows, start)),
+            remote(view, view, c_send.at[along], c_recv.at[along], at(rows, place, 1 - core)),
+        )
+
+    def token_far(along):
+        start = lax.rem(place + count - along, count)
+        view = tokens_ref.at[start, :, pl.ds(pl.multiple_of((1 - core) * width, width), width)]
+        return remote(view, view, c_send.at[along], c_recv.at[along], at(rows, place, 1 - core))
+
+    local_t = pltpu.make_async_copy(s_ref.at[place], tokens_ref.at[place], own.at[2])
+    local_t.start()
+
+    def pass_on(t, side, seq):
+        for got in arrived(t, side, seq):
+            got.wait_recv()
+        for copy in onward(t, side, seq):
+            copy.start()
+
+    for t in range(1, steps + 1):
+        for side in range(2):
+            @pl.when(has(t, side))
+            def _(t=t, side=side):
+                seq = origin(t, side)
+                along_z(t, side, seq, None).wait_recv()
+                if t < steps:
+                    @pl.when(has_next(side))
+                    def _():
+                        along_z(t + 1, side, seq, None).start()
+                for copy in spread(t, side, seq, None):
+                    copy.start()
+        if t == 1:
+            for along in range(1, count):
+                token_copy(along).start()
+            pass_on(0, 0, place)
+        else:
+            for side in range(2):
+                @pl.when(has(t - 1, side))
+                def _(t=t, side=side):
+                    pass_on(t - 1, side, origin(t - 1, side))
+    for side in range(2):
+        @pl.when(has(steps, side))
+        def _(side=side):
+            pass_on(steps, side, origin(steps, side))
+
+    for along in range(1, count):
+        got, on = token_got(along)
+        got.wait_recv()
+        on.start()
+
+    def settle(t, side, seq, src):
+        for copy in spread(t, side, seq, src):
+            copy.wait_send()
+        for copy in onward(t, side, seq):
+            copy.wait_send()
+        for got in far(t, side, seq):
+            got.wait_recv()
+
+    settle(0, 0, place, w_ref)
+    for t in range(1, steps + 1):
+        for side in range(2):
+            @pl.when(has(t, side))
+            def _(t=t, side=side):
+                settle(t, side, origin(t, side), None)
+
+            @pl.when(has(t - 1, side) & has_next(side))
+            def _(t=t, side=side):
+                along_z(t, side, origin(t - 1, side), w_ref if t == 1 else None).wait_send()
+    for copy in vectors:
+        copy.wait_send()
+    for away in range(4):
+        for along in range(count):
+            if away or along:
+                start = (rows ^ away) * count + lax.rem(place + count - along, count)
+                view = vectors_ref.at[start]
+                remote(
+                    view, view, v_send.at[away, along], v_recv.at[away, along],
+                    at(rows ^ away, lax.rem(place + count - along, count)),
+                ).wait_recv()
+    for along in range(1, count):
+        token_copy(along).wait_send()
+        token_got(along)[1].wait_send()
+        token_far(along).wait_recv()
+    local.wait()
+    local_v.wait()
+    local_t.wait()
+
+
+def opening(w, tokens, vector):
+    count = tokens.shape[0]
+    kinds, depth, half = w.shape
+    dma = pltpu.SemaphoreType.DMA
+    pair = [dma((count, 2)), dma((count, 2))]
+    anywhere = pl.BlockSpec(memory_space=pl.ANY)
+    return pl.pallas_call(
+        opening_kernel,
+        in_specs=[anywhere] * 3,
+        out_specs=[anywhere] * 3,
+        out_shape=[
+            jax.ShapeDtypeStruct((kinds, depth * 4 * count, half), w.dtype),
+            jax.ShapeDtypeStruct(tokens.shape, tokens.dtype),
+            jax.ShapeDtypeStruct((4 * count,) + vector.shape, vector.dtype),
+        ],
+        scratch_shapes=pair * 5 + [dma((count,))] * 4 + [dma((4, count))] * 2 + [dma((3,))],
+        compiler_params=pltpu.CompilerParams(collective_id=0, has_side_effects=True),
+    )(w, tokens, vector)
+
+
+def closing_kernel(s_ref, v_ref, tokens_ref, sum_ref, held, t_send, t_recv, c_send, c_recv, v_send, v_recv, own):
+    rows, place, core = lax.axis_index("rows"), lax.axis_index("seq"), lax.axis_index("fsdp")
+    count = s_ref.shape[0]
+    width = s_ref.shape[2] // 2
+
+    def at(row, seq, fsdp=None):
+        return (row, seq, core if fsdp is None else fsdp)
+
+    def hail(device):
+        pl.semaphore_signal(barrier, inc=1, device_id=device, device_id_type=pl.DeviceIdType.MESH)
+
+    barrier = pltpu.get_barrier_semaphore()
+    for away in range(4):
+        for along in range(count):
+            if away or along:
+                hail(at(rows ^ away, lax.rem(place + along, count)))
+    hail(at(rows, place, 1 - core))
+    pl.semaphore_wait(barrier, 4 * count)
+
+    def remote(src, dst, send, recv, device):
+        return pltpu.make_async_remote_copy(
+            src_ref=src, dst_ref=dst, send_sem=send, recv_sem=recv, device_id=device,
+            device_id_type=pl.DeviceIdType.MESH,
+        )
+
+    columns = pl.ds(pl.multiple_of(core * width, width), width)
+    others = pl.ds(pl.multiple_of((1 - core) * width, width), width)
+
+    def token_copy(along):
+        to = lax.rem(place + along, count)
+        return remote(
+            s_ref.at[to, :, columns], tokens_ref.at[place, :, columns], t_send.at[along], t_recv.at[along], at(rows, to)
+        )
+
+    def token_got(along):
+        start = lax.rem(place + count - along, count)
+        view = tokens_ref.at[start, :, columns]
+        return (
+            remote(view, view, t_send.at[along], t_recv.at[along], at(rows, start)),
+            remote(view, view, c_send.at[along], c_recv.at[along], at(rows, place, 1 - core)),
+        )
+
+    def token_far(along):
+        view = tokens_ref.at[lax.rem(place + count - along, count), :, others]
+        return remote(view, view, c_send.at[along], c_recv.at[along], at(rows, place, 1 - core))
+
+    for along in range(1, count):
+        token_copy(along).start()
+    local_t = pltpu.make_async_copy(s_ref.at[place], tokens_ref.at[place], own.at[0])
+    local_t.start()
+    mine = rows * count + place
+    vectors = []
+    for away in range(4):
+        for along in range(count):
+            if away or along:
+                to_row, to_seq = rows ^ away, lax.rem(place + along, count)
+                copy = remote(
+                    v_ref.at[to_row * count + to_seq], held.at[away * count + along],
+                    v_send.at[away, along], v_recv.at[away, along], at(to_row, to_seq),
+                )
+                copy.start()
+                vectors.append(copy)
+    local_v = pltpu.make_async_copy(v_ref.at[mine], held.at[0], own.at[1])
+    local_v.start()
+    local_v.wait()
+    for copy in vectors:
+        copy.wait_recv()
+    sum_ref[...] = jnp.sum(held[...], axis=0)
+    for along in range(1, count):
+        got, on = token_got(along)
+        got.wait_recv()
+        on.start()
+    for copy in vectors:
+        copy.wait_send()
+    for along in range(1, count):
+        token_copy(along).wait_send()
+        token_got(along)[1].wait_send()
+        token_far(along).wait_recv()
+    local_t.wait()
+
+
+def closing(tokens, vectors):
+    count = tokens.shape[0]
+    dma = pltpu.SemaphoreType.DMA
+    anywhere = pl.BlockSpec(memory_space=pl.ANY)
+    return pl.pallas_call(
+        closing_kernel,
+        in_specs=[anywhere] * 2,
+        out_specs=[anywhere, pl.BlockSpec(memory_space=pltpu.VMEM)],
+        out_shape=[
+            jax.ShapeDtypeStruct(tokens.shape, tokens.dtype),
+            jax.ShapeDtypeStruct(vectors.shape[1:], F32),
+        ],
+        scratch_shapes=[pltpu.VMEM(vectors.shape, F32)]
+        + [dma((count,))] * 4
+        + [dma((4, count))] * 2
+        + [dma((2,))],
+        compiler_params=pltpu.CompilerParams(collective_id=1, has_side_effects=True),
+    )(tokens, vectors)
+
+
+def product_kernel(mode, finish, n_extra, n_out, *refs):
+    a_ref, b_ref = refs[:2]
+    extra = refs[2 : 2 + n_extra]
+    outs = refs[-1 - n_out : -1]
+    total = refs[-1]
+    k = pl.program_id(2)
+    last = pl.num_programs(2) - 1
+    dims = {"nn": ((1,), (0,)), "nt": ((1,), (1,)), "tn": ((0,), (0,))}[mode]
+    part = lax.dot_general(a_ref[...], b_ref[...], (dims, ((), ())), preferred_element_type=F32)
+    if last == 0:
+        finish(part, extra, outs)
+        return
+
+    @pl.when(k == 0)
+    def _():
+        total[...] = part
+
+    @pl.when((k > 0) & (k < last))
+    def _():
+        total[...] += part
+
+    @pl.when(k == last)
+    def _():
+        finish(total[...] + part, extra, outs)
+
+
+def finish_cast(total, extra, outs):
+    outs[0][...] = total.astype(outs[0].dtype)
+
+
+def finish_bias(scale, total, extra, outs):
+    outs[0][...] = ((total + extra[0][...]) * scale).astype(BF)
+
+
+def product(a, b, mode, finish=finish_cast, rows=(), deps=(), blocks=(1024, 1024, 2048)):
+    plane = len(b.shape) == 3
+    b_shape = b.shape[-2:]
+    m, depth = a.shape if mode != "tn" else a.shape[::-1]
+    n = b_shape[0] if mode == "nt" else b_shape[1]
+    bm, bn, bk = min(blocks[0], m), min(blocks[1], n), min(blocks[2], depth)
+    spec = pl.BlockSpec
+    a_spec = (
+        spec((bk, bm), lambda j, i, k: (k, i)) if mode == "tn" else spec((bm, bk), lambda j, i, k: (i, k))
+    )
+    if plane:
+        b_spec = spec((None, bn, bk), lambda j, i, k: (k % b.shape[0], j, k // b.shape[0]))
+    elif mode == "nt":
+        b_spec = spec((bn, bk), lambda j, i, k: (j, k))
+    else:
+        b_spec = spec((bk, bn), lambda j, i, k: (k, j))
+    row = spec((1, bn), lambda j, i, k: (0, j))
+    field = spec((bm, bn), lambda j, i, k: (i, j))
+    return pl.pallas_call(
+        functools.partial(product_kernel, mode, finish, len(rows), 1),
+        grid=(n // bn, m // bm, depth // bk),
+        in_specs=[a_spec, b_spec]
+        + [row] * len(rows)
+        + [spec(memory_space=pl.ANY)] * len(deps),
+        out_specs=field,
+        out_shape=jax.ShapeDtypeStruct((m, n), BF),
+        scratch_shapes=[pltpu.VMEM((bm, bn), F32)],
+        cost_estimate=SMALL_COST,
+        compiler_params=pltpu.CompilerParams(vmem_limit_bytes=48 * 2**20),
+    )(a, b, *rows, *deps)
+
+
 def dot_nt(a,b): return lax.dot_general(a,b,(((1,),(1,)),((),())),preferred_element_type=F32)
 def dot_nn(a,b): return lax.dot_general(a,b,(((1,),(0,)),((),())),preferred_element_type=F32)
 
-def fwd_kernel(tile, flags, q_ref, k_ref, v_ref, sk_ref, sv_ref, start_ref, doc_ref, sdoc_ref, o_ref, lse_ref, km, vt, acc, top, total):
+def fwd_kernel(tile, flags, q_ref, k_ref, v_ref, sk_ref, sv_ref, start_ref, doc_ref, sdoc_ref, *rest):
+    o_ref, lse_ref, km, vt, acc, top, total = rest[-7:]
     i = pl.program_id(1)
     seg = k_ref.shape[0]
     lanes = lax.broadcasted_iota(jnp.int32, (1, 128), 1)
@@ -408,34 +798,51 @@
     for h in range(2):
         lse_ref[0, pl.ds(h, 1)] = top[h] + jnp.log(total[h])
 
-def attn_fwd(q, k, v, sk, sv, start, doc, sdoc, flags, tile=512, offs=(0,0,0)):
-    seg, = (q.shape[0],)
-    pairs = sk.shape[1] // 128
+def attn_fwd(q, k, v, sk, sv, start, doc, sdoc, flags, tile, base, pairs, earlier_out=(), deps=()):
+    seg, width = q.shape
     count = seg // tile
-    row = lambda shape, f: pl.BlockSpec(shape, f)
+    spec = pl.BlockSpec
+    extra = tuple(earlier_out) + tuple(deps)
     return pl.pallas_call(
         functools.partial(fwd_kernel, tile),
         grid_spec=pltpu.PrefetchScalarGridSpec(
-            num_scalar_prefetch=1, grid=(pairs, count),
+            num_scalar_prefetch=1,
+            grid=(pairs, count),
             in_specs=[
-                row((tile,128), lambda h,i,f: (i,h+offs[0])),
-                row((seg,128), lambda h,i,f: (0,h+offs[1])),
-                row((seg,128), lambda h,i,f: (0,h+offs[2])),
-                row((128,128), lambda h,i,f: (0,h)),
-                row((128,128), lambda h,i,f: (0,h)),
-                row((1,tile), lambda h,i,f: (0,i)),
-                row((1,tile), lambda h,i,f: (0,i)),
-                row((128,1), lambda h,i,f: (0,0)),
+                spec((tile, 128), lambda h, i, f: (i, h + base)),
+                spec((seg, 128), lambda h, i, f: (0, h + base)),
+                spec((seg, 128), lambda h, i, f: (0, h + base)),
+                spec((128, 128), lambda h, i, f: (0, h + base)),
+                spec((128, 128), lambda h, i, f: (0, h + base)),
+                spec((1, tile), lambda h, i, f: (0, i)),
+                spec((1, tile), lambda h, i, f: (0, i)),
+                spec((128, 1), lambda h, i, f: (0, 0)),
+            ]
+            + [spec(memory_space=pl.ANY)] * len(extra),
+            out_specs=[
+                spec((tile, 128), lambda h, i, f: (i, h + base)),
+                spec((1, 2, tile), lambda h, i, f: (h + base, 0, i)),
             ],
-            out_specs=[row((tile,128), lambda h,i,f: (i,h)), row((1,2,tile), lambda h,i,f: (h,0,i))],
-            scratch_shapes=[pltpu.VMEM((2,seg+128,128),BF), pltpu.VMEM((128,seg+128),BF), pltpu.VMEM((2,HEAD,tile),F32), pltpu.VMEM((2,1,tile),F32), pltpu.VMEM((2,1,tile),F32)],
+            scratch_shapes=[
+                pltpu.VMEM((2, seg + 128, 128), BF),
+                pltpu.VMEM((128, seg + 128), BF),
+                pltpu.VMEM((2, HEAD, tile), F32),
+                pltpu.VMEM((2, 1, tile), F32),
+                pltpu.VMEM((2, 1, tile), F32),
+            ],
         ),
-        out_shape=[jax.ShapeDtypeStruct((seg,pairs*128),BF), jax.ShapeDtypeStruct((pairs,2,seg),F32)],
-        compiler_params=pltpu.CompilerParams(vmem_limit_bytes=48*2**20),
-    )(flags, q, k, v, sk, sv, start, doc, sdoc)
-
-def bwd_kernel(tile, flags, q_ref, k_ref, v_ref, do_ref, o_ref, sk_ref, sv_ref, lse_ref, start_ref, doc_ref, sdoc_ref,
-               dq_ref, dk_ref, dv_ref, dsk_ref, dsv_ref, qm, dom, dqt, delta):
+        out_shape=[
+            jax.ShapeDtypeStruct((seg, width), BF),
+            jax.ShapeDtypeStruct((width // 128, 2, seg), F32),
+        ],
+        input_output_aliases={9: 0, 10: 1} if earlier_out else {},
+        cost_estimate=SMALL_COST,
+        compiler_params=pltpu.CompilerParams(vmem_limit_bytes=40 * 2**20),
+    )(flags, q, k, v, sk, sv, start, doc, sdoc, *extra)
+
+
+def bwd_kernel(tile, flags, q_ref, k_ref, v_ref, do_ref, o_ref, sk_ref, sv_ref, lse_ref, start_ref, doc_ref, sdoc_ref, *rest):
+    dq_ref, dk_ref, dv_ref, dsk_ref, dsv_ref, qm, dom, dqt, delta = rest[-9:]
     j = pl.program_id(1)
     seg = q_ref.shape[0]
     count = seg // tile
@@ -513,38 +920,50 @@
             return 0
         lax.fori_loop(0, count, fin, 0)
 
-def attn_bwd(q, k, v, do, o, sk, sv, lse, start, doc, sdoc, flags, tile=512, offs=(0,0,0)):
+def attn_bwd(q, k, v, do, o, sk, sv, lse, start, doc, sdoc, flags, tile, base, pairs, deps=()):
     seg = q.shape[0]
-    pairs = sk.shape[1] // 128
     count = seg // tile
-    row = lambda shape, f: pl.BlockSpec(shape, f)
     last = count - 1
+    spec = pl.BlockSpec
     return pl.pallas_call(
         functools.partial(bwd_kernel, tile),
         grid_spec=pltpu.PrefetchScalarGridSpec(
-            num_scalar_prefetch=1, grid=(pairs, count + 1),
+            num_scalar_prefetch=1,
+            grid=(pairs, count + 1),
             in_specs=[
-                row((seg,128), lambda h,j,f: (0,h+offs[0])),
-                row((tile,128), lambda h,j,f: (jnp.minimum(j,last),h+offs[1])),
-                row((tile,128), lambda h,j,f: (jnp.minimum(j,last),h+offs[2])),
-                row((seg,128), lambda h,j,f: (0,h)),
-                row((seg,128), lambda h,j,f: (0,h)),
-                row((128,128), lambda h,j,f: (0,h)),
-                row((128,128), lambda h,j,f: (0,h)),
-                row((1,2,seg), lambda h,j,f: (h,0,0)),
-                row((1,seg), lambda h,j,f: (0,0)),
-                row((1,seg), lambda h,j,f: (0,0)),
-                row((128,1), lambda h,j,f: (0,0)),
+                spec((seg, 128), lambda h, j, f: (0, h + base)),
+                spec((tile, 128), lambda h, j, f: (jnp.minimum(j, last), h + base)),
+                spec((tile, 128), lambda h, j, f: (jnp.minimum(j, last), h + base)),
+                spec((seg, 128), lambda h, j, f: (0, h + base)),
+                spec((seg, 128), lambda h, j, f: (0, h + base)),
+                spec((128, 128), lambda h, j, f: (0, h + base)),
+                spec((128, 128), lambda h, j, f: (0, h + base)),
+                spec((1, 2, seg), lambda h, j, f: (h + base, 0, 0)),
+                spec((1, seg), lambda h, j, f: (0, 0)),
+                spec((1, seg), lambda h, j, f: (0, 0)),
+                spec((128, 1), lambda h, j, f: (0, 0)),
+            ]
+            + [spec(memory_space=pl.ANY)] * len(deps),
+            out_specs=[
+                spec((seg, 128), lambda h, j, f: (0, h)),
+                spec((tile, 128), lambda h, j, f: (jnp.minimum(j, last), h)),
+                spec((tile, 128), lambda h, j, f: (jnp.minimum(j, last), h)),
+                spec((128, 128), lambda h, j, f: (0, h)),
+                spec((128, 128), lambda h, j, f: (0, h)),
             ],
-            out_specs=[row((seg,128), lambda h,j,f: (0,h)),
-                       row((tile,128), lambda h,j,f: (jnp.minimum(j,last),h)),
-                       row((tile,128), lambda h,j,f: (jnp.minimum(j,last),h)),
-                       row((128,128), lambda h,j,f: (0,h)), row((128,128), lambda h,j,f: (0,h))],
-            scratch_shapes=[pltpu.VMEM((2,seg,128),BF), pltpu.VMEM((2,seg,128),BF), pltpu.VMEM((128,seg),F32), pltpu.VMEM((2,1,seg),F32)],
+            scratch_shapes=[
+                pltpu.VMEM((2, seg, 128), BF),
+                pltpu.VMEM((2, seg, 128), BF),
+                pltpu.VMEM((128, seg), F32),
+                pltpu.VMEM((2, 1, seg), F32),
+            ],
         ),
-        out_shape=[jax.ShapeDtypeStruct((seg,pairs*128),BF)]*3 + [jax.ShapeDtypeStruct((128,pairs*128),BF)]*2,
-        compiler_params=pltpu.CompilerParams(vmem_limit_bytes=48*2**20),
-    )(flags, q, k, v, do, o, sk, sv, lse, start, doc, sdoc)
+        out_shape=[jax.ShapeDtypeStruct((seg, pairs * 128), BF)] * 3
+        + [jax.ShapeDtypeStruct((128, pairs * 128), BF)] * 2,
+        cost_estimate=SMALL_COST,
+        compiler_params=pltpu.CompilerParams(vmem_limit_bytes=40 * 2**20),
+    )(flags, q, k, v, do, o, sk, sv, lse, start, doc, sdoc, *deps)
+
 
 def make_meta(doc, tile):
     seg=doc.shape[0]; count=seg//tile
@@ -559,75 +978,23 @@
     return start.reshape(1,seg), flags
 
 
-X_FLIP = ((0, 1), (1, 0), (2, 3), (3, 2))
-Y_FLIP = ((0, 2), (2, 0), (1, 3), (3, 1))
+def gate(value, *deps):
+    anywhere = pl.BlockSpec(memory_space=pl.ANY)
+    return pl.pallas_call(
+        lambda *refs: None,
+        in_specs=[anywhere] * (1 + len(deps)),
+        out_specs=anywhere,
+        out_shape=jax.ShapeDtypeStruct(value.shape, value.dtype),
+        input_output_aliases={0: 0},
+        cost_estimate=SMALL_COST,
+    )(value, *deps)
+
+
 BOTH = ("rows", "seq")
-
-
-def over_x(block):
-    return lax.ppermute(block, "rows", X_FLIP)
-
-
-def over_y(block):
-    return lax.ppermute(block, "rows", Y_FLIP)
 
 
 def other_core(block):
     return lax.ppermute(block, "fsdp", ((0, 1), (1, 0)))
-
-
-def cut(field, axis, parts):
-    size = field.shape[axis] // parts
-    return [lax.slice_in_dim(field, n * size, (n + 1) * size, axis=axis) for n in range(parts)]
-
-
-def gather(shard, axis, split):
-    me = lax.axis_index("rows")
-    block = lax.all_gather(shard, "seq", axis=axis, tiled=True)
-    first, second = cut(block, split, 2)
-    width = block.shape[axis]
-    from_x, from_y = over_x(first), over_y(second)
-    pieces = (
-        (0, first, second),
-        (1, from_x, over_x(second)),
-        (2, over_y(first), from_y),
-        (3, over_y(from_x), over_x(from_y)),
-    )
-    shape = list(block.shape)
-    shape[axis] = width * 4
-    whole = jnp.zeros(shape, block.dtype)
-    half = block.shape[split] // 2
-    for away, a, b in pieces:
-        for n, part in enumerate((a, b)):
-            at = [0] * len(shape)
-            at[axis] = (me ^ away) * width
-            at[split] = n * half
-            whole = lax.dynamic_update_slice(whole, part, at)
-    return whole
-
-
-def scatter(partial, axis, split):
-    me = lax.axis_index("rows")
-    width = partial.shape[axis] // 4
-
-    def block(field, away):
-        return lax.dynamic_slice_in_dim(field, (me ^ away) * width, width, axis)
-
-    first, second = cut(partial, split, 2)
-
-    def plus(own, moved):
-        return (own.astype(F32) + moved.astype(F32)).astype(BF)
-
-    far_a = over_x(block(first, 3))
-    far_b = over_y(block(second, 3))
-    near_a = over_x(block(first, 1))
-    near_b = over_y(block(second, 2))
-    last_a = over_y(plus(block(first, 2), far_a))
-    last_b = over_x(plus(block(second, 1), far_b))
-    sum_a = block(first, 0).astype(F32) + near_a.astype(F32) + last_a.astype(F32)
-    sum_b = block(second, 0).astype(F32) + near_b.astype(F32) + last_b.astype(F32)
-    mine = jnp.concatenate((sum_a.astype(BF), sum_b.astype(BF)), axis=split)
-    return lax.psum_scatter(mine, "seq", scatter_dimension=axis, tiled=True).astype(F32)
 
 
 def exchange(field):
@@ -715,7 +1082,12 @@
 
     small = (bias_qv, bias_out, bias_up, bias_down, gain_one, shift_one, gain_two, shift_two)
     sizes = [item.size for item in small]
-    packed = lax.all_gather(jnp.concatenate([item.reshape(-1) for item in small]), BOTH, axis=0)
+    vector = jnp.concatenate([item.reshape(-1) for item in small])
+    room = -(-vector.shape[0] // 2048) * 2048
+    vector = jnp.pad(vector, (0, room - vector.shape[0])).reshape(-1, 128)
+    qkv_full, tokens, packed = opening(w_qkv, states[0], vector)
+    tokens = tokens.reshape(seg_len, model)
+    packed = packed.reshape(packed.shape[0], -1)
     cuts = []
     at = 0
     for size in sizes:
@@ -731,13 +1103,6 @@
     bias_u = spread_last(cuts[2], (hidden_units // HEAD,))
     bias_d = cuts[3].reshape(-1)
     gain_a, shift_a, gain_b, shift_b = [item.reshape(-1) for item in cuts[4:]]
-
-    qkv_full = gather(w_qkv, 1, 2)
-    tokens = exchange(states[0]).reshape(seg_len, model)
-    out_full = gather(w_out, 1, 0)
-    up_full = gather(w_up, 0, 1)
-    down_full = gather(w_down, 1, 0)
-    grad_out = exchange(cotangent[0]).reshape(seg_len, model)
 
     docs = doc_ids[0]
     my_docs = lax.dynamic_index_in_dim(docs, place, 0, keepdims=False)
@@ -756,16 +1121,32 @@
 
     tokens_f = tokens.astype(F32)
     normed_one, mean_one, scale_one = norm_forward(tokens_f, gain_a, shift_a)
-    query = ((mm(normed_one, qkv_full[0]) + bias_pair[0]) * HEAD**-0.5).astype(BF)
-    keys = mm(normed_one, qkv_full[1]).astype(BF)
-    values = (mm(normed_one, qkv_full[2]) + bias_pair[1]).astype(BF)
+    query = product(
+        normed_one, qkv_full[0], "nn", functools.partial(finish_bias, HEAD**-0.5), (bias_pair[:1],)
+    )
+    keys = product(normed_one, qkv_full[1], "nn")
+    values = product(
+        normed_one, qkv_full[2], "nn", functools.partial(finish_bias, 1.0), (bias_pair[1:],)
+    )
+    out_full = lax.all_gather(gate(w_out.T, normed_one), BOTH, axis=0, tiled=True)
+    up_full = lax.all_gather(gate(w_up, values), BOTH, axis=0, tiled=True)
+    grad_out = exchange(gate(cotangent[0], query)).reshape(seg_len, model)
     tail = jnp.stack((keys[seg_len - SUMM :], values[seg_len - SUMM :]))
     lent = jnp.concatenate((shift_by(tail, 1), shift_by(tail, 2)), axis=1)
     lent = jnp.pad(lent, ((0, 0), (0, 128 - 2 * SUMM), (0, 0)))
-    mixed, log_sum = attn_fwd(
-        query, keys, values, lent[0], lent[1], start, doc_row, sum_docs, flags, tile
-    )
-    hidden = tokens_f + both_halves(mm(mixed, out_full)) + bias_o
+    pairs = half // 128
+    each = pairs // 4
+    attended = ()
+    for n in range(4):
+        attended = attn_fwd(
+            query, keys, values, lent[0], lent[1], start, doc_row, sum_docs, flags, tile,
+            n * each, each, attended, (grad_out,) if n == 3 else (),
+        )
+        if n == 0:
+            down_full = lax.all_gather(gate(w_down.T, attended[0]), BOTH, axis=0, tiled=True)
+    mixed, log_sum = attended
+    attended = product(mixed, out_full, "nt")
+    hidden = tokens_f + both_halves(attended) + bias_o
     normed_two, mean_two, scale_two = norm_forward(hidden, gain_b, shift_b)
     up_proj = mm(normed_two, up_full) + bias_u
     bell = jnp.exp(-0.5 * up_proj * up_proj)
@@ -773,51 +1154,86 @@
     activated = (up_proj * area).astype(BF)
     slope = (area + up_proj * bell * 0.3989422804014327).astype(BF)
 
-    grad_w_down = scatter(mm_tn(activated, grad_out).astype(BF), 1, 0)
-    d_up = (mm_nt(grad_out, down_full) * slope.astype(F32)).astype(BF)
-    grad_w_up = scatter(mm_tn(normed_two, d_up).astype(BF), 0, 1)
-    d_norm_two = both_halves(mm_nt(d_up, up_full))
+    def over_rows(partial):
+        return lax.psum_scatter(partial, "rows", scatter_dimension=0, tiled=True)
+
+    def over_seq(partial):
+        return lax.psum_scatter(partial, "seq", scatter_dimension=0, tiled=True).astype(F32)
+
+    down_sum = product(grad_out, activated, "tn")
+    down_rows = over_rows(down_sum)
+    slope = gate(slope, down_sum)
+    d_up = (mm(grad_out, down_full) * slope.astype(F32)).astype(BF)
+    up_sum = product(normed_two, d_up, "tn")
+    d_norm_part = product(d_up, up_full, "nt", deps=(up_sum,))
+    up_turn = gate(up_sum, down_rows, d_norm_part)
+    up_rows = over_rows(up_turn)
+    d_norm_two = both_halves(d_norm_part)
     d_hidden_ln, grad_gain_two, grad_shift_two = norm_backward(
         hidden, mean_two, scale_two, gain_b, d_norm_two
     )
     d_hidden = grad_out.astype(F32) + d_hidden_ln
     d_hidden_low = d_hidden.astype(BF)
-    d_mixed = mm_nt(d_hidden_low, out_full).astype(BF)
-    grad_w_out = scatter(mm_tn(mixed, d_hidden_low).astype(BF), 1, 0)
-
-    out_tokens = (hidden + both_halves(mm(activated, down_full)) + bias_d).astype(BF)
+    d_mixed = product(d_hidden_low, out_full, "nn", deps=(up_turn,))
+    out_sum = product(d_hidden_low, mixed, "tn", deps=(d_mixed,))
+
+    def back(n, deps):
+        return attn_bwd(
+            query, keys, values, d_mixed, mixed, lent[0], lent[1], log_sum, start, doc_row,
+            sum_docs, flags, tile, n * each, each, deps,
+        )
+
+    def own_half(pieces):
+        d_pre, d_keys, d_values, d_lent_k, d_lent_v = [
+            jnp.concatenate(pair, axis=1) for pair in zip(*pieces)
+        ]
+        d_lent = jnp.stack((d_lent_k, d_lent_v))
+        back_home = shift_by(d_lent[:, :SUMM], -1).astype(F32) + shift_by(
+            d_lent[:, SUMM : 2 * SUMM], -2
+        ).astype(F32)
+        ends = jnp.stack((d_keys[seg_len - SUMM :], d_values[seg_len - SUMM :])).astype(F32)
+        ends = (ends + back_home).astype(BF)
+        d_keys = lax.dynamic_update_slice(d_keys, ends[0], (seg_len - SUMM, 0))
+        d_values = lax.dynamic_update_slice(d_values, ends[1], (seg_len - SUMM, 0))
+        grads = jnp.concatenate((d_pre, d_keys, d_values), axis=1)
+        return grads, product(normed_one, grads, "tn", blocks=(1024, grads.shape[1] // 2, 2048))
+
+    piece_0 = back(0, (out_sum,))
+    down_turn = gate(down_rows, up_rows, piece_0[0])
+    out_rows = over_rows(gate(out_sum, up_rows, down_turn))
+    grad_w_down = over_seq(down_turn)
+    piece_1 = back(1, (down_turn,))
+    first_half, first_sum = own_half((piece_0, piece_1))
+    piece_2 = back(2, (first_sum,))
+    first_turn = gate(first_sum, out_rows, piece_2[0])
+    first_rows = over_rows(first_turn)
+    grad_w_up = over_seq(gate(up_rows, first_turn))
+    out_partial = product(activated, down_full, "nt", deps=(first_turn,))
+    out_tokens = (hidden + both_halves(out_partial) + bias_d).astype(BF)
     out_states = exchange(out_tokens.reshape(segs, width, model))[None]
-
-    d_pre, d_keys, d_values, d_lent_k, d_lent_v = attn_bwd(
-        query, keys, values, d_mixed, mixed, lent[0], lent[1], log_sum, start, doc_row, sum_docs, flags, tile
-    )
-    d_lent = jnp.stack((d_lent_k, d_lent_v))
-    back = shift_by(d_lent[:, :SUMM], -1).astype(F32) + shift_by(
-        d_lent[:, SUMM : 2 * SUMM], -2
-    ).astype(F32)
-    ends = jnp.stack((d_keys[seg_len - SUMM :], d_values[seg_len - SUMM :])).astype(F32) + back
-    ends = ends.astype(BF)
-    d_keys = lax.dynamic_update_slice(d_keys, ends[0], (seg_len - SUMM, 0))
-    d_values = lax.dynamic_update_slice(d_values, ends[1], (seg_len - SUMM, 0))
-    d_qkv = (d_pre, d_keys, d_values)
-    grad_w_qkv = scatter(
-        jnp.stack([mm_tn(normed_one, item).astype(BF) for item in d_qkv]), 1, 2
-    )
-    d_norm_one = both_halves(
-        mm_nt(d_pre, qkv_full[0]) + mm_nt(d_keys, qkv_full[1]) + mm_nt(d_values, qkv_full[2])
-    )
+    piece_3 = back(3, (out_partial,))
+    second_half, second_sum = own_half((piece_2, piece_3))
+    second_turn = gate(second_sum, first_rows)
+    second_rows = over_rows(second_turn)
+    d_qkv = jnp.concatenate((first_half, second_half), axis=1)
+    d_norm_one = both_halves(product(d_qkv, qkv_full, "nt", deps=(second_turn,), blocks=(1024, 1024, half // 2)))
+    grad_w_out = over_seq(gate(out_rows, second_turn))
+    qkv_rows = jnp.concatenate((first_rows, second_rows), axis=1)
+    grad_w_qkv = over_seq(qkv_rows)
+    grad_w_qkv = jnp.transpose(grad_w_qkv.reshape(-1, 2, 3, half // 2), (2, 0, 1, 3)).reshape(3, -1, half)
+    grad_w_out = grad_w_out.T
+    grad_w_down = grad_w_down.T
     d_tokens_ln, grad_gain_one, grad_shift_one = norm_backward(
         tokens_f, mean_one, scale_one, gain_a, d_norm_one
     )
     grad_tokens = (d_hidden + d_tokens_ln).astype(BF)
-    grad_states = exchange(grad_tokens.reshape(segs, width, model))[None]
-
     def column_sum(field):
         return jnp.sum(field.astype(F32), axis=0)
 
+    kind_sum = column_sum(d_qkv).reshape(2, 3, half // 2)
     sums = (
         jnp.moveaxis(
-            jnp.stack((column_sum(d_pre), column_sum(d_values))).reshape(2, half // HEAD, shards, -1), 2, 0
+            jnp.stack((kind_sum[:, 0], kind_sum[:, 2])).reshape(2, half // HEAD, shards, -1), 2, 0
         ),
         column_sum(d_hidden),
         jnp.moveaxis(column_sum(d_up).reshape(hidden_units // HEAD, shards, -1), 1, 0),
@@ -827,8 +1243,11 @@
         grad_gain_two,
         grad_shift_two,
     )
-    vector = jnp.concatenate([item.reshape(shards, -1) for item in sums], axis=1)
-    vector = lax.psum_scatter(vector, BOTH, scatter_dimension=0, tiled=False)
+    vectors = jnp.concatenate([item.reshape(shards, -1) for item in sums], axis=1)
+    vectors = jnp.pad(vectors, ((0, 0), (0, room - vectors.shape[1]))).reshape(shards, -1, 128)
+    grad_states, vector = closing(grad_tokens.reshape(segs, width, model), gate(vectors, qkv_rows))
+    grad_states = grad_states[None]
+    vector = vector.reshape(-1)
     small_grads = []
     at = 0
     for item, size in zip(small, sizes):

time: 2310 us -> 1780 us (0.77)
  Pallas kernels: 286 us -> 930 us
  waiting for transfers between devices: 771 us -> 381 us
  matrix products: 444 us -> 101 us
  blocking collectives: 212 us -> 0 us
  starting transfers between devices: 138 us -> 17.4 us
  local copies, waits for them, and re-layouts: 231 us -> 149 us
  other arithmetic: 208 us -> 181 us
    pallas_call x0 -> x28, Pallas kernels: none -> 624 us  [the longest x13 332 us: product(): pl.pallas_call(functools.partial(product_kernel, mode, finish, len(rows),...]
    ppermute x48 -> x0, waiting for transfers between devices: 560 us -> none  [the longest x24 299 us: over_x(): return lax.ppermute(block, 'rows', X_FLIP)]
    dot_general x12 -> x0, matrix products: 295 us -> none  [the longest x6 166 us: dot_nt(): lax.dot_general(a, b, (((1,), (1,)), ((), ())), preferred_element_type=F32)]
    all_gather x1 -> x0, blocking collectives: 212 us -> none  [layer_by_segment(): lax.all_gather(jnp.concatenate([item.reshape(-1) for item in small]), BOT...]
    reduce_scatter x1 -> x9, waiting for transfers between devices: 0.01 us -> 106 us  [the longest x5 80 us: over_rows(): return lax.psum_scatter(partial, 'rows', scatter_dimension=0, tiled=True)]
    ppermute x48 -> x0, starting transfers between devices: 78 us -> none  [the longest x24 60.7 us: over_x(): return lax.ppermute(block, 'rows', X_FLIP)]
    unnamed x202 -> x219, local copies, waits for them, and re-layouts: 36.5 us -> 100 us
    dynamic_update_slice x32 -> x4, local copies, waits for them, and re-layouts: 57.4 us -> 6.55 us  [the longest x2 3.39 us: own_half(): d_values = lax.dynamic_update_slice(d_values, ends[1], (seg_len - SUMM, 0))]
  transfers between devices with their start and end apart: 81 -> 30, of which waited for: 32 -> 15; matrix products, arithmetic and copies ran while one was open for 29% -> 19% of each run, Pallas kernels for 12% -> 43%
where the time goes in v2:
time: 1780 us
  Pallas kernels  930 us (52%)
  waiting for transfers between devices  381 us (21%)
  other arithmetic  181 us (10%)
  local copies, waits for them, and re-layouts  149 us (8%)
  matrix products  101 us (6%)
    pallas_call x13, Pallas kernels, product(): pl.pallas_call(functools.partial(product_kernel, mode, finish, len(rows),...  332 us
    pallas_call x4, Pallas kernels, attn_bwd(): pl.pallas_call(functools.partial(bwd_kernel, tile), grid_spec=pltpu.Prefe...  173 us
    ppermute x6, waiting for transfers between devices, exchange(): lax.ppermute(block, 'seq', [(n, (n + away) % count) for n in range(count)])  165 us
    pallas_call x1, Pallas kernels, opening(): pl.pallas_call(opening_kernel, in_specs=[anywhere] * 3, out_specs=[anywhe...  165 us
    pallas_call x4, Pallas kernels, attn_fwd(): pl.pallas_call(functools.partial(fwd_kernel, tile), grid_spec=pltpu.Prefe...  133 us
    pallas_call x1, Pallas kernels, closing(): pl.pallas_call(closing_kernel, in_specs=[anywhere] * 2, out_specs=[anywhe...  127 us
    dot_general x2, matrix products, dot_nn(): lax.dot_general(a, b, (((1,), (0,)), ((), ())), preferred_element_type=F32)  101 us
    unnamed x219, local copies, waits for them, and re-layouts  100 us
  transfers between devices with their start and end apart: 30, of which 15 were waited for; matrix products, arithmetic and copies ran while one was open for 19% of the time, Pallas kernels for 43%

profile of v2, /device:TPU:0, one launch (start us, length us, event | category | flops | bytes accessed | tf_op | source)
XLA Modules:
  0.0 1775.9 jit_solution(8038844807083041918)
XLA Ops:
  21.6 164.5 %shard_map.254 = (bf16[3,2048,1024]{2,1,0:T(8,128)(2,1)}, bf16[4,512,2048]{2,1,0:T(8,128)(2,1)}, bf16[16,16,128]{2,1,0:T(8,128)(2,1)}) custom-call(bf16[3,128,1024]{2,1,0:T(8,128)(2,1)} %w_ref.1, bf16[4,512,2048]{2,1,0:T(8,128)(2,1)} %bitcast.214, bf16[16,128]{1,0:T(8,128)(2,1)} %pad_bitcast_fusion.1.v_ref), custom_call_target="tpu_custom_call" | custom-call | tf_op jit(solution)/shard_map/pallas_call | solution.py:557
  265.8 33.1 %shard_map.258 = (bf16[2048,1024]{1,0:T(8,128)(2,1)S(1)}, f32[8,2,2048]{2,1,0:T(2,128)S(1)}) custom-call(s32[16]{0:T(128)S(1)} %select_n.106.flags, bf16[2048,1024]{1,0:T(8,128)(2,1)S(1)} %copy-done.2, bf16[2048,1024]{1,0:T(8,128)(2,1)S(1)} %copy-done.16, bf16[2048,1024]{1,0:T(8,128)(2,1)} %copy-done, bf16[128,1024]{1,0:T(8,128)(2,1)S(1)} %get-tuple-element.168.sk_ref, ...), custom_call_target="tpu_custom_call" | custom-call | flops 1000 | bytes 1000 | tf_op jit(solution)/shard_map/pallas_call | solution.py:806
  313.2 25.8 %collective-permute-done.2 = bf16[1,512,1024]{2,1,0:T(8,128)(2,1)S(1)} collective-permute-done((bf16[1,512,1024]{2,1,0:T(8,128)(2,1)S(1)}, bf16[1,512,1024]{2,1,0:T(8,128)(2,1)S(1)}, u32[]{:S(2)}, u32[]{:S(2)}) %collective-permute-start.2) | collective-permute-done | bytes 1048608 | tf_op jit(solution)/shard_map/ppermute | solution.py:1011
  340.2 71.6 %collective-permute-done.3 = bf16[1,512,1024]{2,1,0:T(8,128)(2,1)S(1)} collective-permute-done((bf16[1,512,1024]{2,1,0:T(8,128)(2,1)S(1)}, bf16[1,512,1024]{2,1,0:T(8,128)(2,1)S(1)}, u32[]{:S(2)}, u32[]{:S(2)}) %collective-permute-start.3) | collective-permute-done | bytes 1048608 | tf_op jit(solution)/shard_map/ppermute | solution.py:1011
  420.6 33.1 %shard_map.259 = (bf16[2048,1024]{1,0:T(8,128)(2,1)S(1)}, f32[8,2,2048]{2,1,0:T(2,128)S(1)}) custom-call(s32[16]{0:T(128)S(1)} %select_n.106.flags, bf16[2048,1024]{1,0:T(8,128)(2,1)S(1)} %copy-done.3, bf16[2048,1024]{1,0:T(8,128)(2,1)S(1)} %copy-done.17, bf16[2048,1024]{1,0:T(8,128)(2,1)} %copy-done, ...), custom_call_target="tpu_custom_call", output_to_operand_aliasing={{0}: (9, {}), {1}: (10, {})} | custom-call | flops 1000 | bytes 1000 | tf_op jit(solution)/shard_map/pallas_call | solution.py:806
  453.7 33.3 %shard_map.260 = (bf16[2048,1024]{1,0:T(8,128)(2,1)S(1)}, f32[8,2,2048]{2,1,0:T(2,128)S(1)}) custom-call(s32[16]{0:T(128)S(1)} %select_n.106.flags, bf16[2048,1024]{1,0:T(8,128)(2,1)S(1)} %copy-done.3, bf16[2048,1024]{1,0:T(8,128)(2,1)S(1)} %copy-done.17, bf16[2048,1024]{1,0:T(8,128)(2,1)} %copy-done, ...), custom_call_target="tpu_custom_call", output_to_operand_aliasing={{0}: (9, {}), {1}: (10, {})} | custom-call | flops 1000 | bytes 1000 | tf_op jit(solution)/shard_map/pallas_call | solution.py:806
  509.1 33.1 %shard_map.262 = (bf16[2048,1024]{1,0:T(8,128)(2,1)S(1)}, f32[8,2,2048]{2,1,0:T(2,128)S(1)}) custom-call(s32[16]{0:T(128)S(1)} %select_n.106.flags, bf16[2048,1024]{1,0:T(8,128)(2,1)S(1)} %copy-done.4, bf16[2048,1024]{1,0:T(8,128)(2,1)S(1)} %copy-done.18, bf16[2048,1024]{1,0:T(8,128)(2,1)} %copy-done, ...), custom_call_target="tpu_custom_call", output_to_operand_aliasing={{0}: (9, {}), {1}: (10, {})} | custom-call | flops 1000 | bytes 1000 | tf_op jit(solution)/shard_map/pallas_call | solution.py:806
  606.6 55.9 %fusion.4 = (bf16[2048,4096]{1,0:T(8,128)(2,1)}, bf16[2048,4096]{1,0:T(8,128)(2,1)}) fusion(f32[4096]{0:T(1024)S(1)} %reshape.297, bf16[2048,2048]{1,0:T(8,128)(2,1)} %add_convert_fusion.1.refs_0_, bf16[2048,4096]{1,0:T(8,128)(2,1)} %all-gather.6.cloned.1.call-done.refs_1_), kind=kOutput, calls=%fused_computation.5 | convolution fusion | flops 34460401664 | bytes 58736640 | tf_op jit(solution)/shard_map/dot_general | solution.py:739
  662.5 41.7 %shard_map.267.refs_1_ = bf16[2048,4096]{1,0:T(8,128)(2,1)} custom-call(bf16[2048,2048]{1,0:T(8,128)(2,1)} %bitcast.206, bf16[2048,4096]{1,0:T(8,128)(2,1)} %get-tuple-element.151.refs_1_.refs_0_), custom_call_target="tpu_custom_call" | custom-call | flops 1000 | bytes 1000 | tf_op jit(solution)/shard_map/pallas_call | solution.py:724
  704.2 37.9 %all-gather.8.cloned.1.call-done.refs_1_ = bf16[2048,4096]{1,0:T(8,128)(2,1)} async-done(((bf16[128,4096]{1,0:T(8,128)(2,1)}), bf16[2048,4096]{1,0:T(8,128)(2,1)}) %all-gather.8.cloned.1.call-update) | async-done | bytes 16777232 | tf_op jit(solution)/shard_map/all_gather | solution.py:1146
  742.2 45.0 %convert_reduce_fusion = (f32[4096]{0:T(1024)}, bf16[2048,4096]{1,0:T(8,128)(2,1)}) fusion(bf16[2048,4096]{1,0:T(8,128)(2,1)} %shard_map.268, bf16[2048,2048]{1,0:T(8,128)(2,1)} %bitcast.207, bf16[2048,4096]{1,0:T(8,128)(2,1)} %all-gather.8.cloned.1.call-done.refs_1_), kind=kOutput, calls=%fused_computation.6 | convolution fusion | flops 34401677312 | bytes 58736640 | tf_op jit(solution)/shard_map/dot_general | solution.py:739
  787.2 41.5 %shard_map.269.refs_2_.refs_0_ = bf16[2048,4096]{1,0:T(8,128)(2,1)} custom-call(bf16[2048,2048]{1,0:T(8,128)(2,1)} %add_convert_fusion.1.refs_0_, bf16[2048,4096]{1,0:T(8,128)(2,1)} %get-tuple-element.198.refs_1_.refs_0_), custom_call_target="tpu_custom_call" | custom-call | flops 1000 | bytes 1000 | tf_op jit(solution)/shard_map/pallas_call | solution.py:724
  828.7 44.3 %shard_map.270.refs_2_ = bf16[2048,2048]{1,0:T(8,128)(2,1)} custom-call(bf16[2048,4096]{1,0:T(8,128)(2,1)} %get-tuple-element.198.refs_1_.refs_0_, bf16[2048,4096]{1,0:T(8,128)(2,1)} %all-gather.6.cloned.1.call-done.refs_1_, bf16[2048,4096]{1,0:T(8,128)(2,1)} %shard_map.269.refs_2_.refs_0_), custom_call_target="tpu_custom_call" | custom-call | flops 1000 | bytes 1000 | tf_op jit(solution)/shard_map/pallas_call | solution.py:724
  873.0 36.9 %reduce-scatter.10.cloned.1.call-done.refs_1_.refs_0_ = bf16[512,4096]{1,0:T(8,128)(2,1)} async-done(((bf16[2048,4096]{1,0:T(8,128)(2,1)}), bf16[512,4096]{1,0:T(8,128)(2,1)}) %reduce-scatter.10.cloned.1.call-update) | async-done | bytes 4194320 | tf_op jit(solution)/shard_map/reduce_scatter | solution.py:1158
  997.1 43.4 %shard_map.274 = (bf16[2048,256]{1,0:T(8,128)(2,1)S(1)}, bf16[2048,256]{1,0:T(8,128)(2,1)S(1)}, bf16[2048,256]{1,0:T(8,128)(2,1)S(1)}, bf16[128,256]{1,0:T(8,128)(2,1)S(1)}, bf16[128,256]{1,0:T(8,128)(2,1)S(1)}) custom-call(s32[16]{0:T(128)S(1)} %copy-done.43, bf16[2048,1024]{1,0:T(8,128)(2,1)S(1)} %copy-done.5, bf16[2048,1024]{1,0:T(8,128)(2,1)S(1)} %copy-done.19, ...), custom_call_target="tpu_custom_call" | custom-call | flops 1000 | bytes 1000 | tf_op jit(solution)/shard_map/pallas_call | solution.py:928
  1041.4 25.3 %reduce-scatter.12.cloned.1.call-done.refs_1_.refs_0_ = bf16[512,4096]{1,0:T(8,128)(2,1)} async-done(((bf16[2048,4096]{1,0:T(8,128)(2,1)}), bf16[512,4096]{1,0:T(8,128)(2,1)}) %reduce-scatter.12.cloned.1.call-update) | async-done | bytes 4194320 | tf_op jit(solution)/shard_map/reduce_scatter | solution.py:1158
  1071.4 43.5 %shard_map.276 = (bf16[2048,256]{1,0:T(8,128)(2,1)S(1)}, bf16[2048,256]{1,0:T(8,128)(2,1)S(1)}, bf16[2048,256]{1,0:T(8,128)(2,1)S(1)}, bf16[128,256]{1,0:T(8,128)(2,1)S(1)}, bf16[128,256]{1,0:T(8,128)(2,1)S(1)}) custom-call(s32[16]{0:T(128)S(1)} %copy-done.43, bf16[2048,1024]{1,0:T(8,128)(2,1)S(1)} %copy-done.6, bf16[2048,1024]{1,0:T(8,128)(2,1)S(1)} %copy-done.20, ...), custom_call_target="tpu_custom_call" | custom-call | flops 1000 | bytes 1000 | tf_op jit(solution)/shard_map/pallas_call | solution.py:928
  1160.0 43.1 %shard_map.279 = (bf16[2048,256]{1,0:T(8,128)(2,1)S(1)}, bf16[2048,256]{1,0:T(8,128)(2,1)S(1)}, bf16[2048,256]{1,0:T(8,128)(2,1)S(1)}, bf16[128,256]{1,0:T(8,128)(2,1)S(1)}, bf16[128,256]{1,0:T(8,128)(2,1)S(1)}) custom-call(s32[16]{0:T(128)S(1)} %copy-done.43, bf16[2048,1024]{1,0:T(8,128)(2,1)S(1)} %copy-done.7, bf16[2048,1024]{1,0:T(8,128)(2,1)S(1)} %copy-done.21, ...), custom_call_target="tpu_custom_call" | custom-call | flops 1000 | bytes 1000 | tf_op jit(solution)/shard_map/pallas_call | solution.py:928
  1206.7 44.2 %shard_map.281.rest_0_ = bf16[2048,2048]{1,0:T(8,128)(2,1)} custom-call(bf16[2048,4096]{1,0:T(8,128)(2,1)} %get-tuple-element.151.refs_1_.refs_0_, bf16[2048,4096]{1,0:T(8,128)(2,1)} %all-gather.8.cloned.1.call-done.refs_1_, bf16[2048,1536]{1,0:T(8,128)(2,1)} %shard_map.280.refs_2_.refs_1_), custom_call_target="tpu_custom_call" | custom-call | flops 1000 | bytes 1000 | tf_op jit(solution)/shard_map/pallas_call | solution.py:724
  1251.1 43.2 %shard_map.282 = (bf16[2048,256]{1,0:T(8,128)(2,1)S(1)}, bf16[2048,256]{1,0:T(8,128)(2,1)S(1)}, bf16[2048,256]{1,0:T(8,128)(2,1)S(1)}, bf16[128,256]{1,0:T(8,128)(2,1)S(1)}, bf16[128,256]{1,0:T(8,128)(2,1)S(1)}) custom-call(s32[16]{0:T(128)S(1)} %copy-done.43, bf16[2048,1024]{1,0:T(8,128)(2,1)S(1)} %copy-done.8, bf16[2048,1024]{1,0:T(8,128)(2,1)S(1)} %copy-done.22, ...), custom_call_target="tpu_custom_call" | custom-call | flops 1000 | bytes 1000 | tf_op jit(solution)/shard_map/pallas_call | solution.py:928
  1375.4 46.4 %shard_map.285 = bf16[2048,2048]{1,0:T(8,128)(2,1)} custom-call(bf16[2048,3072]{1,0:T(8,128)(2,1)} %constant_dynamic-update-slice_fusion.8.refs_0_, bf16[3,2048,1024]{2,1,0:T(8,128)(2,1)} %get-tuple-element.49.refs_1_, bf16[2048,1536]{1,0:T(8,128)(2,1)} %shard_map.284.refs_2_.refs_1_), custom_call_target="tpu_custom_call" | custom-call | flops 1000 | bytes 1000 | tf_op jit(solution)/shard_map/pallas_call | solution.py:724
  1467.9 42.5 %collective-permute-done.12 = bf16[1,512,1024]{2,1,0:T(8,128)(2,1)S(1)} collective-permute-done((bf16[1,512,1024]{2,1,0:T(8,128)(2,1)S(1)}, bf16[1,512,1024]{2,1,0:T(8,128)(2,1)S(1)}, u32[]{:S(2)}, u32[]{:S(2)}) %collective-permute-start.12) | collective-permute-done | bytes 1048608 | tf_op jit(solution)/shard_map/ppermute | solution.py:1011
  1565.9 26.3 %reduce-scatter.22.cloned.1.call-done = bf16[128,1024]{1,0:T(8,128)(2,1)} async-done(((bf16[512,1024]{1,0:T(8,128)(2,1)}), bf16[128,1024]{1,0:T(8,128)(2,1)}) %reduce-scatter.22.cloned.1.call-update) | async-done | bytes 262160 | tf_op jit(solution)/shard_map/reduce_scatter | solution.py:1161
  1626.3 127.3 %shard_map.287 = (bf16[4,512,2048]{2,1,0:T(8,128)(2,1)}, f32[16,128]{1,0:T(8,128)}) custom-call(bf16[4,512,2048]{2,1,0:T(8,128)(2,1)} %bitcast.211, f32[16,16,128]{2,1,0:T(8,128)} %shard_map.286.v_ref), custom_call_target="tpu_custom_call" | custom-call | tf_op jit(solution)/shard_map/pallas_call | solution.py:656
  (427 shorter events, 577.0 us)
Async XLA Ops:
  7.2 537.0 %all-gather.4.cloned.1.call-start = ((), (), s32[]{:S(2)}) async-start(), calls=%async_computation.9 | async-start | bytes 4456448 | tf_op jit(solution)/shard_map/all_gather | solution.py:1131
  200.3 406.3 %all-gather.6.cloned.1.call-start = ((), (), s32[]{:S(2)}) async-start(), calls=%async_computation.10 | async-start | bytes 17825792 | tf_op jit(solution)/shard_map/all_gather | solution.py:1132
  224.6 517.6 %all-gather.8.cloned.1.call-start = ((), (), s32[]{:S(2)}) async-start(), calls=%async_computation.11 | async-start | bytes 17825792 | tf_op jit(solution)/shard_map/all_gather | solution.py:1146
  240.2 21.0 %collective-permute-start.1 = (bf16[2,50,1024]{2,1,0:T(8,128)(2,1)S(1)}, bf16[2,50,1024]{2,1,0:T(8,128)(2,1)S(1)}, u32[]{:S(2)}, u32[]{:S(2)}) collective-permute-start(bf16[2,50,1024]{2,1,0:T(8,128)(2,1)S(1)} %pad_maximum_fusion.3), channel_id=1, source_target_pairs={{0,4},{2,6},{1,5},{3,7},{8,12},{10,14},{9,13},{11,15},{16,20},{18,... | collective-permute-start | bytes 614408 | tf_op jit(solution)/shard_map/ppermute | solution.py:1022
  300.9 609.1 %reduce-scatter.10.cloned.1.call-start = ((), (), s32[]{:S(2)}) async-start(), calls=%async_computation.12 | async-start | bytes 20971520 | tf_op jit(solution)/shard_map/reduce_scatter | solution.py:1158
  309.0 30.1 %collective-permute-start.2 = (bf16[1,512,1024]{2,1,0:T(8,128)(2,1)S(1)}, bf16[1,512,1024]{2,1,0:T(8,128)(2,1)S(1)}, u32[]{:S(2)}, u32[]{:S(2)}) collective-permute-start(bf16[1,512,1024]{2,1,0:T(8,128)(2,1)S(1)} %get-tuple-element.165), channel_id=1, source_target_pairs={{0,2},{2,4},{4,6},{6,0},{1,3},{3,5},{5,7},{7,1},{8,10},{10,12},{12... | collective-permute-start | bytes 3145736 | tf_op jit(solution)/shard_map/ppermute | solution.py:1011
  309.0 102.8 %collective-permute-start.3 = (bf16[1,512,1024]{2,1,0:T(8,128)(2,1)S(1)}, bf16[1,512,1024]{2,1,0:T(8,128)(2,1)S(1)}, u32[]{:S(2)}, u32[]{:S(2)}) collective-permute-start(bf16[1,512,1024]{2,1,0:T(8,128)(2,1)S(1)} %get-tuple-element.164), channel_id=1, source_target_pairs={{0,4},{2,6},{4,0},{6,2},{1,5},{3,7},{5,1},{7,3},{8,12},{10,14},{12... | collective-permute-start | bytes 3145736 | tf_op jit(solution)/shard_map/ppermute | solution.py:1011
  309.0 103.9 %collective-permute-start.4 = (bf16[1,512,1024]{2,1,0:T(8,128)(2,1)S(1)}, bf16[1,512,1024]{2,1,0:T(8,128)(2,1)S(1)}, u32[]{:S(2)}, u32[]{:S(2)}) collective-permute-start(bf16[1,512,1024]{2,1,0:T(8,128)(2,1)S(1)} %get-tuple-element.163), channel_id=1, source_target_pairs={{0,6},{2,0},{4,2},{6,4},{1,7},{3,1},{5,3},{7,5},{8,14},{10,8},{12,... | collective-permute-start | bytes 3145736 | tf_op jit(solution)/shard_map/ppermute | solution.py:1011
  414.0 72.9 %collective-permute-start.5 = (bf16[4,512,1024]{2,1,0:T(8,128)(2,1)}, bf16[4,512,1024]{2,1,0:T(8,128)(2,1)}, u32[]{:S(2)}, u32[]{:S(2)}) collective-permute-start(bf16[4,512,1024]{2,1,0:T(8,128)(2,1)} %constant_dynamic-update-slice_fusion.30), channel_id=1, source_target_pairs={{0,1},{1,0},{2,3},{3,2},{4,5},{5,4},{6,7},{7,6},{8,9},{9,8},{10,11... | collective-permute-start | bytes 12582920 | tf_op jit(solution)/shard_map/ppermute | solution.py:997
  704.2 362.6 %reduce-scatter.12.cloned.1.call-start = ((), (), s32[]{:S(2)}) async-start(), calls=%async_computation.13 | async-start | bytes 20971520 | tf_op jit(solution)/shard_map/reduce_scatter | solution.py:1158
  910.0 295.1 %reduce-scatter.14.cloned.1.call-start = ((), (), s32[]{:S(2)}) async-start(), calls=%async_computation.14 | async-start | bytes 5242880 | tf_op jit(solution)/shard_map/reduce_scatter | solution.py:1158
  1066.8 293.9 %reduce-scatter.16.cloned.1.call-start = ((), (), s32[]{:S(2)}) async-start(), calls=%async_computation.15 | async-start | bytes 7864320 | tf_op jit(solution)/shard_map/reduce_scatter | solution.py:1158
  1205.1 309.7 %reduce-scatter.26.cloned.1.call-start = ((), (), s32[]{:S(2)}) async-start(), calls=%async_computation.20 | async-start | bytes 5242880 | tf_op jit(solution)/shard_map/reduce_scatter | solution.py:1161
  1205.8 320.3 %reduce-scatter.24.cloned.1.call-start = ((), (), s32[]{:S(2)}) async-start(), calls=%async_computation.19 | async-start | bytes 5242880 | tf_op jit(solution)/shard_map/reduce_scatter | solution.py:1161
  1206.6 356.0 %reduce-scatter.18.cloned.1.call-start = ((), (), s32[]{:S(2)}) async-start(), calls=%async_computation.16 | async-start | bytes 7864320 | tf_op jit(solution)/shard_map/reduce_scatter | solution.py:1158
  1250.9 170.9 %collective-permute-start.10 = (bf16[2048,2048]{1,0:T(8,128)(2,1)}, bf16[2048,2048]{1,0:T(8,128)(2,1)}, u32[]{:S(2)}, u32[]{:S(2)}) collective-permute-start(bf16[2048,2048]{1,0:T(8,128)(2,1)} %shard_map.281.rest_0_), channel_id=1, source_target_pairs={{0,1},{1,0},{2,3},{3,2},{4,5},{5,4},{6,7},{7,6},{8,9},{9,8},{10,11... | collective-permute-start | bytes 25165832 | tf_op jit(solution)/shard_map/ppermute | solution.py:997
  1295.4 20.1 %collective-permute-start.15 = (bf16[2,50,512]{2,1,0:T(8,128)(2,1)S(1)}, bf16[2,50,512]{2,1,0:T(8,128)(2,1)S(1)}, u32[]{:S(2)}, u32[]{:S(2)}) collective-permute-start(bf16[2,50,512]{2,1,0:T(8,128)(2,1)S(1)} %get-tuple-element.169), channel_id=1, source_target_pairs={{2,0},{4,2},{6,4},{3,1},{5,3},{7,5},{10,8},{12,10},{14,12},{11,9},... | collective-permute-start | bytes 307208 | tf_op jit(solution)/shard_map/ppermute | solution.py:1022
  1296.7 35.8 %collective-permute-start.16 = (bf16[2,50,512]{2,1,0:T(8,128)(2,1)S(1)}, bf16[2,50,512]{2,1,0:T(8,128)(2,1)S(1)}, u32[]{:S(2)}, u32[]{:S(2)}) collective-permute-start(bf16[2,50,512]{2,1,0:T(8,128)(2,1)S(1)} %get-tuple-element.170), channel_id=1, source_target_pairs={{4,0},{6,2},{5,1},{7,3},{12,8},{14,10},{13,9},{15,11},{20,16},{22,... | collective-permute-start | bytes 307208 | tf_op jit(solution)/shard_map/ppermute | solution.py:1022
  1360.7 231.5 %reduce-scatter.22.cloned.1.call-start = ((), (), s32[]{:S(2)}) async-start(), calls=%async_computation.18 | async-start | bytes 1310720 | tf_op jit(solution)/shard_map/reduce_scatter | solution.py:1161
  1421.8 172.4 %collective-permute-start.17 = (bf16[2048,2048]{1,0:T(8,128)(2,1)}, bf16[2048,2048]{1,0:T(8,128)(2,1)}, u32[]{:S(2)}, u32[]{:S(2)}) collective-permute-start(bf16[2048,2048]{1,0:T(8,128)(2,1)} %shard_map.285), channel_id=1, source_target_pairs={{0,1},{1,0},{2,3},{3,2},{4,5},{5,4},{6,7},{7,6},{8,9},{9,8},{10,11... | collective-permute-start | bytes 25165832 | tf_op jit(solution)/shard_map/ppermute | solution.py:997
  1437.9 28.9 %collective-permute-start.11 = (bf16[1,512,1024]{2,1,0:T(8,128)(2,1)S(1)}, bf16[1,512,1024]{2,1,0:T(8,128)(2,1)S(1)}, u32[]{:S(2)}, u32[]{:S(2)}) collective-permute-start(bf16[1,512,1024]{2,1,0:T(8,128)(2,1)S(1)} %get-tuple-element.159), channel_id=1, source_target_pairs={{0,2},{2,4},{4,6},{6,0},{1,3},{3,5},{5,7},{7,1},{8,10},{10,12},{12... | collective-permute-start | bytes 3145736 | tf_op jit(solution)/shard_map/ppermute | solution.py:1011
  1437.9 72.4 %collective-permute-start.12 = (bf16[1,512,1024]{2,1,0:T(8,128)(2,1)S(1)}, bf16[1,512,1024]{2,1,0:T(8,128)(2,1)S(1)}, u32[]{:S(2)}, u32[]{:S(2)}) collective-permute-start(bf16[1,512,1024]{2,1,0:T(8,128)(2,1)S(1)} %get-tuple-element.158), channel_id=1, source_target_pairs={{0,4},{2,6},{4,0},{6,2},{1,5},{3,7},{5,1},{7,3},{8,12},{10,14},{12... | collective-permute-start | bytes 3145736 | tf_op jit(solution)/shard_map/ppermute | solution.py:1011
  1438.0 73.5 %collective-permute-start.13 = (bf16[1,512,1024]{2,1,0:T(8,128)(2,1)S(1)}, bf16[1,512,1024]{2,1,0:T(8,128)(2,1)S(1)}, u32[]{:S(2)}, u32[]{:S(2)}) collective-permute-start(bf16[1,512,1024]{2,1,0:T(8,128)(2,1)S(1)} %get-tuple-element.157), channel_id=1, source_target_pairs={{0,6},{2,0},{4,2},{6,4},{1,7},{3,1},{5,3},{7,5},{8,14},{10,8},{12,... | collective-permute-start | bytes 3145736 | tf_op jit(solution)/shard_map/ppermute | solution.py:1011
  1526.1 231.2 %reduce-scatter.20.cloned.1.call-start = ((), (), s32[]{:S(2)}) async-start(), calls=%async_computation.17 | async-start | bytes 3932160 | tf_op jit(solution)/shard_map/reduce_scatter | solution.py:1161
  (93 other events, 4139.4 us)
Sparse Core Ops, SparseCore 0:
  200.4 73.5 all-gather.3
  277.3 271.5 all-gather.5
  552.3 189.8 all-gather.7
  745.1 164.8 reduce-scatter.9
  912.9 153.8 reduce-scatter.11
  1069.6 52.6 reduce-scatter.13
  1205.2 73.3 reduce-scatter.15
  1281.0 81.6 reduce-scatter.25
  1365.0 78.2 reduce-scatter.23
  1446.4 116.1 reduce-scatter.17
  1565.0 27.1 reduce-scatter.21
  1594.4 96.2 reduce-scatter.19

commit v3 on v2

--- a/solution.py
+++ b/solution.py
@@ -13,6 +13,10 @@
 F32 = jnp.float32
 BF = jnp.bfloat16
 SMALL_COST = pl.CostEstimate(flops=1000, bytes_accessed=1000, transcendentals=0)
+
+
+def told(microseconds):
+    return pl.CostEstimate(flops=int(microseconds * 1e9), bytes_accessed=1000, transcendentals=0)
 
 
 neg_big = -1e30
@@ -460,10 +464,11 @@
     def token_got(along):
         start = lax.rem(place + count - along, count)
         view = tokens_ref.at[start, :, columns]
-        return (
-            remote(view, view, t_send.at[along], t_recv.at[along], at(rows, start)),
-            remote(view, view, c_send.at[along], c_recv.at[along], at(rows, place, 1 - core)),
-        )
+        return remote(view, view, t_send.at[along], t_recv.at[along], at(rows, start))
+
+    def token_on(along):
+        view = tokens_ref.at[lax.rem(place + count - along, count), :, columns]
+        return remote(view, view, c_send.at[along], c_recv.at[along], at(rows, place, 1 - core))
 
     def token_far(along):
         start = lax.rem(place + count - along, count)
@@ -506,9 +511,8 @@
             pass_on(steps, side, origin(steps, side))
 
     for along in range(1, count):
-        got, on = token_got(along)
-        got.wait_recv()
-        on.start()
+        token_got(along).wait_recv()
+        token_on(along).start()
 
     def settle(t, side, seq, src):
         for copy in spread(t, side, seq, src):
@@ -541,7 +545,7 @@
                 ).wait_recv()
     for along in range(1, count):
         token_copy(along).wait_send()
-        token_got(along)[1].wait_send()
+        token_on(along).wait_send()
         token_far(along).wait_recv()
     local.wait()
     local_v.wait()
@@ -605,10 +609,11 @@
     def token_got(along):
         start = lax.rem(place + count - along, count)
         view = tokens_ref.at[start, :, columns]
-        return (
-            remote(view, view, t_send.at[along], t_recv.at[along], at(rows, start)),
-            remote(view, view, c_send.at[along], c_recv.at[along], at(rows, place, 1 - core)),
-        )
+        return remote(view, view, t_send.at[along], t_recv.at[along], at(rows, start))
+
+    def token_on(along):
+        view = tokens_ref.at[lax.rem(place + count - along, count), :, columns]
+        return remote(view, view, c_send.at[along], c_recv.at[along], at(rows, place, 1 - core))
 
     def token_far(along):
         view = tokens_ref.at[lax.rem(place + count - along, count), :, others]
@@ -637,14 +642,13 @@
         copy.wait_recv()
     sum_ref[...] = jnp.sum(held[...], axis=0)
     for along in range(1, count):
-        got, on = token_got(along)
-        got.wait_recv()
-        on.start()
+        token_got(along).wait_recv()
+        token_on(along).start()
     for copy in vectors:
         copy.wait_send()
     for along in range(1, count):
         token_copy(along).wait_send()
-        token_got(along)[1].wait_send()
+        token_on(along).wait_send()
         token_far(along).wait_recv()
     local_t.wait()
 
@@ -669,11 +673,83 @@
     )(tokens, vectors)
 
 
-def product_kernel(mode, finish, n_extra, n_out, *refs):
+class Move:
+    def __init__(self, alongs, src_ref, out_ref, sems):
+        self.alongs, self.src, self.out = alongs, src_ref, out_ref
+        self.t_send, self.t_recv, self.c_send, self.c_recv = sems
+        self.rows, self.place, self.core = [lax.axis_index(name) for name in ("rows", "seq", "fsdp")]
+        self.count = src_ref.shape[0]
+        self.width = src_ref.shape[2] // 2
+
+    def columns(self, core):
+        return pl.ds(pl.multiple_of(core * self.width, self.width), self.width)
+
+    def remote(self, src, dst, send, recv, seq, core):
+        return pltpu.make_async_remote_copy(
+            src_ref=src, dst_ref=dst, send_sem=send, recv_sem=recv, device_id=(self.rows, seq, core),
+            device_id_type=pl.DeviceIdType.MESH,
+        )
+
+    def origin(self, along):
+        return lax.rem(self.place + self.count - along, self.count)
+
+    def sent(self, n, along):
+        to = lax.rem(self.place + along, self.count)
+        src, dst = self.src.at[to, :, self.columns(self.core)], self.out.at[self.place, :, self.columns(self.core)]
+        return self.remote(src, dst, self.t_send.at[n], self.t_recv.at[n], to, self.core)
+
+    def got(self, n, along):
+        start = self.origin(along)
+        view = self.out.at[start, :, self.columns(self.core)]
+        return self.remote(view, view, self.t_send.at[n], self.t_recv.at[n], start, self.core)
+
+    def passed(self, n, along, mine):
+        view = self.out.at[self.origin(along), :, self.columns(self.core if mine else 1 - self.core)]
+        return self.remote(view, view, self.c_send.at[n], self.c_recv.at[n], self.place, 1 - self.core)
+
+    def begin(self):
+        barrier = pltpu.get_barrier_semaphore()
+        peers = sorted(set(self.alongs) | {self.count - along for along in self.alongs})
+        for along in peers:
+            device = (self.rows, lax.rem(self.place + along, self.count), self.core)
+            pl.semaphore_signal(barrier, inc=1, device_id=device, device_id_type=pl.DeviceIdType.MESH)
+        device = (self.rows, self.place, 1 - self.core)
+        pl.semaphore_signal(barrier, inc=1, device_id=device, device_id_type=pl.DeviceIdType.MESH)
+        pl.semaphore_wait(barrier, len(peers) + 1)
+        for n, along in enumerate(self.alongs):
+            self.sent(n, along).start()
+
+    def end(self):
+        for n, along in enumerate(self.alongs):
+            self.got(n, along).wait_recv()
+            self.passed(n, along, True).start()
+        for n, along in enumerate(self.alongs):
+            self.sent(n, along).wait_send()
+            self.passed(n, along, True).wait_send()
+            self.passed(n, along, False).wait_recv()
+
+
+def product_kernel(mode, finish, n_extra, n_in, move, *refs):
+    if move is None:
+        return product_step(mode, finish, n_extra, refs[: 2 + n_extra], refs[n_in:-1], refs[-1])
+    moving = Move(move, refs[2 + n_extra], refs[n_in + 1], refs[-4:])
+    ids = [pl.program_id(n) for n in range(3)]
+    ends = [pl.num_programs(n) - 1 for n in range(3)]
+
+    @pl.when((ids[0] == 0) & (ids[1] == 0) & (ids[2] == 0))
+    def _():
+        moving.begin()
+
+    product_step(mode, finish, n_extra, refs[: 2 + n_extra], refs[n_in : n_in + 1], refs[n_in + 2])
+
+    @pl.when((ids[0] == ends[0]) & (ids[1] == ends[1]) & (ids[2] == ends[2]))
+    def _():
+        moving.end()
+
+
+def product_step(mode, finish, n_extra, refs, outs, total):
     a_ref, b_ref = refs[:2]
-    extra = refs[2 : 2 + n_extra]
-    outs = refs[-1 - n_out : -1]
-    total = refs[-1]
+    extra = refs[2:]
     k = pl.program_id(2)
     last = pl.num_programs(2) - 1
     dims = {"nn": ((1,), (0,)), "nt": ((1,), (1,)), "tn": ((0,), (0,))}[mode]
@@ -703,7 +779,7 @@
     outs[0][...] = ((total + extra[0][...]) * scale).astype(BF)
 
 
-def product(a, b, mode, finish=finish_cast, rows=(), deps=(), blocks=(1024, 1024, 2048)):
+def product(a, b, mode, finish=finish_cast, rows=(), deps=(), planes=(0,), blocks=(1024, 1024, 2048), move=None):
     plane = len(b.shape) == 3
     b_shape = b.shape[-2:]
     m, depth = a.shape if mode != "tn" else a.shape[::-1]
@@ -713,26 +789,46 @@
     a_spec = (
         spec((bk, bm), lambda j, i, k: (k, i)) if mode == "tn" else spec((bm, bk), lambda j, i, k: (i, k))
     )
-    if plane:
-        b_spec = spec((None, bn, bk), lambda j, i, k: (k % b.shape[0], j, k // b.shape[0]))
+    first, turns = planes[0], len(planes)
+    if plane and mode == "nt":
+        b_spec = spec((None, bn, bk), lambda j, i, k: (first + k % turns, j, k // turns))
+    elif plane:
+        b_spec = spec((None, bk, bn), lambda j, i, k: (first, k, j))
     elif mode == "nt":
         b_spec = spec((bn, bk), lambda j, i, k: (j, k))
     else:
         b_spec = spec((bk, bn), lambda j, i, k: (k, j))
     row = spec((1, bn), lambda j, i, k: (0, j))
     field = spec((bm, bn), lambda j, i, k: (i, j))
+    out_specs, out_shape = field, jax.ShapeDtypeStruct((m, n), BF)
+    scratch, aliases, inputs = [pltpu.VMEM((bm, bn), F32)], {}, (a, b, *rows)
+    params = dict(vmem_limit_bytes=48 * 2**20)
+    if move is not None:
+        src, target, alongs, ident = move
+        out_specs, out_shape = (
+            [field, spec(memory_space=pl.ANY)],
+            [out_shape, jax.ShapeDtypeStruct(src.shape, src.dtype)],
+        )
+        dma = pltpu.SemaphoreType.DMA
+        scratch += [dma((len(alongs),))] * 4
+        aliases = {len(inputs) + 1: 1}
+        inputs += (src, target)
+        params.update(collective_id=ident, has_side_effects=True)
+        move = alongs
+    n_in = len(inputs) + len(deps)
     return pl.pallas_call(
-        functools.partial(product_kernel, mode, finish, len(rows), 1),
+        functools.partial(product_kernel, mode, finish, len(rows), n_in, move),
         grid=(n // bn, m // bm, depth // bk),
         in_specs=[a_spec, b_spec]
         + [row] * len(rows)
-        + [spec(memory_space=pl.ANY)] * len(deps),
-        out_specs=field,
-        out_shape=jax.ShapeDtypeStruct((m, n), BF),
-        scratch_shapes=[pltpu.VMEM((bm, bn), F32)],
-        cost_estimate=SMALL_COST,
-        compiler_params=pltpu.CompilerParams(vmem_limit_bytes=48 * 2**20),
-    )(a, b, *rows, *deps)
+        + [spec(memory_space=pl.ANY)] * (n_in - 2 - len(rows)),
+        out_specs=out_specs,
+        out_shape=out_shape,
+        scratch_shapes=scratch,
+        input_output_aliases=aliases,
+        cost_estimate=told(2.0 * m * n * depth / 8e8),
+        compiler_params=pltpu.CompilerParams(**params),
+    )(*inputs, *deps)
 
 
 def dot_nt(a,b): return lax.dot_general(a,b,(((1,),(1,)),((),())),preferred_element_type=F32)
@@ -836,7 +932,7 @@
             jax.ShapeDtypeStruct((width // 128, 2, seg), F32),
         ],
         input_output_aliases={9: 0, 10: 1} if earlier_out else {},
-        cost_estimate=SMALL_COST,
+        cost_estimate=told(4.2 * pairs * 4),
         compiler_params=pltpu.CompilerParams(vmem_limit_bytes=40 * 2**20),
     )(flags, q, k, v, sk, sv, start, doc, sdoc, *extra)
 
@@ -960,7 +1056,7 @@
         ),
         out_shape=[jax.ShapeDtypeStruct((seg, pairs * 128), BF)] * 3
         + [jax.ShapeDtypeStruct((128, pairs * 128), BF)] * 2,
-        cost_estimate=SMALL_COST,
+        cost_estimate=told(5.5 * pairs * 4),
         compiler_params=pltpu.CompilerParams(vmem_limit_bytes=40 * 2**20),
     )(flags, q, k, v, do, o, sk, sv, lse, start, doc, sdoc, *deps)
 
@@ -990,6 +1086,15 @@
     )(value, *deps)
 
 
+def blank(shape, dtype):
+    return pl.pallas_call(
+        lambda ref: None,
+        out_specs=pl.BlockSpec(memory_space=pl.ANY),
+        out_shape=jax.ShapeDtypeStruct(shape, dtype),
+        cost_estimate=SMALL_COST,
+    )()
+
+
 BOTH = ("rows", "seq")
 
 
@@ -997,7 +1102,7 @@
     return lax.ppermute(block, "fsdp", ((0, 1), (1, 0)))
 
 
-def exchange(field):
+def along_line(field, hold=()):
     count = lax.axis_size("seq")
     me = lax.axis_index("seq")
     core = lax.axis_index("fsdp")
@@ -1009,8 +1114,15 @@
     for away in range(1, count):
         block = lax.dynamic_slice_in_dim(mine, lax.rem(me + away, count), 1, 0)
         moved = lax.ppermute(block, "seq", [(n, (n + away) % count) for n in range(count)])
+        moved = gate(moved, *hold) if hold else moved
         got = lax.dynamic_update_slice_in_dim(got, moved, lax.rem(me + count - away, count), 0)
+    return got
+
+
+def between_cores(got, hold=()):
+    core = lax.axis_index("fsdp")
     other = other_core(got)
+    other = gate(other, *hold) if hold else other
     low_half = jnp.where(core == 0, got, other)
     high_half = jnp.where(core == 0, other, got)
     return jnp.concatenate((low_half, high_half), axis=2)
@@ -1085,7 +1197,8 @@
     vector = jnp.concatenate([item.reshape(-1) for item in small])
     room = -(-vector.shape[0] // 2048) * 2048
     vector = jnp.pad(vector, (0, room - vector.shape[0])).reshape(-1, 128)
-    qkv_full, tokens, packed = opening(w_qkv, states[0], vector)
+    attn_weights = jnp.concatenate((w_qkv, w_out.T[None]), axis=0)
+    attn_full, tokens, packed = opening(attn_weights, states[0], vector)
     tokens = tokens.reshape(seg_len, model)
     packed = packed.reshape(packed.shape[0], -1)
     cuts = []
@@ -1122,30 +1235,31 @@
     tokens_f = tokens.astype(F32)
     normed_one, mean_one, scale_one = norm_forward(tokens_f, gain_a, shift_a)
     query = product(
-        normed_one, qkv_full[0], "nn", functools.partial(finish_bias, HEAD**-0.5), (bias_pair[:1],)
-    )
-    keys = product(normed_one, qkv_full[1], "nn")
+        normed_one, attn_full, "nn", functools.partial(finish_bias, HEAD**-0.5), (bias_pair[:1],), planes=(0,)
+    )
+    keys = product(normed_one, attn_full, "nn", planes=(1,))
     values = product(
-        normed_one, qkv_full[2], "nn", functools.partial(finish_bias, 1.0), (bias_pair[1:],)
-    )
-    out_full = lax.all_gather(gate(w_out.T, normed_one), BOTH, axis=0, tiled=True)
-    up_full = lax.all_gather(gate(w_up, values), BOTH, axis=0, tiled=True)
-    grad_out = exchange(gate(cotangent[0], query)).reshape(seg_len, model)
+        normed_one, attn_full, "nn", functools.partial(finish_bias, 1.0), (bias_pair[1:],), planes=(2,)
+    )
+    up_full = lax.all_gather(gate(w_up, normed_one), BOTH, axis=0, tiled=True)
     tail = jnp.stack((keys[seg_len - SUMM :], values[seg_len - SUMM :]))
     lent = jnp.concatenate((shift_by(tail, 1), shift_by(tail, 2)), axis=1)
     lent = jnp.pad(lent, ((0, 0), (0, 128 - 2 * SUMM), (0, 0)))
     pairs = half // 128
     each = pairs // 4
     attended = ()
+    done = []
     for n in range(4):
         attended = attn_fwd(
             query, keys, values, lent[0], lent[1], start, doc_row, sum_docs, flags, tile,
-            n * each, each, attended, (grad_out,) if n == 3 else (),
-        )
-        if n == 0:
-            down_full = lax.all_gather(gate(w_down.T, attended[0]), BOTH, axis=0, tiled=True)
+            n * each, each, attended,
+        )
+        done.append(attended[1])
+    down_full = lax.all_gather(gate(w_down.T, values), BOTH, axis=0, tiled=True)
     mixed, log_sum = attended
-    attended = product(mixed, out_full, "nt")
+    attended = product(mixed, attn_full, "nt", planes=(3,))
+    grad_out = along_line(gate(cotangent[0], query), (done[2],))
+    grad_out = between_cores(grad_out, (attended,)).reshape(seg_len, model)
     hidden = tokens_f + both_halves(attended) + bias_o
     normed_two, mean_two, scale_two = norm_forward(hidden, gain_b, shift_b)
     up_proj = mm(normed_two, up_full) + bias_u
@@ -1158,7 +1272,7 @@
         return lax.psum_scatter(partial, "rows", scatter_dimension=0, tiled=True)
 
     def over_seq(partial):
-        return lax.psum_scatter(partial, "seq", scatter_dimension=0, tiled=True).astype(F32)
+        return lax.psum_scatter(partial, "seq", scatter_dimension=0, tiled=True)
 
     down_sum = product(grad_out, activated, "tn")
     down_rows = over_rows(down_sum)
@@ -1166,26 +1280,27 @@
     d_up = (mm(grad_out, down_full) * slope.astype(F32)).astype(BF)
     up_sum = product(normed_two, d_up, "tn")
     d_norm_part = product(d_up, up_full, "nt", deps=(up_sum,))
-    up_turn = gate(up_sum, down_rows, d_norm_part)
+    d_norm_other = other_core(d_norm_part)
+    up_turn = gate(up_sum, down_rows, d_norm_other)
     up_rows = over_rows(up_turn)
-    d_norm_two = both_halves(d_norm_part)
+    d_norm_two = d_norm_part.astype(F32) + d_norm_other.astype(F32)
     d_hidden_ln, grad_gain_two, grad_shift_two = norm_backward(
         hidden, mean_two, scale_two, gain_b, d_norm_two
     )
     d_hidden = grad_out.astype(F32) + d_hidden_ln
     d_hidden_low = d_hidden.astype(BF)
-    d_mixed = product(d_hidden_low, out_full, "nn", deps=(up_turn,))
+    d_mixed = product(d_hidden_low, attn_full, "nn", deps=(up_turn,), planes=(3,))
     out_sum = product(d_hidden_low, mixed, "tn", deps=(d_mixed,))
 
-    def back(n, deps):
+    def back(n, count, deps):
         return attn_bwd(
             query, keys, values, d_mixed, mixed, lent[0], lent[1], log_sum, start, doc_row,
-            sum_docs, flags, tile, n * each, each, deps,
-        )
-
-    def own_half(pieces):
+            sum_docs, flags, tile, n * each, count * each, deps,
+        )
+
+    def own_half(pieces, move, deps=()):
         d_pre, d_keys, d_values, d_lent_k, d_lent_v = [
-            jnp.concatenate(pair, axis=1) for pair in zip(*pieces)
+            jnp.concatenate(pair, axis=1) if len(pair) > 1 else pair[0] for pair in zip(*pieces)
         ]
         d_lent = jnp.stack((d_lent_k, d_lent_v))
         back_home = shift_by(d_lent[:, :SUMM], -1).astype(F32) + shift_by(
@@ -1196,37 +1311,50 @@
         d_keys = lax.dynamic_update_slice(d_keys, ends[0], (seg_len - SUMM, 0))
         d_values = lax.dynamic_update_slice(d_values, ends[1], (seg_len - SUMM, 0))
         grads = jnp.concatenate((d_pre, d_keys, d_values), axis=1)
-        return grads, product(normed_one, grads, "tn", blocks=(1024, grads.shape[1] // 2, 2048))
-
-    piece_0 = back(0, (out_sum,))
-    down_turn = gate(down_rows, up_rows, piece_0[0])
-    out_rows = over_rows(gate(out_sum, up_rows, down_turn))
-    grad_w_down = over_seq(down_turn)
-    piece_1 = back(1, (down_turn,))
-    first_half, first_sum = own_half((piece_0, piece_1))
-    piece_2 = back(2, (first_sum,))
-    first_turn = gate(first_sum, out_rows, piece_2[0])
+        return grads, product(
+            normed_one, grads, "tn", blocks=(1024, grads.shape[1] // 2, 2048), move=move, deps=deps
+        )
+
+    piece_0 = back(0, 1, (out_sum,))
+    out_partial = product(activated, down_full, "nt", deps=(piece_0[0],))
+    down_turn = gate(down_rows, up_rows, out_partial)
+    down_seq = over_seq(down_turn)
+    grad_w_down = down_seq.astype(F32)
+    out_tokens = (hidden + both_halves(out_partial) + bias_d).astype(BF).reshape(segs, width, model)
+    out_own = lax.dynamic_slice_in_dim(out_tokens, place, 1, 0)
+    out_begun = lax.dynamic_update_slice_in_dim(blank(out_tokens.shape, BF), out_own, place, 0)
+    piece_1 = back(1, 1, (down_turn, out_begun))
+    out_turn = gate(out_sum, down_seq, piece_1[0])
+    out_rows = over_rows(out_turn)
+    first_half, (first_sum, out_moved) = own_half((piece_0, piece_1), (out_tokens, out_begun, (1,), 2), (out_turn,))
+    up_turn_two = gate(up_rows, out_rows, first_sum)
+    up_seq = over_seq(up_turn_two)
+    grad_w_up = up_seq.astype(F32)
+    first_turn = gate(first_sum, up_turn_two)
     first_rows = over_rows(first_turn)
-    grad_w_up = over_seq(gate(up_rows, first_turn))
-    out_partial = product(activated, down_full, "nt", deps=(first_turn,))
-    out_tokens = (hidden + both_halves(out_partial) + bias_d).astype(BF)
-    out_states = exchange(out_tokens.reshape(segs, width, model))[None]
-    piece_3 = back(3, (out_partial,))
-    second_half, second_sum = own_half((piece_2, piece_3))
-    second_turn = gate(second_sum, first_rows)
+    piece_2 = back(2, 2, (first_turn,))
+    second_half, (second_sum, out_moved) = own_half((piece_2,), (out_tokens, out_moved, (segs - 1,), 3))
+    second_turn = gate(second_sum, first_rows, up_seq)
     second_rows = over_rows(second_turn)
     d_qkv = jnp.concatenate((first_half, second_half), axis=1)
-    d_norm_one = both_halves(product(d_qkv, qkv_full, "nt", deps=(second_turn,), blocks=(1024, 1024, half // 2)))
-    grad_w_out = over_seq(gate(out_rows, second_turn))
-    qkv_rows = jnp.concatenate((first_rows, second_rows), axis=1)
-    grad_w_qkv = over_seq(qkv_rows)
-    grad_w_qkv = jnp.transpose(grad_w_qkv.reshape(-1, 2, 3, half // 2), (2, 0, 1, 3)).reshape(3, -1, half)
-    grad_w_out = grad_w_out.T
+    d_norm_part, out_moved = product(
+        d_qkv, attn_full, "nt", deps=(second_turn,), blocks=(1024, 1024, half // 2), planes=(0, 1, 2),
+        move=(out_tokens, out_moved, tuple(range(2, segs - 1)), 4),
+    )
+    out_states = out_moved[None]
+    d_norm_other = other_core(d_norm_part)
+    d_norm_one = d_norm_part.astype(F32) + d_norm_other.astype(F32)
+    out_seq = over_seq(gate(out_rows, second_turn))
     grad_w_down = grad_w_down.T
     d_tokens_ln, grad_gain_one, grad_shift_one = norm_backward(
         tokens_f, mean_one, scale_one, gain_a, d_norm_one
     )
     grad_tokens = (d_hidden + d_tokens_ln).astype(BF)
+    qkv_rows = gate(jnp.concatenate((first_rows, gate(second_rows, d_norm_other)), axis=1), d_norm_other)
+    grad_w_qkv = over_seq(qkv_rows).astype(F32)
+    grad_w_out = gate(out_seq, grad_tokens).astype(F32)
+    grad_w_qkv = jnp.transpose(grad_w_qkv.reshape(-1, 2, 3, half // 2), (2, 0, 1, 3)).reshape(3, -1, half)
+    grad_w_out = grad_w_out.T
     def column_sum(field):
         return jnp.sum(field.astype(F32), axis=0)
 

time: 1780 us -> 1620 us (0.910)
  waiting for transfers between devices: 381 us -> 184 us
  Pallas kernels: 930 us -> 985 us
    ppermute x6 -> x3, waiting for transfers between devices: 165 us -> 13.6 us  [along_line(): lax.ppermute(block, 'seq', [(n, (n + away) % count) for n in range(count)])]
    reduce_scatter x5, waiting for transfers between devices: 80 us -> 10.4 us  [over_rows(): return lax.psum_scatter(partial, 'rows', scatter_dimension=0, tiled=True)]
    pallas_call x13, Pallas kernels: 332 us -> 370 us  [product(): pl.pallas_call(functools.partial(product_kernel, mode, finish, len(rows),...]
    all_gather x3 -> x2, waiting for transfers between devices: 37.9 us -> 71.3 us  [the longest x1 71.3 us: layer_by_segment(): down_full = lax.all_gather(gate(w_down.T, values), BOTH, axis=0, tiled=True)]
    pallas_call x1, Pallas kernels: 165 us -> 193 us  [opening(): pl.pallas_call(opening_kernel, in_specs=[anywhere] * 3, out_specs=[anywhe...]
    pallas_call x4 -> x3, Pallas kernels: 173 us -> 156 us  [attn_bwd(): pl.pallas_call(functools.partial(bwd_kernel, tile), grid_spec=pltpu.Prefe...]
    ppermute x6 -> x5, waiting for transfers between devices: 25.7 us -> 39.9 us  [other_core(): return lax.ppermute(block, 'fsdp', ((0, 1), (1, 0)))]
    unnamed x219 -> x222, local copies, waits for them, and re-layouts: 100 us -> 104 us
  transfers between devices with their start and end apart: 30 -> 25, of which waited for: 15 -> 11; matrix products, arithmetic and copies ran while one was open for 19% -> 19% of each run, Pallas kernels for 43% -> 49%
where the time goes in v3:
time: 1620 us; the launch traced here: 1610 us
  Pallas kernels  985 us (61%)
  waiting for transfers between devices  184 us (11%)
  other arithmetic  173 us (11%)
  local copies, waits for them, and re-layouts  136 us (8%)
  matrix products  101 us (6%)
    pallas_call x13, Pallas kernels, product(): pl.pallas_call(functools.partial(product_kernel, mode, finish, len(rows),...  370 us
    pallas_call x1, Pallas kernels, opening(): pl.pallas_call(opening_kernel, in_specs=[anywhere] * 3, out_specs=[anywhe...  193 us
    pallas_call x3, Pallas kernels, attn_bwd(): pl.pallas_call(functools.partial(bwd_kernel, tile), grid_spec=pltpu.Prefe...  156 us
    pallas_call x1, Pallas kernels, closing(): pl.pallas_call(closing_kernel, in_specs=[anywhere] * 2, out_specs=[anywhe...  145 us
    pallas_call x4, Pallas kernels, attn_fwd(): pl.pallas_call(functools.partial(fwd_kernel, tile), grid_spec=pltpu.Prefe...  121 us
    unnamed x222, local copies, waits for them, and re-layouts  104 us
    dot_general x2, matrix products, dot_nn(): lax.dot_general(a, b, (((1,), (0,)), ((), ())), preferred_element_type=F32)  101 us
    all_gather x1, waiting for transfers between devices, layer_by_segment(): down_full = lax.all_gather(gate(w_down.T, values), BOTH, axis=0, tiled=True)  71.3 us
  transfers between devices with their start and end apart: 25, of which 11 were waited for; matrix products, arithmetic and copies ran while one was open for 19% of the time, Pallas kernels for 49%

profile of v3, /device:TPU:0, one launch (start us, length us, event | category | flops | bytes accessed | tf_op | source)
XLA Modules:
  0.0 1606.4 jit_solution(11291027572662378164)
XLA Ops:
  22.0 192.6 %shard_map.254 = (bf16[4,2048,1024]{2,1,0:T(8,128)(2,1)}, bf16[4,512,2048]{2,1,0:T(8,128)(2,1)}, bf16[16,16,128]{2,1,0:T(8,128)(2,1)}) custom-call(bf16[4,128,1024]{2,1,0:T(8,128)(2,1)} %pad_maximum_fusion.4.w_ref, bf16[4,512,2048]{2,1,0:T(8,128)(2,1)} %bitcast.209, bf16[16,128]{1,0:T(8,128)(2,1)} %pad_bitcast_fusion.1.v_ref), custom_call_target="tpu_custom_call" | custom-call | tf_op jit(solution)/shard_map/pallas_call | solution.py:561
  296.0 30.2 %shard_map.259 = (bf16[2048,1024]{1,0:T(8,128)(2,1)S(1)}, f32[8,2,2048]{2,1,0:T(2,128)S(1)}) custom-call(s32[16]{0:T(128)S(1)} %select_n.90.flags, bf16[2048,1024]{1,0:T(8,128)(2,1)S(1)} %copy-done.10, bf16[2048,1024]{1,0:T(8,128)(2,1)S(1)} %copy-done.35, bf16[2048,1024]{1,0:T(8,128)(2,1)} %copy-done.8, bf16[128,1024]{1,0:T(8,128)(2,1)S(1)} %get-tuple-element.161.sk_ref, ...), custom_call_target="tpu_custom_call" | custom-call | flops 33600000000 | bytes 1000 | tf_op jit(solution)/shard_map/pallas_call | solution.py:902
  326.2 30.2 %shard_map.260 = (bf16[2048,1024]{1,0:T(8,128)(2,1)S(1)}, f32[8,2,2048]{2,1,0:T(2,128)S(1)}) custom-call(s32[16]{0:T(128)S(1)} %select_n.90.flags, bf16[2048,1024]{1,0:T(8,128)(2,1)S(1)} %copy-done.10, bf16[2048,1024]{1,0:T(8,128)(2,1)S(1)} %copy-done.35, bf16[2048,1024]{1,0:T(8,128)(2,1)} %copy-done.8, ...), custom_call_target="tpu_custom_call", output_to_operand_aliasing={{0}: (9, {}), {1}: (10, {})} | custom-call | flops 33600000000 | bytes 1000 | tf_op jit(solution)/shard_map/pallas_call | solution.py:902
  356.4 30.2 %shard_map.261 = (bf16[2048,1024]{1,0:T(8,128)(2,1)S(1)}, f32[8,2,2048]{2,1,0:T(2,128)S(1)}) custom-call(s32[16]{0:T(128)S(1)} %select_n.90.flags, bf16[2048,1024]{1,0:T(8,128)(2,1)S(1)} %copy-done.10, bf16[2048,1024]{1,0:T(8,128)(2,1)S(1)} %copy-done.35, bf16[2048,1024]{1,0:T(8,128)(2,1)} %copy-done.8, ...), custom_call_target="tpu_custom_call", output_to_operand_aliasing={{0}: (9, {}), {1}: (10, {})} | custom-call | flops 33600000000 | bytes 1000 | tf_op jit(solution)/shard_map/pallas_call | solution.py:902
  412.3 30.6 %shard_map.265 = (bf16[2048,1024]{1,0:T(8,128)(2,1)S(1)}, f32[8,2,2048]{2,1,0:T(2,128)S(1)}) custom-call(s32[16]{0:T(128)S(1)} %select_n.90.flags, bf16[2048,1024]{1,0:T(8,128)(2,1)S(1)} %copy-done.11, bf16[2048,1024]{1,0:T(8,128)(2,1)S(1)} %copy-done.36, bf16[2048,1024]{1,0:T(8,128)(2,1)} %copy-done.8, ...), custom_call_target="tpu_custom_call", output_to_operand_aliasing={{0}: (9, {}), {1}: (10, {})} | custom-call | flops 33600000000 | bytes 1000 | tf_op jit(solution)/shard_map/pallas_call | solution.py:902
  493.3 14.6 fusion.41
  526.7 56.0 %multiply_convert_fusion.1 = (bf16[2048,4096]{1,0:T(8,128)(2,1)}, bf16[2048,4096]{1,0:T(8,128)(2,1)}) fusion(f32[4096]{0:T(1024)S(1)} %reshape.297, bf16[2048,2048]{1,0:T(8,128)(2,1)} %add_convert_fusion.1.refs_0_, bf16[2048,4096]{1,0:T(8,128)(2,1)} %all-gather.5.cloned.1.call-done.refs_1_), kind=kOutput, calls=%fused_computation.8 | convolution fusion | flops 34460401664 | bytes 58736640 | tf_op jit(solution)/shard_map/dot_general | solution.py:835
  582.8 42.1 %shard_map.270.refs_1_ = bf16[2048,4096]{1,0:T(8,128)(2,1)} custom-call(bf16[2048,2048]{1,0:T(8,128)(2,1)} %bitcast.202, bf16[2048,4096]{1,0:T(8,128)(2,1)} %get-tuple-element.152.refs_1_.refs_0_), custom_call_target="tpu_custom_call" | custom-call | flops 42949672960 | bytes 1000 | tf_op jit(solution)/shard_map/pallas_call | solution.py:819
  625.0 71.3 %all-gather.3.cloned.1.call-done.refs_1_ = bf16[2048,4096]{1,0:T(8,128)(2,1)} async-done(((bf16[128,4096]{1,0:T(8,128)(2,1)}), bf16[2048,4096]{1,0:T(8,128)(2,1)}) %all-gather.3.cloned.1.call-update) | async-done | bytes 16777232 | tf_op jit(solution)/shard_map/all_gather | solution.py:1258
  696.2 45.3 %convert_reduce_fusion = (f32[4096]{0:T(1024)}, bf16[2048,4096]{1,0:T(8,128)(2,1)}) fusion(bf16[2048,4096]{1,0:T(8,128)(2,1)} %shard_map.271, bf16[2048,2048]{1,0:T(8,128)(2,1)} %bitcast.203, bf16[2048,4096]{1,0:T(8,128)(2,1)} %all-gather.3.cloned.1.call-done.refs_1_), kind=kOutput, calls=%fused_computation.6 | convolution fusion | flops 34401677312 | bytes 58736640 | tf_op jit(solution)/shard_map/dot_general | solution.py:835
  741.5 41.5 %shard_map.272.refs_2_.refs_0_ = bf16[2048,4096]{1,0:T(8,128)(2,1)} custom-call(bf16[2048,2048]{1,0:T(8,128)(2,1)} %add_convert_fusion.1.refs_0_, bf16[2048,4096]{1,0:T(8,128)(2,1)} %get-tuple-element.191.refs_1_.refs_0_), custom_call_target="tpu_custom_call" | custom-call | flops 42949672960 | bytes 1000 | tf_op jit(solution)/shard_map/pallas_call | solution.py:819
  783.0 44.5 %shard_map.273 = bf16[2048,2048]{1,0:T(8,128)(2,1)} custom-call(bf16[2048,4096]{1,0:T(8,128)(2,1)} %get-tuple-element.191.refs_1_.refs_0_, bf16[2048,4096]{1,0:T(8,128)(2,1)} %all-gather.5.cloned.1.call-done.refs_1_, bf16[2048,4096]{1,0:T(8,128)(2,1)} %shard_map.272.refs_2_.refs_0_), custom_call_target="tpu_custom_call" | custom-call | flops 42949672960 | bytes 1000 | tf_op jit(solution)/shard_map/pallas_call | solution.py:819
  852.1 15.3 multiply_reduce_fusion
  867.4 17.0 %fusion.40 = (f32[2048]{0:T(1024)}, f32[2048,2048]{1,0:T(8,128)S(1)}) fusion(f32[2048]{0:T(1024)S(1)} %broadcast_multiply_fusion.2, f32[2048,2048]{1,0:T(8,128)} %get-tuple-element.151, f32[2048]{0:T(1024)S(1)} %copy-done.62, f32[2048]{0:T(1024)S(1)} %broadcast_multiply_fusion.3, f32[2048]{0:T(1024)S(1)} %copy-done.73, ...), kind=kLoop, calls=%fused_computation.161 | loop fusion | flops 54523904 | bytes 58769408 | tf_op jit(solution)/shard_map/reduce_sum | solution.py:1359
  924.1 39.6 %shard_map.277 = (bf16[2048,256]{1,0:T(8,128)(2,1)S(1)}, bf16[2048,256]{1,0:T(8,128)(2,1)S(1)}, bf16[2048,256]{1,0:T(8,128)(2,1)S(1)}, bf16[128,256]{1,0:T(8,128)(2,1)S(1)}, bf16[128,256]{1,0:T(8,128)(2,1)S(1)}) custom-call(s32[16]{0:T(128)S(1)} %select_n.90.flags, bf16[2048,1024]{1,0:T(8,128)(2,1)S(1)} %copy-done.12, bf16[2048,1024]{1,0:T(8,128)(2,1)S(1)} %copy-done.37, ...), custom_call_target="tpu_custom_call" | custom-call | flops 44000002048 | bytes 1000 | tf_op jit(solution)/shard_map/pallas_call | solution.py:1024
  964.7 44.4 %shard_map.278.refs_2_ = bf16[2048,2048]{1,0:T(8,128)(2,1)} custom-call(bf16[2048,4096]{1,0:T(8,128)(2,1)} %get-tuple-element.152.refs_1_.refs_0_, bf16[2048,4096]{1,0:T(8,128)(2,1)} %all-gather.3.cloned.1.call-done.refs_1_, bf16[2048,256]{1,0:T(8,128)(2,1)S(1)} %get-tuple-element.59.refs_2_), custom_call_target="tpu_custom_call" | custom-call | flops 42949672960 | bytes 1000 | tf_op jit(solution)/shard_map/pallas_call | solution.py:819
  1041.6 39.5 %shard_map.281 = (bf16[2048,256]{1,0:T(8,128)(2,1)S(1)}, bf16[2048,256]{1,0:T(8,128)(2,1)S(1)}, bf16[2048,256]{1,0:T(8,128)(2,1)S(1)}, bf16[128,256]{1,0:T(8,128)(2,1)S(1)}, bf16[128,256]{1,0:T(8,128)(2,1)S(1)}) custom-call(s32[16]{0:T(128)S(1)} %select_n.90.flags, bf16[2048,1024]{1,0:T(8,128)(2,1)S(1)} %copy-done.13, bf16[2048,1024]{1,0:T(8,128)(2,1)S(1)} %copy-done.38, ...), custom_call_target="tpu_custom_call" | custom-call | flops 44000002048 | bytes 1000 | tf_op jit(solution)/shard_map/pallas_call | solution.py:1024
  1124.5 33.6 %shard_map.283 = (bf16[2048,1536]{1,0:T(8,128)(2,1)}, bf16[4,512,2048]{2,1,0:T(8,128)(2,1)}) custom-call(bf16[2048,2048]{1,0:T(8,128)(2,1)} %fusion.13.refs_0_.refs_1_, bf16[2048,1536]{1,0:T(8,128)(2,1)} %pad_maximum_fusion.1.refs_1_, bf16[4,512,2048]{2,1,0:T(8,128)(2,1)} %bitcast.205, ...), custom_call_target="tpu_custom_call", output_to_operand_aliasing={{1}: (3, {})} | custom-call | flops 16106127360 | bytes 1000 | tf_op jit(solution)/shard_map/pallas_call | solution.py:819
  1163.8 76.9 %shard_map.286 = (bf16[2048,512]{1,0:T(8,128)(2,1)S(1)}, bf16[2048,512]{1,0:T(8,128)(2,1)S(1)}, bf16[2048,512]{1,0:T(8,128)(2,1)S(1)}, bf16[128,512]{1,0:T(8,128)(2,1)S(1)}, bf16[128,512]{1,0:T(8,128)(2,1)S(1)}) custom-call(s32[16]{0:T(128)S(1)} %copy-done.40, bf16[2048,1024]{1,0:T(8,128)(2,1)S(1)} %copy-done.14, bf16[2048,1024]{1,0:T(8,128)(2,1)} %copy-done.34, ...), custom_call_target="tpu_custom_call" | custom-call | flops 88000004096 | bytes 1000 | tf_op jit(solution)/shard_map/pallas_call | solution.py:1024
  1244.6 20.0 %collective-permute-done.11 = bf16[2,50,512]{2,1,0:T(8,128)(2,1)S(1)} collective-permute-done((bf16[2,50,512]{2,1,0:T(8,128)(2,1)S(1)}, bf16[2,50,512]{2,1,0:T(8,128)(2,1)S(1)}, u32[]{:S(2)}, u32[]{:S(2)}) %collective-permute-start.11) | collective-permute-done | bytes 102432 | tf_op jit(solution)/shard_map/ppermute | solution.py:1134
  1278.0 32.2 %shard_map.287 = (bf16[2048,1536]{1,0:T(8,128)(2,1)}, bf16[4,512,2048]{2,1,0:T(8,128)(2,1)}) custom-call(bf16[2048,2048]{1,0:T(8,128)(2,1)} %fusion.13.refs_0_.refs_1_, bf16[2048,1536]{1,0:T(8,128)(2,1)} %pad_maximum_fusion.2.refs_1_, bf16[4,512,2048]{2,1,0:T(8,128)(2,1)} %bitcast.206, ...), custom_call_target="tpu_custom_call", output_to_operand_aliasing={{1}: (3, {})} | custom-call | flops 16106127360 | bytes 1000 | tf_op jit(solution)/shard_map/pallas_call | solution.py:819
  1322.0 54.9 %shard_map.289 = (bf16[2048,2048]{1,0:T(8,128)(2,1)}, bf16[4,512,2048]{2,1,0:T(8,128)(2,1)}) custom-call(bf16[2048,3072]{1,0:T(8,128)(2,1)} %copy-done.49, bf16[4,2048,1024]{2,1,0:T(8,128)(2,1)} %get-tuple-element.50.refs_1_, bf16[4,512,2048]{2,1,0:T(8,128)(2,1)} %bitcast.207, ...), custom_call_target="tpu_custom_call", output_to_operand_aliasing={{1}: (3, {})} | custom-call | flops 32212254720 | bytes 1000 | tf_op jit(solution)/shard_map/pallas_call | solution.py:819
  1409.1 19.4 %fusion.18.refs_1_ = bf16[2048,2048]{1,0:T(8,128)(2,1)} fusion(f32[2048,2048]{1,0:T(8,128)} %copy-done.46, bf16[4,512,2048]{2,1,0:T(8,128)(2,1)} %get-tuple-element.48, bf16[2048,2048]{1,0:T(8,128)(2,1)} %collective-permute-done.13.refs_1_, bf16[2048,2048]{1,0:T(8,128)(2,1)} %get-tuple-element.79, f32[2048]{0:T(1024)S(1)} %broadcast_multiply_fusion, ...), kind=kLoop, calls=%fused_computation.28 | loop fusion | flops 54525952 | bytes 50372608 | tf_op jit(solution)/shard_map/convert_element_type | solution.py:1352
  1431.2 144.7 %shard_map.293 = (bf16[4,512,2048]{2,1,0:T(8,128)(2,1)}, f32[16,128]{1,0:T(8,128)}) custom-call(bf16[4,512,2048]{2,1,0:T(8,128)(2,1)} %bitcast.199, f32[16,16,128]{2,1,0:T(8,128)} %shard_map.292.v_ref), custom_call_target="tpu_custom_call" | custom-call | tf_op jit(solution)/shard_map/pallas_call | solution.py:660
  (414 shorter events, 424.5 us)
Async XLA Ops:
  7.3 519.5 %all-gather.5.cloned.1.call-start = ((), (), s32[]{:S(2)}) async-start(), calls=%async_computation.10 | async-start | bytes 17825792 | tf_op jit(solution)/shard_map/all_gather | solution.py:1244
  229.4 466.8 %all-gather.3.cloned.1.call-start = ((), (), s32[]{:S(2)}) async-start(), calls=%async_computation.9 | async-start | bytes 17825792 | tf_op jit(solution)/shard_map/all_gather | solution.py:1258
  258.7 32.6 %collective-permute-start.2 = (bf16[2,50,1024]{2,1,0:T(8,128)(2,1)S(1)}, bf16[2,50,1024]{2,1,0:T(8,128)(2,1)S(1)}, u32[]{:S(2)}, u32[]{:S(2)}) collective-permute-start(bf16[2,50,1024]{2,1,0:T(8,128)(2,1)S(1)} %pad_maximum_fusion.5), channel_id=1, source_target_pairs={{0,4},{2,6},{1,5},{3,7},{8,12},{10,14},{9,13},{11,15},{16,20},{18,... | collective-permute-start | bytes 614408 | tf_op jit(solution)/shard_map/ppermute | solution.py:1134
  260.0 31.3 %collective-permute-start.1 = (bf16[2,50,1024]{2,1,0:T(8,128)(2,1)S(1)}, bf16[2,50,1024]{2,1,0:T(8,128)(2,1)S(1)}, u32[]{:S(2)}, u32[]{:S(2)}) collective-permute-start(bf16[2,50,1024]{2,1,0:T(8,128)(2,1)S(1)} %pad_maximum_fusion.5), channel_id=1, source_target_pairs={{0,2},{2,4},{4,6},{1,3},{3,5},{5,7},{8,10},{10,12},{12,14},{9,11},... | collective-permute-start | bytes 614408 | tf_op jit(solution)/shard_map/ppermute | solution.py:1134
  285.2 104.0 %collective-permute-start.4 = (bf16[1,512,1024]{2,1,0:T(8,128)(2,1)}, bf16[1,512,1024]{2,1,0:T(8,128)(2,1)}, u32[]{:S(2)}, u32[]{:S(2)}) collective-permute-start(bf16[1,512,1024]{2,1,0:T(8,128)(2,1)} %get-tuple-element.156), channel_id=1, source_target_pairs={{0,6},{2,0},{4,2},{6,4},{1,7},{3,1},{5,3},{7,5},{8,14},{10,8},{12,... | collective-permute-start | bytes 3145736 | tf_op jit(solution)/shard_map/ppermute | solution.py:1116
  285.2 117.7 %collective-permute-start.3 = (bf16[1,512,1024]{2,1,0:T(8,128)(2,1)}, bf16[1,512,1024]{2,1,0:T(8,128)(2,1)S(1)}, u32[]{:S(2)}, u32[]{:S(2)}) collective-permute-start(bf16[1,512,1024]{2,1,0:T(8,128)(2,1)} %get-tuple-element.157), channel_id=1, source_target_pairs={{0,4},{2,6},{4,0},{6,2},{1,5},{3,7},{5,1},{7,3},{8,12},{10,14},{12... | collective-permute-start | bytes 3145736 | tf_op jit(solution)/shard_map/ppermute | solution.py:1116
  285.2 118.6 %collective-permute-start = (bf16[1,512,1024]{2,1,0:T(8,128)(2,1)}, bf16[1,512,1024]{2,1,0:T(8,128)(2,1)S(1)}, u32[]{:S(2)}, u32[]{:S(2)}) collective-permute-start(bf16[1,512,1024]{2,1,0:T(8,128)(2,1)} %get-tuple-element.158), channel_id=1, source_target_pairs={{0,2},{2,4},{4,6},{6,0},{1,3},{3,5},{5,7},{7,1},{8,10},{10,12},{12... | collective-permute-start | bytes 3145736 | tf_op jit(solution)/shard_map/ppermute | solution.py:1116
  289.5 561.8 %reduce-scatter.10.cloned.1.call-start = ((), (), s32[]{:S(2)}) async-start(), calls=%async_computation.11 | async-start | bytes 20971520 | tf_op jit(solution)/shard_map/reduce_scatter | solution.py:1272
  459.7 33.6 %collective-permute-start.6 = (bf16[2048,2048]{1,0:T(8,128)(2,1)}, bf16[2048,2048]{1,0:T(8,128)(2,1)}, u32[]{:S(2)}, u32[]{:S(2)}) collective-permute-start(bf16[2048,2048]{1,0:T(8,128)(2,1)} %shard_map.266.refs_1_), channel_id=1, source_target_pairs={{0,1},{1,0},{2,3},{3,2},{4,5},{5,4},{6,7},{7,6},{8,9},{9,8},{10,11... | collective-permute-start | bytes 25165832 | tf_op jit(solution)/shard_map/ppermute | solution.py:1102
  464.2 15.0 collective-permute-start.5
  624.9 384.2 %reduce-scatter.12.cloned.1.call-start = ((), (), s32[]{:S(2)}) async-start(), calls=%async_computation.12 | async-start | bytes 20971520 | tf_op jit(solution)/shard_map/reduce_scatter | solution.py:1272
  827.5 13.5 collective-permute-start.7
  851.4 243.3 %reduce-scatter.14.cloned.1.call-start = ((), (), s32[]{:S(2)}) async-start(), calls=%async_computation.13 | async-start | bytes 5242880 | tf_op jit(solution)/shard_map/reduce_scatter | solution.py:1275
  1009.1 13.5 collective-permute-start.8
  1009.2 148.9 %reduce-scatter.16.cloned.1.call-start = ((), (), s32[]{:S(2)}) async-start(), calls=%async_computation.14 | async-start | bytes 5242880 | tf_op jit(solution)/shard_map/reduce_scatter | solution.py:1272
  1094.7 215.4 %reduce-scatter.20.cloned.1.call-start = ((), (), s32[]{:S(2)}) async-start(), calls=%async_computation.16 | async-start | bytes 5242880 | tf_op jit(solution)/shard_map/reduce_scatter | solution.py:1275
  1097.6 17.3 %collective-permute-start.10 = (bf16[2,50,512]{2,1,0:T(8,128)(2,1)S(1)}, bf16[2,50,512]{2,1,0:T(8,128)(2,1)S(1)}, u32[]{:S(2)}, u32[]{:S(2)}) collective-permute-start(bf16[2,50,512]{2,1,0:T(8,128)(2,1)S(1)} %get-tuple-element.165), channel_id=1, source_target_pairs={{4,0},{6,2},{5,1},{7,3},{12,8},{14,10},{13,9},{15,11},{20,16},{22,... | collective-permute-start | bytes 307208 | tf_op jit(solution)/shard_map/ppermute | solution.py:1134
  1158.2 152.0 %reduce-scatter.18.cloned.1.call-start = ((), (), s32[]{:S(2)}) async-start(), calls=%async_computation.15 | async-start | bytes 7864320 | tf_op jit(solution)/shard_map/reduce_scatter | solution.py:1272
  1158.9 233.5 %reduce-scatter.22.cloned.1.call-start = ((), (), s32[]{:S(2)}) async-start(), calls=%async_computation.17 | async-start | bytes 7864320 | tf_op jit(solution)/shard_map/reduce_scatter | solution.py:1272
  1242.0 22.7 %collective-permute-start.11 = (bf16[2,50,512]{2,1,0:T(8,128)(2,1)S(1)}, bf16[2,50,512]{2,1,0:T(8,128)(2,1)S(1)}, u32[]{:S(2)}, u32[]{:S(2)}) collective-permute-start(bf16[2,50,512]{2,1,0:T(8,128)(2,1)S(1)} %get-tuple-element.162), channel_id=1, source_target_pairs={{2,0},{4,2},{6,4},{3,1},{5,3},{7,5},{10,8},{12,10},{14,12},{11,9},... | collective-permute-start | bytes 307208 | tf_op jit(solution)/shard_map/ppermute | solution.py:1134
  1243.3 27.4 %collective-permute-start.12 = (bf16[2,50,512]{2,1,0:T(8,128)(2,1)S(1)}, bf16[2,50,512]{2,1,0:T(8,128)(2,1)S(1)}, u32[]{:S(2)}, u32[]{:S(2)}) collective-permute-start(bf16[2,50,512]{2,1,0:T(8,128)(2,1)S(1)} %get-tuple-element.163), channel_id=1, source_target_pairs={{4,0},{6,2},{5,1},{7,3},{12,8},{14,10},{13,9},{15,11},{20,16},{22,... | collective-permute-start | bytes 307208 | tf_op jit(solution)/shard_map/ppermute | solution.py:1134
  1310.3 118.2 %reduce-scatter.26.cloned.1.call-start = ((), (), s32[]{:S(2)}) async-start(), calls=%async_computation.19 | async-start | bytes 1310720 | tf_op jit(solution)/shard_map/reduce_scatter | solution.py:1275
  1376.9 15.5 collective-permute-start.13
  1379.8 199.8 %reduce-scatter.24.cloned.1.call-start = ((), (), s32[]{:S(2)}) async-start(), calls=%async_computation.18 | async-start | bytes 3932160 | tf_op jit(solution)/shard_map/reduce_scatter | solution.py:1275
  (91 other events, 5365.6 us)
Sparse Core Ops, SparseCore 0:
  229.5 259.2 all-gather.4
  491.6 204.6 all-gather.2
  699.3 152.0 reduce-scatter.9
  854.3 153.8 reduce-scatter.11
  1010.3 84.3 reduce-scatter.13
  1097.8 55.8 reduce-scatter.15
  1158.3 76.1 reduce-scatter.19
  1237.8 70.7 reduce-scatter.17
  1311.8 72.5 reduce-scatter.21
  1386.7 27.1 reduce-scatter.25
  1416.7 114.6 reduce-scatter.23

commit v4 on v3

--- a/solution.py
+++ b/solution.py
@@ -671,6 +671,47 @@
         + [dma((2,))],
         compiler_params=pltpu.CompilerParams(collective_id=1, has_side_effects=True),
     )(tokens, vectors)
+
+
+def norm_back_kernel(field_ref, own_ref, other_ref, rest_ref, gain_ref, *outs):
+    field = field_ref[...].astype(F32)
+    width = field.shape[1]
+    grad = own_ref[...].astype(F32) + other_ref[...].astype(F32)
+    centered = field - jnp.sum(field, axis=1, keepdims=True) * (1.0 / width)
+    variance = jnp.sum(centered * centered, axis=1, keepdims=True) * (1.0 / width)
+    scale = lax.rsqrt(variance + norm_eps)
+    unit = centered * scale
+    scaled = grad * gain_ref[...]
+    mean_one = jnp.sum(scaled, axis=1, keepdims=True) * (1.0 / width)
+    mean_two = jnp.sum(scaled * unit, axis=1, keepdims=True) * (1.0 / width)
+    total = rest_ref[...].astype(F32) + scale * (scaled - mean_one - unit * mean_two)
+    sums_ref = outs[-1]
+    for ref in outs[:-1]:
+        ref[...] = total.astype(ref.dtype)
+
+    @pl.when(pl.program_id(0) == 0)
+    def _():
+        sums_ref[...] = jnp.zeros_like(sums_ref)
+
+    for n, item in enumerate((grad * unit, grad, total)):
+        sums_ref[pl.ds(n, 1)] += jnp.sum(item, axis=0, keepdims=True)
+
+
+def norm_back(field, own, other, rest, gain, kinds):
+    tokens, width = field.shape
+    rows = min(256, tokens)
+    block = pl.BlockSpec((rows, width), lambda i: (i, 0))
+    flat = lambda n: pl.BlockSpec((n, width), lambda i: (0, 0))
+    return pl.pallas_call(
+        norm_back_kernel,
+        grid=(tokens // rows,),
+        in_specs=[block] * 4 + [flat(1)],
+        out_specs=[block] * len(kinds) + [flat(8)],
+        out_shape=[jax.ShapeDtypeStruct(field.shape, kind) for kind in kinds]
+        + [jax.ShapeDtypeStruct((8, width), F32)],
+        cost_estimate=told(15.0),
+        compiler_params=pltpu.CompilerParams(vmem_limit_bytes=48 * 2**20),
+    )(field, own, other, rest, gain.reshape(1, width))
 
 
 class Move:
@@ -1095,6 +1136,23 @@
     )()
 
 
+def copied(blocks):
+    block = pl.BlockSpec((1,) + blocks.shape[1:], lambda i: (i, 0, 0))
+
+    def kernel(source, target):
+        target[...] = source[...]
+
+    return pl.pallas_call(
+        kernel,
+        grid=blocks.shape[:1],
+        in_specs=[block],
+        out_specs=block,
+        out_shape=jax.ShapeDtypeStruct(blocks.shape, blocks.dtype),
+        cost_estimate=told(6.0),
+        compiler_params=pltpu.CompilerParams(vmem_limit_bytes=24 * 2**20),
+    )(blocks)
+
+
 BOTH = ("rows", "seq")
 
 
@@ -1102,19 +1160,19 @@
     return lax.ppermute(block, "fsdp", ((0, 1), (1, 0)))
 
 
-def along_line(field, hold=()):
+def along_line(field, begin, hold):
     count = lax.axis_size("seq")
     me = lax.axis_index("seq")
     core = lax.axis_index("fsdp")
     half = field.shape[2] // 2
-    mine = lax.dynamic_slice_in_dim(field, core * half, half, 2)
+    mine = gate(lax.dynamic_slice_in_dim(field, core * half, half, 2), begin)
     got = jnp.zeros_like(mine)
     own = lax.dynamic_slice_in_dim(mine, me, 1, 0)
     got = lax.dynamic_update_slice_in_dim(got, own, me, 0)
     for away in range(1, count):
         block = lax.dynamic_slice_in_dim(mine, lax.rem(me + away, count), 1, 0)
         moved = lax.ppermute(block, "seq", [(n, (n + away) % count) for n in range(count)])
-        moved = gate(moved, *hold) if hold else moved
+        moved = gate(moved, *hold)
         got = lax.dynamic_update_slice_in_dim(got, moved, lax.rem(me + count - away, count), 0)
     return got
 
@@ -1144,16 +1202,7 @@
     centered = field - row_mean
     variance = jnp.mean(centered * centered, axis=-1, keepdims=True)
     scale = lax.rsqrt(variance + norm_eps)
-    return (centered * scale * gain_vec + shift_vec).astype(BF), row_mean, scale
-
-
-def norm_backward(field, row_mean, scale, gain_vec, grad):
-    unit = (field - row_mean) * scale
-    scaled = grad * gain_vec
-    mean_one = jnp.mean(scaled, axis=-1, keepdims=True)
-    mean_two = jnp.mean(scaled * unit, axis=-1, keepdims=True)
-    d_field = scale * (scaled - mean_one - unit * mean_two)
-    return d_field, jnp.sum(grad * unit, axis=0), jnp.sum(grad, axis=0)
+    return (centered * scale * gain_vec + shift_vec).astype(BF)
 
 
 def mm(a, b):
@@ -1233,7 +1282,7 @@
     doc_row = my_docs.reshape(1, seg_len)
 
     tokens_f = tokens.astype(F32)
-    normed_one, mean_one, scale_one = norm_forward(tokens_f, gain_a, shift_a)
+    normed_one = norm_forward(tokens_f, gain_a, shift_a)
     query = product(
         normed_one, attn_full, "nn", functools.partial(finish_bias, HEAD**-0.5), (bias_pair[:1],), planes=(0,)
     )
@@ -1241,7 +1290,7 @@
     values = product(
         normed_one, attn_full, "nn", functools.partial(finish_bias, 1.0), (bias_pair[1:],), planes=(2,)
     )
-    up_full = lax.all_gather(gate(w_up, normed_one), BOTH, axis=0, tiled=True)
+    up_full = lax.all_gather(gate(w_up, tokens), BOTH, axis=0, tiled=True)
     tail = jnp.stack((keys[seg_len - SUMM :], values[seg_len - SUMM :]))
     lent = jnp.concatenate((shift_by(tail, 1), shift_by(tail, 2)), axis=1)
     lent = jnp.pad(lent, ((0, 0), (0, 128 - 2 * SUMM), (0, 0)))
@@ -1258,10 +1307,10 @@
     down_full = lax.all_gather(gate(w_down.T, values), BOTH, axis=0, tiled=True)
     mixed, log_sum = attended
     attended = product(mixed, attn_full, "nt", planes=(3,))
-    grad_out = along_line(gate(cotangent[0], query), (done[2],))
+    grad_out = along_line(cotangent[0], query, (done[2],))
     grad_out = between_cores(grad_out, (attended,)).reshape(seg_len, model)
     hidden = tokens_f + both_halves(attended) + bias_o
-    normed_two, mean_two, scale_two = norm_forward(hidden, gain_b, shift_b)
+    normed_two = norm_forward(hidden, gain_b, shift_b)
     up_proj = mm(normed_two, up_full) + bias_u
     bell = jnp.exp(-0.5 * up_proj * up_proj)
     area = 0.5 * (1.0 + lax.erf(up_proj * (0.5**0.5)))
@@ -1279,16 +1328,17 @@
     slope = gate(slope, down_sum)
     d_up = (mm(grad_out, down_full) * slope.astype(F32)).astype(BF)
     up_sum = product(normed_two, d_up, "tn")
+    def column_sum(field):
+        return jnp.sum(field.astype(F32), axis=0)
+
     d_norm_part = product(d_up, up_full, "nt", deps=(up_sum,))
-    d_norm_other = other_core(d_norm_part)
+    sum_grad_out = column_sum(grad_out)
+    d_norm_other = gate(other_core(d_norm_part), sum_grad_out)
     up_turn = gate(up_sum, down_rows, d_norm_other)
     up_rows = over_rows(up_turn)
-    d_norm_two = d_norm_part.astype(F32) + d_norm_other.astype(F32)
-    d_hidden_ln, grad_gain_two, grad_shift_two = norm_backward(
-        hidden, mean_two, scale_two, gain_b, d_norm_two
-    )
-    d_hidden = grad_out.astype(F32) + d_hidden_ln
-    d_hidden_low = d_hidden.astype(BF)
+    d_hidden, d_hidden_low, sums_two = norm_back(
+        hidden, d_norm_part, d_norm_other, grad_out, gain_b, (F32, BF)
+    )
     d_mixed = product(d_hidden_low, attn_full, "nn", deps=(up_turn,), planes=(3,))
     out_sum = product(d_hidden_low, mixed, "tn", deps=(d_mixed,))
 
@@ -1341,35 +1391,29 @@
         d_qkv, attn_full, "nt", deps=(second_turn,), blocks=(1024, 1024, half // 2), planes=(0, 1, 2),
         move=(out_tokens, out_moved, tuple(range(2, segs - 1)), 4),
     )
-    out_states = out_moved[None]
-    d_norm_other = other_core(d_norm_part)
-    d_norm_one = d_norm_part.astype(F32) + d_norm_other.astype(F32)
-    out_seq = over_seq(gate(out_rows, second_turn))
+    out_states = copied(out_moved)[None]
+    kind_sum = column_sum(d_qkv).reshape(2, 3, half // 2)
+    d_norm_other = gate(other_core(d_norm_part), kind_sum, out_states)
+    grad_tokens, sums_one = norm_back(
+        tokens, d_norm_part, d_norm_other, d_hidden, gain_a, (BF,)
+    )
     grad_w_down = grad_w_down.T
-    d_tokens_ln, grad_gain_one, grad_shift_one = norm_backward(
-        tokens_f, mean_one, scale_one, gain_a, d_norm_one
-    )
-    grad_tokens = (d_hidden + d_tokens_ln).astype(BF)
-    qkv_rows = gate(jnp.concatenate((first_rows, gate(second_rows, d_norm_other)), axis=1), d_norm_other)
-    grad_w_qkv = over_seq(qkv_rows).astype(F32)
-    grad_w_out = gate(out_seq, grad_tokens).astype(F32)
+    qkv_rows = jnp.concatenate((out_rows, first_rows, gate(second_rows, d_norm_other)), axis=1)
+    attn_seq = over_seq(qkv_rows).astype(F32)
+    grad_w_out, grad_w_qkv = attn_seq[:, :half].T, attn_seq[:, half:]
     grad_w_qkv = jnp.transpose(grad_w_qkv.reshape(-1, 2, 3, half // 2), (2, 0, 1, 3)).reshape(3, -1, half)
-    grad_w_out = grad_w_out.T
-    def column_sum(field):
-        return jnp.sum(field.astype(F32), axis=0)
-
-    kind_sum = column_sum(d_qkv).reshape(2, 3, half // 2)
+
     sums = (
         jnp.moveaxis(
             jnp.stack((kind_sum[:, 0], kind_sum[:, 2])).reshape(2, half // HEAD, shards, -1), 2, 0
         ),
-        column_sum(d_hidden),
+        sums_two[2],
         jnp.moveaxis(column_sum(d_up).reshape(hidden_units // HEAD, shards, -1), 1, 0),
-        column_sum(grad_out),
-        grad_gain_one,
-        grad_shift_one,
-        grad_gain_two,
-        grad_shift_two,
+        sum_grad_out,
+        sums_one[0],
+        sums_one[1],
+        sums_two[0],
+        sums_two[1],
     )
     vectors = jnp.concatenate([item.reshape(shards, -1) for item in sums], axis=1)
     vectors = jnp.pad(vectors, ((0, 0), (0, room - vectors.shape[1]))).reshape(shards, -1, 128)

time: 1620 us -> 1590 us (0.981)
  Pallas kernels: 985 us -> 1080 us
  other arithmetic: 173 us -> 115 us
  waiting for transfers between devices: 184 us -> 128 us
    pallas_call x0 -> x3, Pallas kernels: none -> 52.7 us  [the longest x2 49.2 us: norm_back(): pl.pallas_call(norm_back_kernel, grid=(tokens // rows,), in_specs=[block]...]
    reduce_sum x2 -> x0, other arithmetic: 28.3 us -> none  [norm_backward(): return (d_field, jnp.sum(grad * unit, axis=0), jnp.sum(grad, axis=0))]
    ppermute x6, waiting for transfers between devices: 37.3 us -> 11 us  [shift_by(): return lax.ppermute(field, 'seq', perm)]
    convert_element_type x4, other arithmetic: 38.7 us -> 19.5 us  [the longest x2 18.6 us: norm_forward(): return (centered * scale * gain_vec + shift_vec).astype(BF)]
    all_gather x1, waiting for transfers between devices: 71.3 us -> 52 us  [layer_by_segment(): down_full = lax.all_gather(gate(w_down.T, values), BOTH, axis=0, tiled=True)]
    reduce_sum x3 -> x2, other arithmetic: 25 us -> 8.52 us  [column_sum(): return jnp.sum(field.astype(F32), axis=0)]
    unnamed x222 -> x200, local copies, waits for them, and re-layouts: 104 us -> 90 us
  transfers between devices with their start and end apart: 25 -> 24, of which waited for: 11 -> 10; matrix products, arithmetic and copies ran while one was open for 19% -> 17% of each run, Pallas kernels for 49% -> 56%
where the time goes in v4:
time: 1590 us
  Pallas kernels  1080 us (68%)
  local copies, waits for them, and re-layouts  132 us (8%)
  waiting for transfers between devices  128 us (8%)
  other arithmetic  115 us (7%)
  matrix products  102 us (6%)
  between operations  15.9 us (1%)
    pallas_call x13, Pallas kernels, product(): pl.pallas_call(functools.partial(product_kernel, mode, finish, len(rows),...  378 us
    pallas_call x1, Pallas kernels, opening(): pl.pallas_call(opening_kernel, in_specs=[anywhere] * 3, out_specs=[anywhe...  193 us
    pallas_call x3, Pallas kernels, attn_bwd(): pl.pallas_call(functools.partial(bwd_kernel, tile), grid_spec=pltpu.Prefe...  171 us
    pallas_call x1, Pallas kernels, closing(): pl.pallas_call(closing_kernel, in_specs=[anywhere] * 2, out_specs=[anywhe...  151 us
    pallas_call x4, Pallas kernels, attn_fwd(): pl.pallas_call(functools.partial(fwd_kernel, tile), grid_spec=pltpu.Prefe...  133 us
    dot_general x2, matrix products, dot_nn(): lax.dot_general(a, b, (((1,), (0,)), ((), ())), preferred_element_type=F32)  102 us
    unnamed x200, local copies, waits for them, and re-layouts  90 us
    all_gather x1, waiting for transfers between devices, layer_by_segment(): down_full = lax.all_gather(gate(w_down.T, values), BOTH, axis=0, tiled=True)  52 us
  transfers between devices with their start and end apart: 24, of which 10 were waited for; matrix products, arithmetic and copies ran while one was open for 17% of the time, Pallas kernels for 56%

profile of v4, /device:TPU:0, one launch (start us, length us, event | category | flops | bytes accessed | tf_op | source)
XLA Modules:
  0.0 1586.2 jit_solution(8794433687281755609)
XLA Ops:
  20.5 192.6 %shard_map.254 = (bf16[4,2048,1024]{2,1,0:T(8,128)(2,1)}, bf16[4,512,2048]{2,1,0:T(8,128)(2,1)}, bf16[16,16,128]{2,1,0:T(8,128)(2,1)}) custom-call(bf16[4,128,1024]{2,1,0:T(8,128)(2,1)} %pad_maximum_fusion.4.w_ref, bf16[4,512,2048]{2,1,0:T(8,128)(2,1)} %bitcast.170, bf16[16,128]{1,0:T(8,128)(2,1)} %pad_bitcast_fusion.1.v_ref), custom_call_target="tpu_custom_call" | custom-call | tf_op jit(solution)/shard_map/pallas_call | solution.py:561
  246.8 14.0 shard_map.257.v_ref.refs_1_
  306.5 33.1 %shard_map.258 = (bf16[2048,1024]{1,0:T(8,128)(2,1)S(1)}, f32[8,2,2048]{2,1,0:T(2,128)S(1)}) custom-call(s32[16]{0:T(128)S(1)} %select_n.80.flags, bf16[2048,1024]{1,0:T(8,128)(2,1)S(1)} %copy-done.11, bf16[2048,1024]{1,0:T(8,128)(2,1)S(1)} %copy-done.46, bf16[2048,1024]{1,0:T(8,128)(2,1)} %copy-done.9, bf16[128,1024]{1,0:T(8,128)(2,1)S(1)} %get-tuple-element.161.sk_ref, ...), custom_call_target="tpu_custom_call" | custom-call | flops 33600000000 | bytes 1000 | tf_op jit(solution)/shard_map/pallas_call | solution.py:943
  339.6 33.1 %shard_map.259 = (bf16[2048,1024]{1,0:T(8,128)(2,1)S(1)}, f32[8,2,2048]{2,1,0:T(2,128)S(1)}) custom-call(s32[16]{0:T(128)S(1)} %select_n.80.flags, bf16[2048,1024]{1,0:T(8,128)(2,1)S(1)} %copy-done.11, bf16[2048,1024]{1,0:T(8,128)(2,1)S(1)} %copy-done.46, bf16[2048,1024]{1,0:T(8,128)(2,1)} %copy-done.9, ...), custom_call_target="tpu_custom_call", output_to_operand_aliasing={{0}: (9, {}), {1}: (10, {})} | custom-call | flops 33600000000 | bytes 1000 | tf_op jit(solution)/shard_map/pallas_call | solution.py:943
  372.7 33.1 %shard_map.260 = (bf16[2048,1024]{1,0:T(8,128)(2,1)S(1)}, f32[8,2,2048]{2,1,0:T(2,128)S(1)}) custom-call(s32[16]{0:T(128)S(1)} %select_n.80.flags, bf16[2048,1024]{1,0:T(8,128)(2,1)S(1)} %copy-done.11, bf16[2048,1024]{1,0:T(8,128)(2,1)S(1)} %copy-done.46, bf16[2048,1024]{1,0:T(8,128)(2,1)} %copy-done.9, ...), custom_call_target="tpu_custom_call", output_to_operand_aliasing={{0}: (9, {}), {1}: (10, {})} | custom-call | flops 33600000000 | bytes 1000 | tf_op jit(solution)/shard_map/pallas_call | solution.py:943
  417.9 33.2 %shard_map.261 = (bf16[2048,1024]{1,0:T(8,128)(2,1)S(1)}, f32[8,2,2048]{2,1,0:T(2,128)S(1)}) custom-call(s32[16]{0:T(128)S(1)} %select_n.80.flags, bf16[2048,1024]{1,0:T(8,128)(2,1)S(1)} %copy-done.12, bf16[2048,1024]{1,0:T(8,128)(2,1)S(1)} %copy-done.47, bf16[2048,1024]{1,0:T(8,128)(2,1)} %copy-done.9, ...), custom_call_target="tpu_custom_call", output_to_operand_aliasing={{0}: (9, {}), {1}: (10, {})} | custom-call | flops 33600000000 | bytes 1000 | tf_op jit(solution)/shard_map/pallas_call | solution.py:943
  501.5 15.4 fusion.25
  534.6 57.0 %multiply_convert_fusion.1 = (bf16[2048,4096]{1,0:T(8,128)(2,1)}, bf16[2048,4096]{1,0:T(8,128)(2,1)}) fusion(f32[4096]{0:T(1024)S(1)} %reshape.255, bf16[2048,2048]{1,0:T(8,128)(2,1)} %add_convert_fusion.1.refs_0_, bf16[2048,4096]{1,0:T(8,128)(2,1)} %all-gather.5.cloned.1.call-done.refs_1_), kind=kOutput, calls=%fused_computation.8 | convolution fusion | flops 34460401664 | bytes 58736640 | tf_op jit(solution)/shard_map/dot_general | solution.py:876
  591.6 41.9 %shard_map.270.refs_1_ = bf16[2048,4096]{1,0:T(8,128)(2,1)} custom-call(bf16[2048,2048]{1,0:T(8,128)(2,1)} %bitcast.171, bf16[2048,4096]{1,0:T(8,128)(2,1)} %get-tuple-element.152.refs_1_.refs_0_), custom_call_target="tpu_custom_call" | custom-call | flops 42949672960 | bytes 1000 | tf_op jit(solution)/shard_map/pallas_call | solution.py:860
  633.6 52.0 %all-gather.3.cloned.1.call-done.refs_1_ = bf16[2048,4096]{1,0:T(8,128)(2,1)} async-done(((bf16[128,4096]{1,0:T(8,128)(2,1)}), bf16[2048,4096]{1,0:T(8,128)(2,1)}) %all-gather.3.cloned.1.call-update) | async-done | bytes 16777232 | tf_op jit(solution)/shard_map/all_gather | solution.py:1307
  685.6 45.3 %convert_reduce_fusion = (f32[4096]{0:T(1024)}, bf16[2048,4096]{1,0:T(8,128)(2,1)}) fusion(bf16[2048,4096]{1,0:T(8,128)(2,1)} %shard_map.271, bf16[2048,2048]{1,0:T(8,128)(2,1)} %bitcast.172, bf16[2048,4096]{1,0:T(8,128)(2,1)} %all-gather.3.cloned.1.call-done.refs_1_), kind=kOutput, calls=%fused_computation.6 | convolution fusion | flops 34401677312 | bytes 58736640 | tf_op jit(solution)/shard_map/dot_general | solution.py:876
  731.0 41.5 %shard_map.272.refs_2_.refs_0_ = bf16[2048,4096]{1,0:T(8,128)(2,1)} custom-call(bf16[2048,2048]{1,0:T(8,128)(2,1)} %add_convert_fusion.1.refs_0_, bf16[2048,4096]{1,0:T(8,128)(2,1)} %get-tuple-element.198.refs_1_.refs_0_), custom_call_target="tpu_custom_call" | custom-call | flops 42949672960 | bytes 1000 | tf_op jit(solution)/shard_map/pallas_call | solution.py:860
  772.4 44.4 %shard_map.273.own_ref = bf16[2048,2048]{1,0:T(8,128)(2,1)} custom-call(bf16[2048,4096]{1,0:T(8,128)(2,1)} %get-tuple-element.198.refs_1_.refs_0_, bf16[2048,4096]{1,0:T(8,128)(2,1)} %all-gather.5.cloned.1.call-done.refs_1_, bf16[2048,4096]{1,0:T(8,128)(2,1)} %shard_map.272.refs_2_.refs_0_), custom_call_target="tpu_custom_call" | custom-call | flops 42949672960 | bytes 1000 | tf_op jit(solution)/shard_map/pallas_call | solution.py:860
  830.3 13.8 reduce-scatter.9.cloned.1.call-done.refs_1_.refs_0_
  844.2 27.3 %shard_map.275 = (f32[2048,2048]{1,0:T(8,128)}, bf16[2048,2048]{1,0:T(8,128)(2,1)}, f32[8,2048]{1,0:T(8,128)S(1)}) custom-call(f32[2048,2048]{1,0:T(8,128)} %get-tuple-element.151.field_ref, bf16[2048,2048]{1,0:T(8,128)(2,1)} %shard_map.273.own_ref, bf16[2048,2048]{1,0:T(8,128)(2,1)} %shard_map.274.other_ref.refs_2_, bf16[2048,2048]{1,0:T(8,128)(2,1)} %bitcast.173, ...), custom_call_target="tpu_custom_call" | custom-call | flops 15000000512 | bytes 1000 | tf_op jit(solution)/shard_map/pallas_call | solution.py:705
  902.2 43.5 %shard_map.279 = (bf16[2048,256]{1,0:T(8,128)(2,1)S(1)}, bf16[2048,256]{1,0:T(8,128)(2,1)S(1)}, bf16[2048,256]{1,0:T(8,128)(2,1)S(1)}, bf16[128,256]{1,0:T(8,128)(2,1)S(1)}, bf16[128,256]{1,0:T(8,128)(2,1)S(1)}) custom-call(s32[16]{0:T(128)S(1)} %copy-done.51, bf16[2048,1024]{1,0:T(8,128)(2,1)S(1)} %copy-done.13, bf16[2048,1024]{1,0:T(8,128)(2,1)S(1)} %copy-done.48, ...), custom_call_target="tpu_custom_call" | custom-call | flops 44000002048 | bytes 1000 | tf_op jit(solution)/shard_map/pallas_call | solution.py:1065
  946.9 44.2 %shard_map.280.refs_2_ = bf16[2048,2048]{1,0:T(8,128)(2,1)} custom-call(bf16[2048,4096]{1,0:T(8,128)(2,1)} %get-tuple-element.152.refs_1_.refs_0_, bf16[2048,4096]{1,0:T(8,128)(2,1)} %all-gather.3.cloned.1.call-done.refs_1_, bf16[2048,256]{1,0:T(8,128)(2,1)S(1)} %get-tuple-element.65.refs_2_), custom_call_target="tpu_custom_call" | custom-call | flops 42949672960 | bytes 1000 | tf_op jit(solution)/shard_map/pallas_call | solution.py:860
  1023.1 43.2 %shard_map.283 = (bf16[2048,256]{1,0:T(8,128)(2,1)S(1)}, bf16[2048,256]{1,0:T(8,128)(2,1)S(1)}, bf16[2048,256]{1,0:T(8,128)(2,1)S(1)}, bf16[128,256]{1,0:T(8,128)(2,1)S(1)}, bf16[128,256]{1,0:T(8,128)(2,1)S(1)}) custom-call(s32[16]{0:T(128)S(1)} %copy-done.52, bf16[2048,1024]{1,0:T(8,128)(2,1)S(1)} %copy-done.14, bf16[2048,1024]{1,0:T(8,128)(2,1)S(1)} %copy-done.49, ...), custom_call_target="tpu_custom_call" | custom-call | flops 44000002048 | bytes 1000 | tf_op jit(solution)/shard_map/pallas_call | solution.py:1065
  1104.0 33.3 %shard_map.285 = (bf16[2048,1536]{1,0:T(8,128)(2,1)}, bf16[4,512,2048]{2,1,0:T(8,128)(2,1)}) custom-call(bf16[2048,2048]{1,0:T(8,128)(2,1)} %fusion.8.refs_0_, bf16[2048,1536]{1,0:T(8,128)(2,1)} %pad_maximum_fusion.1.refs_1_, bf16[4,512,2048]{2,1,0:T(8,128)(2,1)} %bitcast.166, ...), custom_call_target="tpu_custom_call", output_to_operand_aliasing={{1}: (3, {})} | custom-call | flops 16106127360 | bytes 1000 | tf_op jit(solution)/shard_map/pallas_call | solution.py:860
  1142.7 84.6 %shard_map.288 = (bf16[2048,512]{1,0:T(8,128)(2,1)S(1)}, bf16[2048,512]{1,0:T(8,128)(2,1)S(1)}, bf16[2048,512]{1,0:T(8,128)(2,1)S(1)}, bf16[128,512]{1,0:T(8,128)(2,1)S(1)}, bf16[128,512]{1,0:T(8,128)(2,1)S(1)}) custom-call(s32[16]{0:T(128)S(1)} %copy-done.53, bf16[2048,1024]{1,0:T(8,128)(2,1)S(1)} %copy-done.15, bf16[2048,1024]{1,0:T(8,128)(2,1)} %copy-done.45, ...), custom_call_target="tpu_custom_call" | custom-call | flops 88000004096 | bytes 1000 | tf_op jit(solution)/shard_map/pallas_call | solution.py:1065
  1245.9 40.5 %shard_map.289 = (bf16[2048,1536]{1,0:T(8,128)(2,1)}, bf16[4,512,2048]{2,1,0:T(8,128)(2,1)}) custom-call(bf16[2048,2048]{1,0:T(8,128)(2,1)} %fusion.8.refs_0_, bf16[2048,1536]{1,0:T(8,128)(2,1)} %pad_maximum_fusion.2.refs_1_, bf16[4,512,2048]{2,1,0:T(8,128)(2,1)} %bitcast.167, ...), custom_call_target="tpu_custom_call", output_to_operand_aliasing={{1}: (3, {})} | custom-call | flops 16106127360 | bytes 1000 | tf_op jit(solution)/shard_map/pallas_call | solution.py:860
  1300.5 55.0 %shard_map.291 = (bf16[2048,2048]{1,0:T(8,128)(2,1)}, bf16[4,512,2048]{2,1,0:T(8,128)(2,1)}) custom-call(bf16[2048,3072]{1,0:T(8,128)(2,1)} %constant_dynamic-update-slice_fusion.4.refs_0_, bf16[4,2048,1024]{2,1,0:T(8,128)(2,1)} %get-tuple-element.55.refs_1_, bf16[4,512,2048]{2,1,0:T(8,128)(2,1)} %bitcast.168, ...), custom_call_target="tpu_custom_call", output_to_operand_aliasing={{1}: (3, {})} | custom-call | flops 32212254720 | bytes 1000 | tf_op jit(solution)/shard_map/pallas_call | solution.py:860
  1383.1 21.9 %shard_map.294 = (bf16[2048,2048]{1,0:T(8,128)(2,1)}, f32[8,2048]{1,0:T(8,128)S(1)}) custom-call(bf16[2048,2048]{1,0:T(8,128)(2,1)} %bitcast.164, bf16[2048,2048]{1,0:T(8,128)(2,1)} %get-tuple-element.85.own_ref, bf16[2048,2048]{1,0:T(8,128)(2,1)} %shard_map.293.other_ref.refs_1_, f32[2048,2048]{1,0:T(8,128)} %get-tuple-element.86.rest_ref, ...), custom_call_target="tpu_custom_call" | custom-call | flops 15000000512 | bytes 1000 | tf_op jit(solution)/shard_map/pallas_call | solution.py:705
  1405.7 151.2 %shard_map.297 = (bf16[4,512,2048]{2,1,0:T(8,128)(2,1)}, f32[16,128]{1,0:T(8,128)}) custom-call(bf16[4,512,2048]{2,1,0:T(8,128)(2,1)} %bitcast.175, f32[16,16,128]{2,1,0:T(8,128)} %shard_map.296.v_ref), custom_call_target="tpu_custom_call" | custom-call | tf_op jit(solution)/shard_map/pallas_call | solution.py:660
  (387 shorter events, 375.3 us)
Async XLA Ops:
  7.2 527.4 %all-gather.5.cloned.1.call-start = ((), (), s32[]{:S(2)}) async-start(), calls=%async_computation.9 | async-start | bytes 17825792 | tf_op jit(solution)/shard_map/all_gather | solution.py:1293
  213.2 472.5 %all-gather.3.cloned.1.call-start = ((), (), s32[]{:S(2)}) async-start(), calls=%async_computation.8 | async-start | bytes 17825792 | tf_op jit(solution)/shard_map/all_gather | solution.py:1307
  262.9 37.9 %collective-permute-start = (bf16[2,50,1024]{2,1,0:T(8,128)(2,1)S(1)}, bf16[2,50,1024]{2,1,0:T(8,128)(2,1)S(1)}, u32[]{:S(2)}, u32[]{:S(2)}) collective-permute-start(bf16[2,50,1024]{2,1,0:T(8,128)(2,1)S(1)} %pad_maximum_fusion.5), channel_id=1, source_target_pairs={{0,2},{2,4},{4,6},{1,3},{3,5},{5,7},{8,10},{10,12},{12,14},{9,11},... | collective-permute-start | bytes 614408 | tf_op jit(solution)/shard_map/ppermute | solution.py:1192
  284.2 16.6 %collective-permute-start.1 = (bf16[2,50,1024]{2,1,0:T(8,128)(2,1)S(1)}, bf16[2,50,1024]{2,1,0:T(8,128)(2,1)}, u32[]{:S(2)}, u32[]{:S(2)}) collective-permute-start(bf16[2,50,1024]{2,1,0:T(8,128)(2,1)S(1)} %pad_maximum_fusion.5), channel_id=1, source_target_pairs={{0,4},{2,6},{1,5},{3,7},{8,12},{10,14},{9,13},{11,15},{16,20},{18,... | collective-permute-start | bytes 614408 | tf_op jit(solution)/shard_map/ppermute | solution.py:1192
  293.1 115.3 %collective-permute-start.3 = (bf16[1,512,1024]{2,1,0:T(8,128)(2,1)}, bf16[1,512,1024]{2,1,0:T(8,128)(2,1)}, u32[]{:S(2)}, u32[]{:S(2)}) collective-permute-start(bf16[1,512,1024]{2,1,0:T(8,128)(2,1)} %get-tuple-element.158), channel_id=1, source_target_pairs={{0,2},{2,4},{4,6},{6,0},{1,3},{3,5},{5,7},{7,1},{8,10},{10,12},{12... | collective-permute-start | bytes 3145736 | tf_op jit(solution)/shard_map/ppermute | solution.py:1174
  293.2 115.3 %collective-permute-start.4 = (bf16[1,512,1024]{2,1,0:T(8,128)(2,1)}, bf16[1,512,1024]{2,1,0:T(8,128)(2,1)S(1)}, u32[]{:S(2)}, u32[]{:S(2)}) collective-permute-start(bf16[1,512,1024]{2,1,0:T(8,128)(2,1)} %get-tuple-element.157), channel_id=1, source_target_pairs={{0,4},{2,6},{4,0},{6,2},{1,5},{3,7},{5,1},{7,3},{8,12},{10,14},{12... | collective-permute-start | bytes 3145736 | tf_op jit(solution)/shard_map/ppermute | solution.py:1174
  293.2 116.3 %collective-permute-start.5 = (bf16[1,512,1024]{2,1,0:T(8,128)(2,1)}, bf16[1,512,1024]{2,1,0:T(8,128)(2,1)S(1)}, u32[]{:S(2)}, u32[]{:S(2)}) collective-permute-start(bf16[1,512,1024]{2,1,0:T(8,128)(2,1)} %get-tuple-element.156), channel_id=1, source_target_pairs={{0,6},{2,0},{4,2},{6,4},{1,7},{3,1},{5,3},{7,5},{8,14},{10,8},{12,... | collective-permute-start | bytes 3145736 | tf_op jit(solution)/shard_map/ppermute | solution.py:1174
  299.3 544.9 %reduce-scatter.9.cloned.1.call-start = ((), (), s32[]{:S(2)}) async-start(), calls=%async_computation.10 | async-start | bytes 20971520 | tf_op jit(solution)/shard_map/reduce_scatter | solution.py:1321
  468.0 33.6 %collective-permute-start.2 = (bf16[2048,2048]{1,0:T(8,128)(2,1)}, bf16[2048,2048]{1,0:T(8,128)(2,1)}, u32[]{:S(2)}, u32[]{:S(2)}) collective-permute-start(bf16[2048,2048]{1,0:T(8,128)(2,1)} %shard_map.262.refs_1_), channel_id=1, source_target_pairs={{0,1},{1,0},{2,3},{3,2},{4,5},{5,4},{6,7},{7,6},{8,9},{9,8},{10,11... | collective-permute-start | bytes 25165832 | tf_op jit(solution)/shard_map/ppermute | solution.py:1160
  472.4 15.1 collective-permute-start.6
  633.5 367.4 %reduce-scatter.11.cloned.1.call-start = ((), (), s32[]{:S(2)}) async-start(), calls=%async_computation.11 | async-start | bytes 20971520 | tf_op jit(solution)/shard_map/reduce_scatter | solution.py:1321
  816.8 13.5 collective-permute-start.7
  844.2 235.7 %reduce-scatter.13.cloned.1.call-start = ((), (), s32[]{:S(2)}) async-start(), calls=%async_computation.12 | async-start | bytes 5242880 | tf_op jit(solution)/shard_map/reduce_scatter | solution.py:1324
  991.1 13.5 collective-permute-start.8
  1001.0 136.3 %reduce-scatter.15.cloned.1.call-start = ((), (), s32[]{:S(2)}) async-start(), calls=%async_computation.13 | async-start | bytes 5242880 | tf_op jit(solution)/shard_map/reduce_scatter | solution.py:1321
  1079.9 206.5 %reduce-scatter.19.cloned.1.call-start = ((), (), s32[]{:S(2)}) async-start(), calls=%async_computation.15 | async-start | bytes 5242880 | tf_op jit(solution)/shard_map/reduce_scatter | solution.py:1324
  1083.3 11.2 collective-permute-start.10
  1084.6 9.9 collective-permute-start.9
  1137.3 152.0 %reduce-scatter.17.cloned.1.call-start = ((), (), s32[]{:S(2)}) async-start(), calls=%async_computation.14 | async-start | bytes 7864320 | tf_op jit(solution)/shard_map/reduce_scatter | solution.py:1321
  1138.1 232.2 %reduce-scatter.21.cloned.1.call-start = ((), (), s32[]{:S(2)}) async-start(), calls=%async_computation.16 | async-start | bytes 7864320 | tf_op jit(solution)/shard_map/reduce_scatter | solution.py:1321
  1228.7 9.8 collective-permute-start.11
  1230.0 8.5 collective-permute-start.12
  1289.4 271.2 %reduce-scatter.23.cloned.1.call-start = ((), (), s32[]{:S(2)}) async-start(), calls=%async_computation.17 | async-start | bytes 5242880 | tf_op jit(solution)/shard_map/reduce_scatter | solution.py:1324
  1355.5 14.7 collective-permute-start.13
  (80 other events, 1289.0 us)
Sparse Core Ops, SparseCore 0:
  213.3 270.5 all-gather.4
  486.6 198.9 all-gather.2
  688.7 155.4 reduce-scatter.8
  847.1 153.8 reduce-scatter.10
  1003.1 76.7 reduce-scatter.12
  1083.0 53.1 reduce-scatter.14
  1138.5 76.7 reduce-scatter.18
  1218.6 70.7 reduce-scatter.16
  1292.6 71.1 reduce-scatter.20
  1375.5 139.3 reduce-scatter.22

commit v5 on v4

--- a/solution.py
+++ b/solution.py
@@ -1399,9 +1399,17 @@
     )
     grad_w_down = grad_w_down.T
     qkv_rows = jnp.concatenate((out_rows, first_rows, gate(second_rows, d_norm_other)), axis=1)
-    attn_seq = over_seq(qkv_rows).astype(F32)
-    grad_w_out, grad_w_qkv = attn_seq[:, :half].T, attn_seq[:, half:]
-    grad_w_qkv = jnp.transpose(grad_w_qkv.reshape(-1, 2, 3, half // 2), (2, 0, 1, 3)).reshape(3, -1, half)
+    attn_seq = over_seq(qkv_rows)
+    grad_w_out = attn_seq[:, :half].astype(F32).T
+    piece = half // 2
+
+    def columns_of(kind, part):
+        first = half + (3 * part + kind) * piece
+        return attn_seq[:, first : first + piece]
+
+    grad_w_qkv = jnp.stack(
+        [jnp.concatenate((columns_of(kind, 0), columns_of(kind, 1)), axis=1) for kind in range(3)]
+    ).astype(F32)
 
     sums = (
         jnp.moveaxis(

time: 1590 us -> 1590 us (level)
  waiting for transfers between devices: 128 us -> 172 us
  Pallas kernels: 1080 us -> 1040 us
    ppermute x6, waiting for transfers between devices: 11 us -> 30.5 us  [shift_by(): return lax.ppermute(field, 'seq', perm)]
    unnamed x200 -> x197, local copies, waits for them, and re-layouts: 90 us -> 87.6 us
  transfers between devices with their start and end apart: 24 -> 24, of which waited for: 10 -> 10; matrix products, arithmetic and copies ran while one was open for 17% -> 17% of each run, Pallas kernels for 56% -> 54%
where the time goes in v5:
time: 1590 us
  Pallas kernels  1040 us (65%)
  waiting for transfers between devices  172 us (11%)
  local copies, waits for them, and re-layouts  126 us (8%)
  other arithmetic  116 us (7%)
  matrix products  101 us (6%)
  between operations  15.9 us (1%)
    pallas_call x13, Pallas kernels, product(): pl.pallas_call(functools.partial(product_kernel, mode, finish, len(rows),...  370 us
    pallas_call x1, Pallas kernels, opening(): pl.pallas_call(opening_kernel, in_specs=[anywhere] * 3, out_specs=[anywhe...  193 us
    pallas_call x3, Pallas kernels, attn_bwd(): pl.pallas_call(functools.partial(bwd_kernel, tile), grid_spec=pltpu.Prefe...  156 us
    pallas_call x1, Pallas kernels, closing(): pl.pallas_call(closing_kernel, in_specs=[anywhere] * 2, out_specs=[anywhe...  152 us
    pallas_call x4, Pallas kernels, attn_fwd(): pl.pallas_call(functools.partial(fwd_kernel, tile), grid_spec=pltpu.Prefe...  121 us
    dot_general x2, matrix products, dot_nn(): lax.dot_general(a, b, (((1,), (0,)), ((), ())), preferred_element_type=F32)  101 us
    unnamed x197, local copies, waits for them, and re-layouts  87.6 us
    all_gather x1, waiting for transfers between devices, layer_by_segment(): down_full = lax.all_gather(gate(w_down.T, values), BOTH, axis=0, tiled=True)  65.7 us
  transfers between devices with their start and end apart: 24, of which 10 were waited for; matrix products, arithmetic and copies ran while one was open for 17% of the time, Pallas kernels for 54%

profile of v5, /device:TPU:0, one launch (start us, length us, event | category | flops | bytes accessed | tf_op | source)
XLA Modules:
  0.0 1588.5 jit_solution(1815884118421953143)
XLA Ops:
  20.5 192.6 %shard_map.254 = (bf16[4,2048,1024]{2,1,0:T(8,128)(2,1)}, bf16[4,512,2048]{2,1,0:T(8,128)(2,1)}, bf16[16,16,128]{2,1,0:T(8,128)(2,1)}) custom-call(bf16[4,128,1024]{2,1,0:T(8,128)(2,1)} %pad_maximum_fusion.4.w_ref, bf16[4,512,2048]{2,1,0:T(8,128)(2,1)} %bitcast.172, bf16[16,128]{1,0:T(8,128)(2,1)} %pad_bitcast_fusion.1.v_ref), custom_call_target="tpu_custom_call" | custom-call | tf_op jit(solution)/shard_map/pallas_call | solution.py:561
  306.5 30.2 %shard_map.258 = (bf16[2048,1024]{1,0:T(8,128)(2,1)S(1)}, f32[8,2,2048]{2,1,0:T(2,128)S(1)}) custom-call(s32[16]{0:T(128)S(1)} %select_n.80.flags, bf16[2048,1024]{1,0:T(8,128)(2,1)S(1)} %copy-done.11, bf16[2048,1024]{1,0:T(8,128)(2,1)S(1)} %copy-done.46, bf16[2048,1024]{1,0:T(8,128)(2,1)} %copy-done.9, bf16[128,1024]{1,0:T(8,128)(2,1)S(1)} %get-tuple-element.167.sk_ref, ...), custom_call_target="tpu_custom_call" | custom-call | flops 33600000000 | bytes 1000 | tf_op jit(solution)/shard_map/pallas_call | solution.py:943
  336.6 30.2 %shard_map.259 = (bf16[2048,1024]{1,0:T(8,128)(2,1)S(1)}, f32[8,2,2048]{2,1,0:T(2,128)S(1)}) custom-call(s32[16]{0:T(128)S(1)} %select_n.80.flags, bf16[2048,1024]{1,0:T(8,128)(2,1)S(1)} %copy-done.11, bf16[2048,1024]{1,0:T(8,128)(2,1)S(1)} %copy-done.46, bf16[2048,1024]{1,0:T(8,128)(2,1)} %copy-done.9, ...), custom_call_target="tpu_custom_call", output_to_operand_aliasing={{0}: (9, {}), {1}: (10, {})} | custom-call | flops 33600000000 | bytes 1000 | tf_op jit(solution)/shard_map/pallas_call | solution.py:943
  366.8 30.2 %shard_map.260 = (bf16[2048,1024]{1,0:T(8,128)(2,1)S(1)}, f32[8,2,2048]{2,1,0:T(2,128)S(1)}) custom-call(s32[16]{0:T(128)S(1)} %select_n.80.flags, bf16[2048,1024]{1,0:T(8,128)(2,1)S(1)} %copy-done.11, bf16[2048,1024]{1,0:T(8,128)(2,1)S(1)} %copy-done.46, bf16[2048,1024]{1,0:T(8,128)(2,1)} %copy-done.9, ...), custom_call_target="tpu_custom_call", output_to_operand_aliasing={{0}: (9, {}), {1}: (10, {})} | custom-call | flops 33600000000 | bytes 1000 | tf_op jit(solution)/shard_map/pallas_call | solution.py:943
  409.2 30.3 %shard_map.261 = (bf16[2048,1024]{1,0:T(8,128)(2,1)S(1)}, f32[8,2,2048]{2,1,0:T(2,128)S(1)}) custom-call(s32[16]{0:T(128)S(1)} %select_n.80.flags, bf16[2048,1024]{1,0:T(8,128)(2,1)S(1)} %copy-done.12, bf16[2048,1024]{1,0:T(8,128)(2,1)S(1)} %copy-done.47, bf16[2048,1024]{1,0:T(8,128)(2,1)} %copy-done.9, ...), custom_call_target="tpu_custom_call", output_to_operand_aliasing={{0}: (9, {}), {1}: (10, {})} | custom-call | flops 33600000000 | bytes 1000 | tf_op jit(solution)/shard_map/pallas_call | solution.py:943
  522.1 56.0 %multiply_convert_fusion.1 = (bf16[2048,4096]{1,0:T(8,128)(2,1)}, bf16[2048,4096]{1,0:T(8,128)(2,1)}) fusion(f32[4096]{0:T(1024)S(1)} %reshape.247, bf16[2048,2048]{1,0:T(8,128)(2,1)} %add_convert_fusion.1.refs_0_, bf16[2048,4096]{1,0:T(8,128)(2,1)} %all-gather.5.cloned.1.call-done.refs_1_), kind=kOutput, calls=%fused_computation.8 | convolution fusion | flops 34460401664 | bytes 58736640 | tf_op jit(solution)/shard_map/dot_general | solution.py:876
  578.1 41.7 %shard_map.270.refs_1_ = bf16[2048,4096]{1,0:T(8,128)(2,1)} custom-call(bf16[2048,2048]{1,0:T(8,128)(2,1)} %bitcast.173, bf16[2048,4096]{1,0:T(8,128)(2,1)} %get-tuple-element.152.refs_1_.refs_0_), custom_call_target="tpu_custom_call" | custom-call | flops 42949672960 | bytes 1000 | tf_op jit(solution)/shard_map/pallas_call | solution.py:860
  619.9 65.7 %all-gather.3.cloned.1.call-done.refs_1_ = bf16[2048,4096]{1,0:T(8,128)(2,1)} async-done(((bf16[128,4096]{1,0:T(8,128)(2,1)}), bf16[2048,4096]{1,0:T(8,128)(2,1)}) %all-gather.3.cloned.1.call-update) | async-done | bytes 16777232 | tf_op jit(solution)/shard_map/all_gather | solution.py:1307
  685.6 45.3 %convert_reduce_fusion = (f32[4096]{0:T(1024)}, bf16[2048,4096]{1,0:T(8,128)(2,1)}) fusion(bf16[2048,4096]{1,0:T(8,128)(2,1)} %shard_map.271, bf16[2048,2048]{1,0:T(8,128)(2,1)} %bitcast.174, bf16[2048,4096]{1,0:T(8,128)(2,1)} %all-gather.3.cloned.1.call-done.refs_1_), kind=kOutput, calls=%fused_computation.6 | convolution fusion | flops 34401677312 | bytes 58736640 | tf_op jit(solution)/shard_map/dot_general | solution.py:876
  731.0 41.5 %shard_map.272.refs_2_.refs_0_ = bf16[2048,4096]{1,0:T(8,128)(2,1)} custom-call(bf16[2048,2048]{1,0:T(8,128)(2,1)} %add_convert_fusion.1.refs_0_, bf16[2048,4096]{1,0:T(8,128)(2,1)} %get-tuple-element.204.refs_1_.refs_0_), custom_call_target="tpu_custom_call" | custom-call | flops 42949672960 | bytes 1000 | tf_op jit(solution)/shard_map/pallas_call | solution.py:860
  772.5 44.4 %shard_map.273.own_ref = bf16[2048,2048]{1,0:T(8,128)(2,1)} custom-call(bf16[2048,4096]{1,0:T(8,128)(2,1)} %get-tuple-element.204.refs_1_.refs_0_, bf16[2048,4096]{1,0:T(8,128)(2,1)} %all-gather.5.cloned.1.call-done.refs_1_, bf16[2048,4096]{1,0:T(8,128)(2,1)} %shard_map.272.refs_2_.refs_0_), custom_call_target="tpu_custom_call" | custom-call | flops 42949672960 | bytes 1000 | tf_op jit(solution)/shard_map/pallas_call | solution.py:860
  830.4 19.9 %reduce-scatter.9.cloned.1.call-done.refs_1_.refs_0_ = bf16[512,4096]{1,0:T(8,128)(2,1)} async-done(((bf16[2048,4096]{1,0:T(8,128)(2,1)}), bf16[512,4096]{1,0:T(8,128)(2,1)}) %reduce-scatter.9.cloned.1.call-update) | async-done | bytes 4194320 | tf_op jit(solution)/shard_map/reduce_scatter | solution.py:1321
  850.4 27.3 %shard_map.275 = (f32[2048,2048]{1,0:T(8,128)}, bf16[2048,2048]{1,0:T(8,128)(2,1)}, f32[8,2048]{1,0:T(8,128)S(1)}) custom-call(f32[2048,2048]{1,0:T(8,128)} %get-tuple-element.151.field_ref, bf16[2048,2048]{1,0:T(8,128)(2,1)} %shard_map.273.own_ref, bf16[2048,2048]{1,0:T(8,128)(2,1)} %shard_map.274.other_ref.refs_2_, bf16[2048,2048]{1,0:T(8,128)(2,1)} %bitcast.175, ...), custom_call_target="tpu_custom_call" | custom-call | flops 15000000512 | bytes 1000 | tf_op jit(solution)/shard_map/pallas_call | solution.py:705
  908.3 39.9 %shard_map.279 = (bf16[2048,256]{1,0:T(8,128)(2,1)S(1)}, bf16[2048,256]{1,0:T(8,128)(2,1)S(1)}, bf16[2048,256]{1,0:T(8,128)(2,1)S(1)}, bf16[128,256]{1,0:T(8,128)(2,1)S(1)}, bf16[128,256]{1,0:T(8,128)(2,1)S(1)}) custom-call(s32[16]{0:T(128)S(1)} %copy-done.51, bf16[2048,1024]{1,0:T(8,128)(2,1)S(1)} %copy-done.13, bf16[2048,1024]{1,0:T(8,128)(2,1)S(1)} %copy-done.48, ...), custom_call_target="tpu_custom_call" | custom-call | flops 44000002048 | bytes 1000 | tf_op jit(solution)/shard_map/pallas_call | solution.py:1065
  949.4 44.2 %shard_map.280.refs_2_ = bf16[2048,2048]{1,0:T(8,128)(2,1)} custom-call(bf16[2048,4096]{1,0:T(8,128)(2,1)} %get-tuple-element.152.refs_1_.refs_0_, bf16[2048,4096]{1,0:T(8,128)(2,1)} %all-gather.3.cloned.1.call-done.refs_1_, bf16[2048,256]{1,0:T(8,128)(2,1)S(1)} %get-tuple-element.65.refs_2_), custom_call_target="tpu_custom_call" | custom-call | flops 42949672960 | bytes 1000 | tf_op jit(solution)/shard_map/pallas_call | solution.py:860
  1026.1 39.5 %shard_map.283 = (bf16[2048,256]{1,0:T(8,128)(2,1)S(1)}, bf16[2048,256]{1,0:T(8,128)(2,1)S(1)}, bf16[2048,256]{1,0:T(8,128)(2,1)S(1)}, bf16[128,256]{1,0:T(8,128)(2,1)S(1)}, bf16[128,256]{1,0:T(8,128)(2,1)S(1)}) custom-call(s32[16]{0:T(128)S(1)} %copy-done.52, bf16[2048,1024]{1,0:T(8,128)(2,1)S(1)} %copy-done.14, bf16[2048,1024]{1,0:T(8,128)(2,1)S(1)} %copy-done.49, ...), custom_call_target="tpu_custom_call" | custom-call | flops 44000002048 | bytes 1000 | tf_op jit(solution)/shard_map/pallas_call | solution.py:1065
  1069.8 16.3 %reduce-scatter.13.cloned.1.call-done.refs_1_ = bf16[128,4096]{1,0:T(8,128)(2,1)} async-done(((bf16[512,4096]{1,0:T(8,128)(2,1)}), bf16[128,4096]{1,0:T(8,128)(2,1)}) %reduce-scatter.13.cloned.1.call-update) | async-done | bytes 1048592 | tf_op jit(solution)/shard_map/reduce_scatter | solution.py:1324
  1109.8 33.3 %shard_map.285 = (bf16[2048,1536]{1,0:T(8,128)(2,1)}, bf16[4,512,2048]{2,1,0:T(8,128)(2,1)}) custom-call(bf16[2048,2048]{1,0:T(8,128)(2,1)} %fusion.8.refs_0_, bf16[2048,1536]{1,0:T(8,128)(2,1)} %pad_maximum_fusion.1.refs_1_, bf16[4,512,2048]{2,1,0:T(8,128)(2,1)} %bitcast.168, ...), custom_call_target="tpu_custom_call", output_to_operand_aliasing={{1}: (3, {})} | custom-call | flops 16106127360 | bytes 1000 | tf_op jit(solution)/shard_map/pallas_call | solution.py:860
  1148.6 76.9 %shard_map.288 = (bf16[2048,512]{1,0:T(8,128)(2,1)S(1)}, bf16[2048,512]{1,0:T(8,128)(2,1)S(1)}, bf16[2048,512]{1,0:T(8,128)(2,1)S(1)}, bf16[128,512]{1,0:T(8,128)(2,1)S(1)}, bf16[128,512]{1,0:T(8,128)(2,1)S(1)}) custom-call(s32[16]{0:T(128)S(1)} %copy-done.53, bf16[2048,1024]{1,0:T(8,128)(2,1)S(1)} %copy-done.15, bf16[2048,1024]{1,0:T(8,128)(2,1)} %copy-done.45, ...), custom_call_target="tpu_custom_call" | custom-call | flops 88000004096 | bytes 1000 | tf_op jit(solution)/shard_map/pallas_call | solution.py:1065
  1229.5 20.7 %collective-permute-done.11 = bf16[2,50,512]{2,1,0:T(8,128)(2,1)S(1)} collective-permute-done((bf16[2,50,512]{2,1,0:T(8,128)(2,1)S(1)}, bf16[2,50,512]{2,1,0:T(8,128)(2,1)S(1)}, u32[]{:S(2)}, u32[]{:S(2)}) %collective-permute-start.11) | collective-permute-done | bytes 102432 | tf_op jit(solution)/shard_map/ppermute | solution.py:1192
  1263.6 31.6 %shard_map.289 = (bf16[2048,1536]{1,0:T(8,128)(2,1)}, bf16[4,512,2048]{2,1,0:T(8,128)(2,1)}) custom-call(bf16[2048,2048]{1,0:T(8,128)(2,1)} %fusion.8.refs_0_, bf16[2048,1536]{1,0:T(8,128)(2,1)} %pad_maximum_fusion.2.refs_1_, bf16[4,512,2048]{2,1,0:T(8,128)(2,1)} %bitcast.169, ...), custom_call_target="tpu_custom_call", output_to_operand_aliasing={{1}: (3, {})} | custom-call | flops 16106127360 | bytes 1000 | tf_op jit(solution)/shard_map/pallas_call | solution.py:860
  1307.2 55.5 %shard_map.291 = (bf16[2048,2048]{1,0:T(8,128)(2,1)}, bf16[4,512,2048]{2,1,0:T(8,128)(2,1)}) custom-call(bf16[2048,3072]{1,0:T(8,128)(2,1)} %constant_dynamic-update-slice_fusion.4.refs_0_, bf16[4,2048,1024]{2,1,0:T(8,128)(2,1)} %get-tuple-element.55.refs_1_, bf16[4,512,2048]{2,1,0:T(8,128)(2,1)} %bitcast.170, ...), custom_call_target="tpu_custom_call", output_to_operand_aliasing={{1}: (3, {})} | custom-call | flops 32212254720 | bytes 1000 | tf_op jit(solution)/shard_map/pallas_call | solution.py:860
  1390.3 21.9 %shard_map.294 = (bf16[2048,2048]{1,0:T(8,128)(2,1)}, f32[8,2048]{1,0:T(8,128)S(1)}) custom-call(bf16[2048,2048]{1,0:T(8,128)(2,1)} %bitcast.166, bf16[2048,2048]{1,0:T(8,128)(2,1)} %get-tuple-element.85.own_ref, bf16[2048,2048]{1,0:T(8,128)(2,1)} %shard_map.293.other_ref.refs_1_, f32[2048,2048]{1,0:T(8,128)} %get-tuple-element.86.rest_ref, ...), custom_call_target="tpu_custom_call" | custom-call | flops 15000000512 | bytes 1000 | tf_op jit(solution)/shard_map/pallas_call | solution.py:705
  1412.9 151.5 %shard_map.297 = (bf16[4,512,2048]{2,1,0:T(8,128)(2,1)}, f32[16,128]{1,0:T(8,128)}) custom-call(bf16[4,512,2048]{2,1,0:T(8,128)(2,1)} %bitcast.177, f32[16,16,128]{2,1,0:T(8,128)} %shard_map.296.v_ref), custom_call_target="tpu_custom_call" | custom-call | tf_op jit(solution)/shard_map/pallas_call | solution.py:660
  (385 shorter events, 385.8 us)
Async XLA Ops:
  7.2 514.9 %all-gather.5.cloned.1.call-start = ((), (), s32[]{:S(2)}) async-start(), calls=%async_computation.9 | async-start | bytes 17825792 | tf_op jit(solution)/shard_map/all_gather | solution.py:1293
  213.2 472.5 %all-gather.3.cloned.1.call-start = ((), (), s32[]{:S(2)}) async-start(), calls=%async_computation.8 | async-start | bytes 17825792 | tf_op jit(solution)/shard_map/all_gather | solution.py:1307
  262.9 37.9 %collective-permute-start = (bf16[2,50,1024]{2,1,0:T(8,128)(2,1)S(1)}, bf16[2,50,1024]{2,1,0:T(8,128)(2,1)S(1)}, u32[]{:S(2)}, u32[]{:S(2)}) collective-permute-start(bf16[2,50,1024]{2,1,0:T(8,128)(2,1)S(1)} %pad_maximum_fusion.5), channel_id=1, source_target_pairs={{0,2},{2,4},{4,6},{1,3},{3,5},{5,7},{8,10},{10,12},{12,14},{9,11},... | collective-permute-start | bytes 614408 | tf_op jit(solution)/shard_map/ppermute | solution.py:1192
  284.2 16.6 %collective-permute-start.1 = (bf16[2,50,1024]{2,1,0:T(8,128)(2,1)S(1)}, bf16[2,50,1024]{2,1,0:T(8,128)(2,1)}, u32[]{:S(2)}, u32[]{:S(2)}) collective-permute-start(bf16[2,50,1024]{2,1,0:T(8,128)(2,1)S(1)} %pad_maximum_fusion.5), channel_id=1, source_target_pairs={{0,4},{2,6},{1,5},{3,7},{8,12},{10,14},{9,13},{11,15},{16,20},{18,... | collective-permute-start | bytes 614408 | tf_op jit(solution)/shard_map/ppermute | solution.py:1192
  293.1 106.5 %collective-permute-start.3 = (bf16[1,512,1024]{2,1,0:T(8,128)(2,1)}, bf16[1,512,1024]{2,1,0:T(8,128)(2,1)}, u32[]{:S(2)}, u32[]{:S(2)}) collective-permute-start(bf16[1,512,1024]{2,1,0:T(8,128)(2,1)} %get-tuple-element.158), channel_id=1, source_target_pairs={{0,2},{2,4},{4,6},{6,0},{1,3},{3,5},{5,7},{7,1},{8,10},{10,12},{12... | collective-permute-start | bytes 3145736 | tf_op jit(solution)/shard_map/ppermute | solution.py:1174
  293.2 106.5 %collective-permute-start.4 = (bf16[1,512,1024]{2,1,0:T(8,128)(2,1)}, bf16[1,512,1024]{2,1,0:T(8,128)(2,1)S(1)}, u32[]{:S(2)}, u32[]{:S(2)}) collective-permute-start(bf16[1,512,1024]{2,1,0:T(8,128)(2,1)} %get-tuple-element.157), channel_id=1, source_target_pairs={{0,4},{2,6},{4,0},{6,2},{1,5},{3,7},{5,1},{7,3},{8,12},{10,14},{12... | collective-permute-start | bytes 3145736 | tf_op jit(solution)/shard_map/ppermute | solution.py:1174
  293.2 107.5 %collective-permute-start.5 = (bf16[1,512,1024]{2,1,0:T(8,128)(2,1)}, bf16[1,512,1024]{2,1,0:T(8,128)(2,1)S(1)}, u32[]{:S(2)}, u32[]{:S(2)}) collective-permute-start(bf16[1,512,1024]{2,1,0:T(8,128)(2,1)} %get-tuple-element.156), channel_id=1, source_target_pairs={{0,6},{2,0},{4,2},{6,4},{1,7},{3,1},{5,3},{7,5},{8,14},{10,8},{12,... | collective-permute-start | bytes 3145736 | tf_op jit(solution)/shard_map/ppermute | solution.py:1174
  299.3 551.1 %reduce-scatter.9.cloned.1.call-start = ((), (), s32[]{:S(2)}) async-start(), calls=%async_computation.10 | async-start | bytes 20971520 | tf_op jit(solution)/shard_map/reduce_scatter | solution.py:1321
  456.3 33.6 %collective-permute-start.2 = (bf16[2048,2048]{1,0:T(8,128)(2,1)}, bf16[2048,2048]{1,0:T(8,128)(2,1)}, u32[]{:S(2)}, u32[]{:S(2)}) collective-permute-start(bf16[2048,2048]{1,0:T(8,128)(2,1)} %shard_map.262.refs_1_), channel_id=1, source_target_pairs={{0,1},{1,0},{2,3},{3,2},{4,5},{5,4},{6,7},{7,6},{8,9},{9,8},{10,11... | collective-permute-start | bytes 25165832 | tf_op jit(solution)/shard_map/ppermute | solution.py:1160
  460.7 15.1 collective-permute-start.6
  619.8 387.3 %reduce-scatter.11.cloned.1.call-start = ((), (), s32[]{:S(2)}) async-start(), calls=%async_computation.11 | async-start | bytes 20971520 | tf_op jit(solution)/shard_map/reduce_scatter | solution.py:1321
  816.9 13.5 collective-permute-start.7
  850.4 235.7 %reduce-scatter.13.cloned.1.call-start = ((), (), s32[]{:S(2)}) async-start(), calls=%async_computation.12 | async-start | bytes 5242880 | tf_op jit(solution)/shard_map/reduce_scatter | solution.py:1324
  993.7 13.5 collective-permute-start.8
  1007.1 136.0 %reduce-scatter.15.cloned.1.call-start = ((), (), s32[]{:S(2)}) async-start(), calls=%async_computation.13 | async-start | bytes 5242880 | tf_op jit(solution)/shard_map/reduce_scatter | solution.py:1321
  1086.1 209.2 %reduce-scatter.19.cloned.1.call-start = ((), (), s32[]{:S(2)}) async-start(), calls=%async_computation.15 | async-start | bytes 5242880 | tf_op jit(solution)/shard_map/reduce_scatter | solution.py:1324
  1089.4 11.1 collective-permute-start.10
  1090.7 9.8 collective-permute-start.9
  1143.2 152.8 %reduce-scatter.17.cloned.1.call-start = ((), (), s32[]{:S(2)}) async-start(), calls=%async_computation.14 | async-start | bytes 7864320 | tf_op jit(solution)/shard_map/reduce_scatter | solution.py:1321
  1144.0 233.5 %reduce-scatter.21.cloned.1.call-start = ((), (), s32[]{:S(2)}) async-start(), calls=%async_computation.16 | async-start | bytes 7864320 | tf_op jit(solution)/shard_map/reduce_scatter | solution.py:1321
  1226.8 23.4 %collective-permute-start.11 = (bf16[2,50,512]{2,1,0:T(8,128)(2,1)S(1)}, bf16[2,50,512]{2,1,0:T(8,128)(2,1)S(1)}, u32[]{:S(2)}, u32[]{:S(2)}) collective-permute-start(bf16[2,50,512]{2,1,0:T(8,128)(2,1)S(1)} %get-tuple-element.168), channel_id=1, source_target_pairs={{2,0},{4,2},{6,4},{3,1},{5,3},{7,5},{10,8},{12,10},{14,12},{11,9},... | collective-permute-start | bytes 307208 | tf_op jit(solution)/shard_map/ppermute | solution.py:1192
  1228.1 28.1 %collective-permute-start.12 = (bf16[2,50,512]{2,1,0:T(8,128)(2,1)S(1)}, bf16[2,50,512]{2,1,0:T(8,128)(2,1)S(1)}, u32[]{:S(2)}, u32[]{:S(2)}) collective-permute-start(bf16[2,50,512]{2,1,0:T(8,128)(2,1)S(1)} %get-tuple-element.169), channel_id=1, source_target_pairs={{4,0},{6,2},{5,1},{7,3},{12,8},{14,10},{13,9},{15,11},{20,16},{22,... | collective-permute-start | bytes 307208 | tf_op jit(solution)/shard_map/ppermute | solution.py:1192
  1296.1 272.0 %reduce-scatter.23.cloned.1.call-start = ((), (), s32[]{:S(2)}) async-start(), calls=%async_computation.17 | async-start | bytes 5242880 | tf_op jit(solution)/shard_map/reduce_scatter | solution.py:1324
  1362.7 14.7 collective-permute-start.13
  (79 other events, 1223.4 us)
Sparse Core Ops, SparseCore 0:
  213.3 270.5 all-gather.4
  486.6 198.9 all-gather.2
  688.7 161.5 reduce-scatter.8
  853.2 153.8 reduce-scatter.10
  1009.3 76.7 reduce-scatter.12
  1089.1 53.7 reduce-scatter.14
  1145.2 76.7 reduce-scatter.18
  1225.3 70.7 reduce-scatter.16
  1299.3 71.9 reduce-scatter.20
  1382.7 140.0 reduce-scatter.22
